TPU v7x, 128 devices: a whole 4x4x4 slice. The times are simulated.
128 devices in a mesh: sec: 4 (over y), brick: 32 (over x, z, core).
Axes of the slice: x: 4, y: 4, z: 4, core: 2. Of those that a mesh axis runs over, the one named last changes fastest.
Arguments:
- melt: float32 [64, 16, 7, 512], P('brick', None, None, 'sec'), may hold values from -6 to 6
- grain_velocity: float32 [32768, 3, 128], P(('sec', 'brick')), may hold values from -6 to 6
- grain_radius: float32 [32768, 128], P(('sec', 'brick')), may hold values from 0.5 to 2
- parcel_cell: int32 [32768, 128], P(('sec', 'brick')), may hold values from 0 to 4095
- target_brick: int32 [32768], P(('sec', 'brick')), may hold values from 0 to 127, as said below
- block_count: int32 [32768], P(('sec', 'brick')), may hold values from 64 to 128
- slope: float32 [3], replicated, may hold values from -2 to -0.5
- partition: float32 [3], replicated, may hold values from 0.1 to 0.9
- diffusivity: float32 [7], replicated, may hold values from 0.08 to 0.16
Outputs:
- melt_out: float32 [64, 16, 7, 512], P('brick', None, None, 'sec')
- velocity_out: float32 [32768, 3, 128], P(('sec', 'brick'))
- radius_out: float32 [32768, 128], P(('sec', 'brick'))
Inputs may be any that keep to these rules, and one draw needn't show every extreme that they name: `target_brick`: each device's 256 blocks name at most 4 blocks for any one brick; in every draw one brick, the same for all devices, is named by exactly 4 blocks of every device. The live parcels of a block are its first block_count slots.
All inputs are finite; a program needn't handle non-finite values.
Results may differ from a plain program's by a relative error of at most 0.0003.
The roundings to bfloat16 on the way count: a program that leaves them out, or rounds other values in their place, can miss the bound.
Values sent between devices are 32-bit elements; how exact they have to be, the bound alone decides.
No kernel may reach another device: no remote copies, remote signals or barrier semaphores. Data moves between devices by JAX's collectives and lax.ppermute only.
A program may use at most 64 MiB of HBM per device.

v0:
```python
import jax
import jax.numpy as jnp
from jax import lax
from jax.sharding import PartitionSpec as P

GROUP = 32
ITERS = 2


GROW = 0.4
DRAG = 0.25
MOMENT = 0.4
LATENT = 0.5
SETTLE = 0.1


def with_halo(shard, sides, width):
    for axis, dim in sides:
        devices, length = (lax.axis_size(axis), shard.shape[dim])
        up = [(i, (i + 1) % devices) for i in range(devices - 1)]
        down = [(j, i) for i, j in up]
        last = lax.slice_in_dim(shard, length - width, length, axis=dim)
        first = lax.slice_in_dim(shard, 0, width, axis=dim)
        before = lax.ppermute(last, axis, up)
        after = lax.ppermute(first, axis, down)
        shard = jnp.concatenate([before, shard, after], axis=dim)
    return shard


def grain_physics(probe, velocity, radius, slope, partition):
    flow = probe[..., 0:3]
    temper = probe[..., 3]
    concen = probe[..., 4:]
    under = jnp.sum(concen * slope, axis=-1) - temper
    growth = GROW * jax.nn.softplus(under)
    beta = DRAG / (radius * radius)
    slip = flow - velocity
    momentum = -(MOMENT * radius * radius * radius * beta)[..., None] * slip
    heat = LATENT * growth * radius
    solute = (1.0 - partition) * concen * (growth * radius)[..., None]
    sources = jnp.concatenate([momentum, heat[..., None], solute], axis=-1)
    settle = jnp.array([0.0, 0.0, SETTLE], jnp.float32)
    new_velocity = velocity + beta[..., None] * slip - settle * radius[..., None]
    new_radius = radius + growth / radius
    return (sources, new_velocity, new_radius)


def send_out(velocity, radius, cells, counts):
    return (
        lax.all_to_all(velocity, ("sec", "brick"), split_axis=0, concat_axis=0, tiled=True),
        lax.all_to_all(radius, ("sec", "brick"), split_axis=0, concat_axis=0, tiled=True),
        lax.all_to_all(cells, ("sec", "brick"), split_axis=0, concat_axis=0, tiled=True),
        lax.all_to_all(counts, ("sec", "brick"), split_axis=0, concat_axis=0, tiled=True),
    )


def send_back(velocity, radius):
    return (
        lax.all_to_all(velocity, ("sec", "brick"), split_axis=0, concat_axis=0, tiled=True),
        lax.all_to_all(radius, ("sec", "brick"), split_axis=0, concat_axis=0, tiled=True),
    )


def couple(melt, velocity, radius, cells, counts, slope, partition, diffusivity):
    size_x, size_y, comps, size_z = melt.shape
    columns = size_x * size_y
    received, _, slot_count = velocity.shape
    lowered = melt.astype(jnp.bfloat16)
    table = jnp.transpose(lowered, (3, 2, 0, 1)).reshape(size_z, comps * columns)
    groups = received // GROUP
    z_range = jnp.arange(size_z, dtype=jnp.int32)
    col_range = jnp.arange(columns, dtype=jnp.int32)
    slot_range = jnp.arange(slot_count, dtype=jnp.int32)

    def turn(acc, items):
        velo_g, radi_g, cell_g, count_g = items
        live_p = (slot_range[None, :] < count_g[:, None]).reshape(-1)
        cell_p = cell_g.reshape(-1)
        velo_p = jnp.transpose(velo_g, (0, 2, 1)).reshape(-1, 3)
        radi_p = radi_g.reshape(-1)
        pick_z = (cell_p[:, None] % size_z == z_range[None, :]).astype(jnp.bfloat16)
        pick_col = (cell_p[:, None] // size_z == col_range[None, :]).astype(jnp.bfloat16)
        lifted = jnp.dot(pick_z, table, preferred_element_type=jnp.bfloat16).reshape(
            -1, comps, columns
        )
        probe = jnp.sum((lifted * pick_col[:, None, :]).astype(jnp.float32), axis=2)
        sources, new_velo, new_radi = grain_physics(probe, velo_p, radi_p, slope, partition)
        sources = jnp.where(live_p[:, None], sources, 0.0).astype(jnp.bfloat16)
        spread = (sources[:, :, None] * pick_col[:, None, :]).reshape(-1, comps * columns)
        acc = acc + lax.dot_general(
            pick_z, spread, (((0,), (0,)), ((), ())), preferred_element_type=jnp.float32
        )
        new_velo = jnp.where(live_p[:, None], new_velo, velo_p)
        new_radi = jnp.where(live_p, new_radi, radi_p)
        new_velo = jnp.transpose(new_velo.reshape(GROUP, slot_count, 3), (0, 2, 1))
        return (acc, (new_velo, new_radi.reshape(GROUP, slot_count)))

    start = jnp.zeros((size_z, comps * columns), jnp.float32)
    items = (
        velocity.reshape(groups, GROUP, 3, slot_count),
        radius.reshape(groups, GROUP, slot_count),
        cells.reshape(groups, GROUP, slot_count),
        counts.reshape(groups, GROUP),
    )
    acc, (new_velo, new_radi) = lax.scan(turn, start, items)
    deposit = jnp.transpose(acc.reshape(size_z, comps, size_x, size_y), (2, 3, 1, 0))
    padded = with_halo(melt, (("sec", 3), ("brick", 0)), 1)
    padded = jnp.pad(padded, ((0, 0), (1, 1), (0, 0), (0, 0)))
    beside = padded[2:, 1:-1, :, 1:-1] + padded[:-2, 1:-1, :, 1:-1]
    beside = beside + padded[1:-1, 2:, :, 1:-1] + padded[1:-1, :-2, :, 1:-1]
    beside = beside + padded[1:-1, 1:-1, :, 2:] + padded[1:-1, 1:-1, :, :-2]
    new_melt = melt + diffusivity[None, None, :, None] * (beside - 6.0 * melt) + deposit
    return (
        new_melt,
        new_velo.reshape(received, 3, slot_count),
        new_radi.reshape(received, slot_count),
    )


def local(
    melt,
    grain_velocity,
    grain_radius,
    parcel_cell,
    target_brick,
    block_count,
    slope,
    partition,
    diffusivity,
):
    device_count = lax.axis_size(("sec", "brick"))
    nblocks = target_brick.shape[0]
    cap = max(2, 2 * nblocks // device_count)
    slot_total = device_count * cap
    order = jnp.arange(nblocks, dtype=jnp.int32)
    earlier = (target_brick[:, None] == target_brick[None, :]) & (order[None, :] < order[:, None])
    ranking = jnp.sum(earlier.astype(jnp.int32), axis=1)
    slot_of = target_brick * cap + ranking
    holder = jnp.full((slot_total,), nblocks, jnp.int32).at[slot_of].set(order)
    filled = holder < nblocks
    source = jnp.minimum(holder, nblocks - 1)
    cells_sent = parcel_cell[source]
    counts_sent = jnp.where(filled, block_count[source], 0)
    velocity = grain_velocity
    radius = grain_radius
    got = send_out(velocity[source], radius[source], cells_sent, counts_sent)
    held_velo, held_radi = (got[0], got[1])
    for step in range(ITERS):
        melt, held_velo, held_radi = couple(
            melt, held_velo, held_radi, got[2], got[3], slope, partition, diffusivity
        )
    back = send_back(held_velo, held_radi)
    velocity = back[0][slot_of]
    radius = back[1][slot_of]
    return (melt, velocity, radius)


def solution(mesh):
    return jax.shard_map(
        local,
        mesh=mesh,
        in_specs=(
            P("brick", None, None, "sec"),
            P(("sec", "brick"), None, None),
            P(("sec", "brick"), None),
            P(("sec", "brick"), None),
            P(("sec", "brick")),
            P(("sec", "brick")),
            P(),
            P(),
            P(),
        ),
        out_specs=(
            P("brick", None, None, "sec"),
            P(("sec", "brick"), None, None),
            P(("sec", "brick"), None),
        ),
        check_vma=False,
    )
```

profile of v0, /device:TPU:14, one launch (start us, length us, event | category | flops | bytes accessed | tf_op | source)
XLA Modules:
  0.0 408.1 jit_solution(15955496170679695934)
XLA Ops:
  3.7 3.6 gather_fusion.1
  8.1 10.4 %all-to-all-start.1 = ((s32[128,4,1]{1,2,0:T(1,128)}), s32[128,4,1]{1,2,0:T(1,128)S(1)}, u32[]{:S(2)}, u32[]{:S(2)}) async-start(s32[128,4,1]{1,2,0:T(1,128)} %bitcast.2), calls=%async_computation.1 | async-start | bytes 131072 | tf_op jit(solution)/shard_map/all_to_all | solution.py:53
  20.1 5.6 %all-to-all-done.1 = s32[128,4,1]{1,2,0:T(1,128)S(1)} async-done(((s32[128,4,1]{1,2,0:T(1,128)}), s32[128,4,1]{1,2,0:T(1,128)S(1)}, u32[]{:S(2)}, u32[]{:S(2)}) %all-to-all-start.1) | async-done | bytes 2080 | tf_op jit(solution)/shard_map/all_to_all | solution.py:53
  25.7 6.7 %all-to-all-start = ((s32[128,4,128]{2,1,0:T(4,128)}), s32[128,4,128]{2,1,0:T(4,128)S(1)}, u32[]{:S(2)}, u32[]{:S(2)}) async-start(s32[128,4,128]{2,1,0:T(4,128)} %bitcast), calls=%async_computation | async-start | bytes 524288 | tf_op jit(solution)/shard_map/all_to_all | solution.py:52
  36.3 4.9 %all-to-all-done = s32[128,4,128]{2,1,0:T(4,128)S(1)} async-done(((s32[128,4,128]{2,1,0:T(4,128)}), s32[128,4,128]{2,1,0:T(4,128)S(1)}, u32[]{:S(2)}, u32[]{:S(2)}) %all-to-all-start) | async-done | bytes 262176 | tf_op jit(solution)/shard_map/all_to_all | solution.py:52
  41.2 6.9 %all-to-all-start.3 = ((f32[512,3,128]{2,1,0:T(4,128)}), f32[512,3,128]{2,1,0:T(4,128)S(1)}, u32[]{:S(2)}, u32[]{:S(2)}) async-start(f32[512,3,128]{2,1,0:T(4,128)} %copy.57), calls=%async_computation.3 | async-start | bytes 2097152 | tf_op jit(solution)/shard_map/all_to_all | solution.py:50
  48.2 3.4 collective-permute-start
  54.0 8.4 %collective-permute-done = f32[2,16,7,1]{3,1,0,2:T(8,128)S(1)} collective-permute-done((f32[2,16,7,1]{3,1,0,2:T(8,128)S(1)}, f32[2,16,7,1]{3,1,0,2:T(8,128)S(1)}, u32[]{:S(2)}, u32[]{:S(2)}) %collective-permute-start) | collective-permute-done | bytes 928 | tf_op jit(solution)/shard_map/ppermute | solution.py:24
  63.8 5.2 %collective-permute-start.2 = (f32[1,16,7,130]{3,1,0,2:T(8,128)S(1)}, f32[1,16,7,130]{3,1,0,2:T(8,128)S(1)}, u32[]{:S(2)}, u32[]{:S(2)}) collective-permute-start(f32[1,16,7,130]{3,1,0,2:T(8,128)S(1)} %get-tuple-element.825), channel_id=1, source_target_pairs={{1,0},{2,1},{3,2},{4,3},{5,4},{6,5},{7,6},{8,7},{9,8},{10,9},{11,1... | collective-permute-start | bytes 174728 | tf_op jit(solution)/shard_map/ppermute | solution.py:25
  72.6 10.0 %all-to-all-start.2 = ((f32[128,4,128]{2,1,0:T(4,128)}), f32[128,4,128]{2,1,0:T(4,128)}, u32[]{:S(2)}, u32[]{:S(2)}) async-start(f32[128,4,128]{2,1,0:T(4,128)} %bitcast.3), calls=%async_computation.2 | async-start | bytes 524288 | tf_op jit(solution)/shard_map/all_to_all | solution.py:51
  85.9 5.0 %all-to-all-done.2 = f32[128,4,128]{2,1,0:T(4,128)} async-done(((f32[128,4,128]{2,1,0:T(4,128)}), f32[128,4,128]{2,1,0:T(4,128)}, u32[]{:S(2)}, u32[]{:S(2)}) %all-to-all-start.2) | async-done | bytes 262176 | tf_op jit(solution)/shard_map/all_to_all | solution.py:51
  91.6 133.3 %while.40 = (s32[]{:T(128)}, f32[128,224]{0,1:T(8,128)}, f32[16,32,3,128]{3,1,2,0:T(8,128)}, f32[16,32,128]{2,1,0:T(8,128)}, s32[16,32,128]{2,1,0:T(8,128)S(1)},...) while((s32[]{:T(128)}, f32[128,224]{0,1:T(8,128)}, ...), condition=%wide.region_5.6_spmd.clone.clone.clone, body=%wide.region_2.5_spmd.sunk.clone.clone.clone.sunk | while | flops 475373568 | bytes 9795291 | solution.py:105
  91.7 2.5 fusion.101
  99.2 2.5 fusion.101
  107.6 2.5 fusion.101
  116.0 2.5 fusion.101
  141.1 2.5 fusion.101
  157.9 2.5 fusion.101
  174.7 2.5 fusion.101
  208.2 2.5 fusion.101
  216.6 2.5 fusion.101
  227.5 134.2 %while.41 = (s32[]{:T(128)}, f32[128,224]{0,1:T(8,128)}, f32[16,32,3,128]{3,1,0,2:T(8,128)}, f32[16,32,128]{2,1,0:T(8,128)}, s32[16,32,128]{2,1,0:T(8,128)S(1)},...) while((s32[]{:T(128)}, f32[128,224]{0,1:T(8,128)}, ...), condition=%wide.region_9.10_spmd.clone.clone.clone, body=%wide.region_6.9_spmd.sunk.clone.clone.clone.sunk | while | flops 475373568 | bytes 10712851 | solution.py:105
  303.0 2.5 fusion.112
  311.4 2.5 fusion.112
  319.8 2.5 fusion.112
  361.7 6.9 %all-to-all-start.5 = ((f32[128,4,128]{2,1,0:T(4,128)}), f32[128,4,128]{2,1,0:T(4,128)S(1)}, u32[]{:S(2)}, u32[]{:S(2)}) async-start(f32[128,4,128]{2,1,0:T(4,128)} %bitcast.15), calls=%async_computation.5 | async-start | bytes 524288 | tf_op jit(solution)/shard_map/all_to_all | solution.py:60
  368.7 3.4 collective-permute-start.4
  374.5 2.7 copy.63
  377.3 9.7 %all-to-all-start.4 = ((f32[512,3,128]{2,1,0:T(4,128)}), f32[512,3,128]{2,1,0:T(4,128)S(1)}, u32[]{:S(2)}, u32[]{:S(2)}) async-start(f32[512,3,128]{2,1,0:T(4,128)} %copy.63), calls=%async_computation.4 | async-start | bytes 2097152 | tf_op jit(solution)/shard_map/all_to_all | solution.py:59
  387.2 5.4 %collective-permute-start.6 = (f32[1,16,7,130]{3,1,0,2:T(8,128)S(1)}, f32[1,16,7,130]{3,1,0,2:T(8,128)S(1)}, u32[]{:S(2)}, u32[]{:S(2)}) collective-permute-start(f32[1,16,7,130]{3,1,0,2:T(8,128)S(1)} %get-tuple-element.823), channel_id=1, source_target_pairs={{1,0},{2,1},{3,2},{4,3},{5,4},{6,5},{7,6},{8,7},{9,8},{10,9},{11,1... | collective-permute-start | bytes 174728 | tf_op jit(solution)/shard_map/ppermute | solution.py:25
  394.5 5.1 %collective-permute-done.6 = f32[1,16,7,130]{3,1,0,2:T(8,128)S(1)} collective-permute-done((f32[1,16,7,130]{3,1,0,2:T(8,128)S(1)}, f32[1,16,7,130]{3,1,0,2:T(8,128)S(1)}, u32[]{:S(2)}, u32[]{:S(2)}) %collective-permute-start.6) | collective-permute-done | bytes 58272 | tf_op jit(solution)/shard_map/ppermute | solution.py:25
  399.6 4.2 %collective-permute-done.7 = f32[1,16,7,130]{3,1,0,2:T(8,128)S(1)} collective-permute-done((f32[1,16,7,130]{3,1,0,2:T(8,128)S(1)}, f32[1,16,7,130]{3,1,0,2:T(8,128)S(1)}, u32[]{:S(2)}, u32[]{:S(2)}) %collective-permute-start.7) | collective-permute-done | bytes 58272 | tf_op jit(solution)/shard_map/ppermute | solution.py:24
  (801 shorter events, 266.5 us)
Async XLA Ops:
  0.6 31.9 %copy-start = (f32[256,3,128]{2,0,1:T(8,128)S(1)}, f32[256,3,128]{2,0,1:T(8,128)}, u32[]{:S(2)}) copy-start(f32[256,3,128]{2,0,1:T(8,128)} %param.16) | copy-start | bytes 1179652
  0.6 17.8 %copy-start.1 = (s32[256,128]{1,0:T(8,128)S(1)}, s32[256,128]{1,0:T(8,128)}, u32[]{:S(2)}) copy-start(s32[256,128]{1,0:T(8,128)} %param.18) | copy-start | bytes 393220
  8.1 17.7 %all-to-all-start.1 = ((s32[128,4,1]{1,2,0:T(1,128)}), s32[128,4,1]{1,2,0:T(1,128)S(1)}, u32[]{:S(2)}, u32[]{:S(2)}) async-start(s32[128,4,1]{1,2,0:T(1,128)} %bitcast.2), calls=%async_computation.1 | async-start | bytes 131072 | tf_op jit(solution)/shard_map/all_to_all | solution.py:53
  25.7 15.4 %all-to-all-start = ((s32[128,4,128]{2,1,0:T(4,128)}), s32[128,4,128]{2,1,0:T(4,128)S(1)}, u32[]{:S(2)}, u32[]{:S(2)}) async-start(s32[128,4,128]{2,1,0:T(4,128)} %bitcast), calls=%async_computation | async-start | bytes 524288 | tf_op jit(solution)/shard_map/all_to_all | solution.py:52
  34.8 13.3 %copy-start.3 = (f32[2,16,7,128]{3,1,2,0:T(8,128)S(1)}, f32[2,16,7,128]{3,1,2,0:T(8,128)}, u32[]{:S(2)}) copy-start(f32[2,16,7,128]{3,1,2,0:T(8,128)} %param.15) | copy-start | bytes 344068
  36.3 34.6 %copy-start.2 = (f32[256,128]{1,0:T(8,128)S(1)}, f32[256,128]{1,0:T(8,128)}, u32[]{:S(2)}) copy-start(f32[256,128]{1,0:T(8,128)} %param.17) | copy-start | bytes 393220
  41.2 31.4 %all-to-all-start.3 = ((f32[512,3,128]{2,1,0:T(4,128)}), f32[512,3,128]{2,1,0:T(4,128)S(1)}, u32[]{:S(2)}, u32[]{:S(2)}) async-start(f32[512,3,128]{2,1,0:T(4,128)} %copy.57), calls=%async_computation.3 | async-start | bytes 2097152 | tf_op jit(solution)/shard_map/all_to_all | solution.py:50
  48.2 14.2 %collective-permute-start = (f32[2,16,7,1]{3,1,0,2:T(8,128)S(1)}, f32[2,16,7,1]{3,1,0,2:T(8,128)S(1)}, u32[]{:S(2)}, u32[]{:S(2)}) collective-permute-start(f32[2,16,7,1]{3,1,0,2:T(8,128)S(1)} %get-tuple-element.829), channel_id=1, source_target_pairs={{0,32},{32,64},{64,96},{1,33},{33,65},{65,97},{2,34},{34,66},{66,9... | collective-permute-start | bytes 2696 | tf_op jit(solution)/shard_map/ppermute | solution.py:24
  51.6 12.0 %collective-permute-start.1 = (f32[2,16,7,1]{3,1,0,2:T(8,128)S(1)}, f32[2,16,7,1]{3,1,0,2:T(8,128)S(1)}, u32[]{:S(2)}, u32[]{:S(2)}) collective-permute-start(f32[2,16,7,1]{3,1,0,2:T(8,128)S(1)} %get-tuple-element.828), channel_id=1, source_target_pairs={{32,0},{64,32},{96,64},{33,1},{65,33},{97,65},{34,2},{66,34},{98,6... | collective-permute-start | bytes 2696 | tf_op jit(solution)/shard_map/ppermute | solution.py:25
  63.6 21.1 %copy-start.4 = (f32[2,16,7,1]{3,1,0,2:T(8,128)}, f32[2,16,7,1]{3,1,0,2:T(8,128)S(1)}, u32[]{:S(2)}) copy-start(f32[2,16,7,1]{3,1,0,2:T(8,128)S(1)} %collective-permute-done.1) | copy-start | bytes 2692
  63.8 20.9 %collective-permute-start.2 = (f32[1,16,7,130]{3,1,0,2:T(8,128)S(1)}, f32[1,16,7,130]{3,1,0,2:T(8,128)S(1)}, u32[]{:S(2)}, u32[]{:S(2)}) collective-permute-start(f32[1,16,7,130]{3,1,0,2:T(8,128)S(1)} %get-tuple-element.825), channel_id=1, source_target_pairs={{1,0},{2,1},{3,2},{4,3},{5,4},{6,5},{7,6},{8,7},{9,8},{10,9},{11,1... | collective-permute-start | bytes 174728 | tf_op jit(solution)/shard_map/ppermute | solution.py:25
  69.0 15.7 %collective-permute-start.3 = (f32[1,16,7,130]{3,1,0,2:T(8,128)S(1)}, f32[1,16,7,130]{3,1,0,2:T(8,128)S(1)}, u32[]{:S(2)}, u32[]{:S(2)}) collective-permute-start(f32[1,16,7,130]{3,1,0,2:T(8,128)S(1)} %get-tuple-element.824), channel_id=1, source_target_pairs={{0,1},{1,2},{2,3},{3,4},{4,5},{5,6},{6,7},{7,8},{8,9},{9,10},{10,1... | collective-permute-start | bytes 174728 | tf_op jit(solution)/shard_map/ppermute | solution.py:24
  72.6 18.3 %all-to-all-start.2 = ((f32[128,4,128]{2,1,0:T(4,128)}), f32[128,4,128]{2,1,0:T(4,128)}, u32[]{:S(2)}, u32[]{:S(2)}) async-start(f32[128,4,128]{2,1,0:T(4,128)} %bitcast.3), calls=%async_computation.2 | async-start | bytes 524288 | tf_op jit(solution)/shard_map/all_to_all | solution.py:51
  83.3 8.3 %copy-start.10 = (f32[3]{0:T(128)S(1)}, f32[3]{0:T(128)}, u32[]{:S(2)}) copy-start(f32[3]{0:T(128)} %param.21) | copy-start | bytes 40
  83.3 8.3 %copy-start.11 = (f32[3]{0:T(128)S(1)}, f32[3]{0:T(128)}, u32[]{:S(2)}) copy-start(f32[3]{0:T(128)} %constant.211.clone..sunk.8) | copy-start | bytes 40
  83.3 8.3 %copy-start.13 = (f32[3]{0:T(128)S(1)}, f32[3]{0:T(128)}, u32[]{:S(2)}) copy-start(f32[3]{0:T(128)} %param.22) | copy-start | bytes 40
  91.6 133.3 %copy-start.12 = (f32[7]{0:T(128)S(1)}, f32[7]{0:T(128)}, u32[]{:S(2)}) copy-start(f32[7]{0:T(128)} %param.23) | copy-start | bytes 88
  281.0 3.7 copy-start.7
  289.4 3.7 copy-start.7
  306.1 3.7 copy-start.7
  314.5 3.7 copy-start.7
  322.9 3.7 copy-start.7
  339.7 3.7 copy-start.7
  348.1 3.7 copy-start.7
  356.5 3.7 copy-start.7
  361.7 15.6 %all-to-all-start.5 = ((f32[128,4,128]{2,1,0:T(4,128)}), f32[128,4,128]{2,1,0:T(4,128)S(1)}, u32[]{:S(2)}, u32[]{:S(2)}) async-start(f32[128,4,128]{2,1,0:T(4,128)} %bitcast.15), calls=%async_computation.5 | async-start | bytes 524288 | tf_op jit(solution)/shard_map/all_to_all | solution.py:60
  368.7 18.3 %collective-permute-start.4 = (f32[2,16,7,1]{3,1,0,2:T(8,128)S(1)}, f32[2,16,7,1]{3,1,0,2:T(8,128)S(1)}, u32[]{:S(2)}, u32[]{:S(2)}) collective-permute-start(f32[2,16,7,1]{3,1,0,2:T(8,128)S(1)} %get-tuple-element.827), channel_id=1, source_target_pairs={{0,32},{32,64},{64,96},{1,33},{33,65},{65,97},{2,34},{34,66},{66,9... | collective-permute-start | bytes 2696 | tf_op jit(solution)/shard_map/ppermute | solution.py:24
  372.1 14.9 %collective-permute-start.5 = (f32[2,16,7,1]{3,1,0,2:T(8,128)S(1)}, f32[2,16,7,1]{3,1,0,2:T(8,128)S(1)}, u32[]{:S(2)}, u32[]{:S(2)}) collective-permute-start(f32[2,16,7,1]{3,1,0,2:T(8,128)S(1)} %get-tuple-element.826), channel_id=1, source_target_pairs={{32,0},{64,32},{96,64},{33,1},{65,33},{97,65},{34,2},{66,34},{98,6... | collective-permute-start | bytes 2696 | tf_op jit(solution)/shard_map/ppermute | solution.py:25
  377.2 26.9 %copy-start.9 = (f32[128,224]{0,1:T(8,128)S(1)}, f32[128,224]{0,1:T(8,128)}, u32[]{:S(2)}) copy-start(f32[128,224]{0,1:T(8,128)} %get-tuple-element.444) | copy-start | bytes 344068
  377.3 29.1 %all-to-all-start.4 = ((f32[512,3,128]{2,1,0:T(4,128)}), f32[512,3,128]{2,1,0:T(4,128)S(1)}, u32[]{:S(2)}, u32[]{:S(2)}) async-start(f32[512,3,128]{2,1,0:T(4,128)} %copy.63), calls=%async_computation.4 | async-start | bytes 2097152 | tf_op jit(solution)/shard_map/all_to_all | solution.py:59
  387.2 12.4 %collective-permute-start.6 = (f32[1,16,7,130]{3,1,0,2:T(8,128)S(1)}, f32[1,16,7,130]{3,1,0,2:T(8,128)S(1)}, u32[]{:S(2)}, u32[]{:S(2)}) collective-permute-start(f32[1,16,7,130]{3,1,0,2:T(8,128)S(1)} %get-tuple-element.823), channel_id=1, source_target_pairs={{1,0},{2,1},{3,2},{4,3},{5,4},{6,5},{7,6},{8,7},{9,8},{10,9},{11,1... | collective-permute-start | bytes 174728 | tf_op jit(solution)/shard_map/ppermute | solution.py:25
  392.6 11.2 %collective-permute-start.7 = (f32[1,16,7,130]{3,1,0,2:T(8,128)S(1)}, f32[1,16,7,130]{3,1,0,2:T(8,128)S(1)}, u32[]{:S(2)}, u32[]{:S(2)}) collective-permute-start(f32[1,16,7,130]{3,1,0,2:T(8,128)S(1)} %get-tuple-element.822), channel_id=1, source_target_pairs={{0,1},{1,2},{2,3},{3,4},{4,5},{5,6},{6,7},{7,8},{8,9},{9,10},{10,1... | collective-permute-start | bytes 174728 | tf_op jit(solution)/shard_map/ppermute | solution.py:24
  (26 other events, 42.0 us)
where the time goes:
time: 413 us; the launch traced here: 408 us
  matrix products  130 us (31%)
  other arithmetic  95 us (23%)
  starting transfers between devices  76.6 us (19%)
  local copies, waits for them, and re-layouts  67 us (16%)
  waiting for transfers between devices  34.4 us (8%)
    dot_general x32, matrix products, turn(): jnp.dot(pick_z, table, preferred_element_type=jnp.bfloat16)  78.8 us
    dot_general x32, matrix products, turn(): lax.dot_general(pick_z, spread, (((0,), (0,)), ((), ())), preferred_eleme...  51.5 us
    dynamic_update_slice x32, other arithmetic, couple(): acc, (new_velo, new_radi) = lax.scan(turn, start, items)  44.8 us
    while x96, local copies, waits for them, and re-layouts  23.2 us
    dynamic_update_slice x32, local copies, waits for them, and re-layouts, couple(): acc, (new_velo, new_radi) = lax.scan(turn, start, items)  20.1 us
    reduce_sum x32, other arithmetic, turn(): probe = jnp.sum((lifted * pick_col[:, None, :]).astype(jnp.float32), axis=2)  17.9 us
    ppermute x4, starting transfers between devices, with_halo(): after = lax.ppermute(first, axis, down)  15.4 us
    ppermute x4, waiting for transfers between devices, with_halo(): before = lax.ppermute(last, axis, up)  12.6 us
  transfers between devices with their start and end apart: 14, of which 8 were waited for; matrix products, arithmetic and copies ran while one was open for 4% of the time, Pallas kernels for 0%

commit v1 on v0

v1 whole, which is shorter than its diff:
```python
import jax
import jax.numpy as jnp
from jax import lax
from jax.experimental import pallas as pl
from jax.experimental.pallas import tpu as pltpu
from jax.sharding import PartitionSpec as P

AXES = ("sec", "brick")
CAP = 4
LANES = 128
COMPS = 7
SEND = 5
BACK = 4
GROUP = 8

GROW = 0.4
DRAG = 0.25
MOMENT = 0.4
LATENT = 0.5
SETTLE = 0.1

VMEM = pl.BlockSpec(memory_space=pltpu.VMEM)
SMEM = pl.BlockSpec(memory_space=pltpu.SMEM)
LIMIT = 48 * 2**20


def pack_kernel(target, count, velo, radi, cell, sent, slot_of, seen):
    blocks = radi.shape[0]
    bricks = seen.shape[0]
    sent[...] = jnp.full(sent.shape, -1.0, jnp.float32)
    lane = lax.broadcasted_iota(jnp.int32, (1, LANES), 1)

    def clear(i, _):
        seen[i] = 0
        return 0

    lax.fori_loop(0, bricks, clear, 0, unroll=8)

    def place(k, _):
        brick = target[k]
        rank = seen[brick]
        seen[brick] = rank + 1
        slot = brick * CAP + rank
        slot_of[k] = slot
        row = slot * SEND
        for c in range(3):
            sent[pl.ds(row + c, 1), :] = velo[k, pl.ds(c, 1), :]
        sent[pl.ds(row + 3, 1), :] = radi[pl.ds(k, 1), :]
        where = cell[pl.ds(k, 1), :].astype(jnp.float32)
        sent[pl.ds(row + 4, 1), :] = jnp.where(lane < count[k], where, -1.0)
        return 0

    lax.fori_loop(0, blocks, place, 0, unroll=4)


def unpack_kernel(slot_of, back, velo, radi):
    blocks = radi.shape[0]

    def place(k, _):
        row = slot_of[k] * BACK
        for c in range(3):
            velo[k, pl.ds(c, 1), :] = back[pl.ds(row + c, 1), :]
        radi[pl.ds(k, 1), :] = back[pl.ds(row + 3, 1), :]
        return 0

    lax.fori_loop(0, blocks, place, 0, unroll=4)


def diffused(melt, low_x, high_x, low_z, high_z, rate):
    rows, size_z = melt.shape
    size_y = low_x.shape[0]
    lane = lax.broadcasted_iota(jnp.int32, (rows, size_z), 1)
    level = lax.broadcasted_iota(jnp.int32, (rows, size_z), 0) % size_y
    below_x = jnp.concatenate([low_x, melt[:-size_y]], axis=0)
    above_x = jnp.concatenate([melt[size_y:], high_x], axis=0)
    below_y = jnp.where(level == 0, 0.0, pltpu.roll(melt, 1, 0))
    above_y = jnp.where(level == size_y - 1, 0.0, pltpu.roll(melt, rows - 1, 0))
    below_z = jnp.where(lane == 0, low_z, pltpu.roll(melt, 1, 1))
    above_z = jnp.where(lane == size_z - 1, high_z, pltpu.roll(melt, size_z - 1, 1))
    beside = above_x + below_x + above_y + below_y + above_z + below_z
    return melt + rate * (beside - 6.0 * melt)


def deposit_of(acc, comp, size_x, size_y):
    part = acc[comp * size_y : (comp + 1) * size_y, :]
    size_z = part.shape[1] // size_x
    return jnp.concatenate(
        [part[:, x * size_z : (x + 1) * size_z] for x in range(size_x)], axis=0
    )


def steps_kernel(
    slope, partition, rate, got, melt, low_x, high_x, low_z, high_z, back, melt_mid, acc, table
):
    size_y = low_x.shape[1]
    columns = melt.shape[1]
    size_z = melt.shape[2]
    size_x = columns // size_y
    groups = got.shape[0] // (SEND * GROUP)
    row_iota = lax.broadcasted_iota(jnp.int32, (size_x * size_z, LANES), 0)
    y_iota = lax.broadcasted_iota(jnp.int32, (size_y, LANES), 0)

    def one_step(first):
        acc[...] = jnp.zeros_like(acc)

        def group(g, _):
            def rows(field):
                if first:
                    return got[pl.ds(g * (SEND * GROUP) + field, GROUP, stride=SEND), :]
                return back[pl.ds(g * (BACK * GROUP) + field, GROUP, stride=BACK), :]

            cell = got[pl.ds(g * (SEND * GROUP) + 4, GROUP, stride=SEND), :].astype(jnp.int32)
            live = cell >= 0
            z = cell & (size_z - 1)
            column = cell >> 7
            probe = [jnp.zeros((GROUP, LANES), jnp.float32)] * COMPS
            for j in range(columns):
                here = column == j
                for c in range(COMPS):
                    line = jnp.broadcast_to(table[c, j : j + 1, :], (GROUP, LANES))
                    picked = jnp.take_along_axis(line, z, axis=1)
                    probe[c] = jnp.where(here, picked, probe[c])
            velo = [rows(0), rows(1), rows(2)]
            radi = rows(3)
            under = (
                probe[4] * slope[0] + probe[5] * slope[1] + probe[6] * slope[2]
            ) - probe[3]
            growth = GROW * (jnp.maximum(under, 0.0) + jnp.log1p(jnp.exp(-jnp.abs(under))))
            beta = DRAG / (radi * radi)
            push = -(MOMENT * radi * radi * radi * beta)
            slip = [probe[c] - velo[c] for c in range(3)]
            fed = growth * radi
            sources = [push * slip[c] for c in range(3)] + [LATENT * growth * radi]
            sources += [(1.0 - partition[s]) * probe[4 + s] * fed for s in range(3)]
            new_velo = [velo[c] + beta * slip[c] for c in range(3)]
            new_velo[2] = new_velo[2] - SETTLE * radi
            new_radi = radi + growth / radi
            base = g * (BACK * GROUP)
            for c in range(3):
                back[pl.ds(base + c, GROUP, stride=BACK), :] = jnp.where(live, new_velo[c], velo[c])
            back[pl.ds(base + 3, GROUP, stride=BACK), :] = jnp.where(live, new_radi, radi)
            y = jnp.where(live, column & (size_y - 1), size_y)
            line = ((column >> 4) * size_z) | z
            lefts, rights = [], []
            for b in range(GROUP):
                mask = y_iota == y[b : b + 1, :]
                lefts.append(
                    jnp.concatenate(
                        [jnp.where(mask, s[b : b + 1, :], 0.0).astype(jnp.bfloat16) for s in sources],
                        axis=0,
                    )
                )
                rights.append((row_iota == line[b : b + 1, :]).astype(jnp.bfloat16))
            left = jnp.concatenate(lefts, axis=1)
            right = jnp.concatenate(rights, axis=1)
            acc[...] += lax.dot_general(
                left, right, (((1,), (1,)), ((), ())), preferred_element_type=jnp.float32
            )
            return 0

        lax.fori_loop(0, groups, group, 0)

    table[...] = melt[...].astype(jnp.bfloat16).astype(jnp.float32)
    one_step(True)
    for c in range(COMPS):
        fresh = diffused(melt[c], low_x[c], high_x[c], low_z[c], high_z[c], rate[c])
        fresh = fresh + deposit_of(acc, c, size_x, size_y)
        melt_mid[c] = fresh
        table[c] = fresh.astype(jnp.bfloat16).astype(jnp.float32)
    one_step(False)


def finish_kernel(rate, melt, acc, low_x, high_x, low_z, high_z, out):
    size_y = low_x.shape[1]
    size_x = melt.shape[1] // size_y
    for c in range(COMPS):
        fresh = diffused(melt[c], low_x[c], high_x[c], low_z[c], high_z[c], rate[c])
        out[c] = fresh + deposit_of(acc, c, size_x, size_y)


def kernel_call(kernel, outs, in_specs, out_specs, scratch=()):
    return pl.pallas_call(
        kernel,
        out_shape=outs,
        in_specs=in_specs,
        out_specs=out_specs,
        scratch_shapes=list(scratch),
        compiler_params=pltpu.CompilerParams(vmem_limit_bytes=LIMIT),
    )


def shape(*dims):
    return jax.ShapeDtypeStruct(dims, jnp.float32)


def neighbours(melt, size_y):
    def shift(edge, axis, step):
        n = lax.axis_size(axis)
        return lax.ppermute(edge, axis, [(i, i + step) for i in range(n) if 0 <= i + step < n])

    low_x = shift(melt[:, -size_y:, :], "brick", 1)
    high_x = shift(melt[:, :size_y, :], "brick", -1)
    low_z = shift(melt[:, :, -1], "sec", 1)[:, :, None]
    high_z = shift(melt[:, :, 0], "sec", -1)[:, :, None]
    return low_x, high_x, low_z, high_z


def run_steps(got, melt, halo, slope, partition, rate, size_y):
    comps, columns, size_z = melt.shape
    size_x = columns // size_y
    slots = got.shape[0] // SEND
    return kernel_call(
        steps_kernel,
        (
            shape(slots * BACK, LANES),
            shape(comps, columns, size_z),
            shape(comps * size_y, size_x * size_z),
        ),
        [SMEM, SMEM, SMEM] + [VMEM] * 6,
        (VMEM, VMEM, VMEM),
        [pltpu.VMEM((comps, columns, size_z), jnp.float32)],
    )(slope, partition, rate, got, melt, *halo)


def exchange(rows, devices):
    each = rows.shape[0] // CAP
    swapped = lax.all_to_all(
        rows.reshape(each, CAP, LANES), AXES, split_axis=0, concat_axis=0, tiled=True
    )
    return swapped.reshape(rows.shape)


def local(melt, velocity, radius, cell, target, count, slope, partition, rate):
    devices = lax.axis_size(AXES)
    size_x, size_y, comps, size_z = melt.shape
    blocks = target.shape[0]
    slots = devices * CAP
    sent, slot_of = kernel_call(
        pack_kernel,
        (shape(slots * SEND, LANES), jax.ShapeDtypeStruct((blocks,), jnp.int32)),
        [SMEM, SMEM, VMEM, VMEM, VMEM],
        (VMEM, SMEM),
        [pltpu.SMEM((devices,), jnp.int32)],
    )(target, count, velocity, radius, cell)
    got = exchange(sent, devices)
    start = jnp.transpose(melt, (2, 0, 1, 3)).reshape(comps, size_x * size_y, size_z)
    halo = neighbours(start, size_y)
    back, middle, acc = run_steps(got, start, halo, slope, partition, rate, size_y)
    returned = exchange(back, devices)
    halo = neighbours(middle, size_y)
    final = kernel_call(
        finish_kernel,
        shape(comps, size_x * size_y, size_z),
        [SMEM] + [VMEM] * 6,
        VMEM,
    )(rate, middle, acc, *halo)
    melt_out = jnp.transpose(final.reshape(comps, size_x, size_y, size_z), (1, 2, 0, 3))
    velocity_out, radius_out = kernel_call(
        unpack_kernel,
        (shape(blocks, 3, LANES), shape(blocks, LANES)),
        [SMEM, VMEM],
        (VMEM, VMEM),
    )(slot_of, returned)
    return melt_out, velocity_out, radius_out


def solution(mesh):
    return jax.shard_map(
        local,
        mesh=mesh,
        in_specs=(
            P("brick", None, None, "sec"),
            P(AXES, None, None),
            P(AXES, None),
            P(AXES, None),
            P(AXES),
            P(AXES),
            P(),
            P(),
            P(),
        ),
        out_specs=(P("brick", None, None, "sec"), P(AXES, None, None), P(AXES, None)),
        check_vma=False,
    )
```

time: 413 us -> 134 us (0.32)
  matrix products: 130 us -> 0 us
  other arithmetic: 95 us -> 0 us
  Pallas kernels: 0 us -> 70.1 us
  local copies, waits for them, and re-layouts: 67 us -> 6.76 us
  starting transfers between devices: 76.6 us -> 45.3 us
  waiting for transfers between devices: 34.4 us -> 8.02 us
    dot_general x64 -> x0, matrix products: 130 us -> none  [the longest x32 78.8 us: turn(): jnp.dot(pick_z, table, preferred_element_type=jnp.bfloat16)]
    pallas_call x0 -> x4, Pallas kernels: none -> 70.1 us  [the longest x1 64.1 us: run_steps(): kernel_call(steps_kernel, (shape(slots * BACK, LANES), shape(comps, colum...]
    dynamic_update_slice x32 -> x0, other arithmetic: 44.8 us -> none  [couple(): acc, (new_velo, new_radi) = lax.scan(turn, start, items)]
    all_to_all x6 -> x2, starting transfers between devices: 50.5 us -> 18.3 us  [exchange(): lax.all_to_all(rows.reshape(each, CAP, LANES), AXES, split_axis=0, concat...]
    while x96 -> x0, local copies, waits for them, and re-layouts: 23.2 us -> none
    reduce_sum x65 -> x0, other arithmetic: 22.4 us -> none  [the longest x32 17.9 us: turn(): probe = jnp.sum((lifted * pick_col[:, None, :]).astype(jnp.float32), axis=2)]
    dynamic_update_slice x32 -> x0, local copies, waits for them, and re-layouts: 20.1 us -> none  [couple(): acc, (new_velo, new_radi) = lax.scan(turn, start, items)]
    all_to_all x6 -> x2, waiting for transfers between devices: 15.5 us -> 0.01 us  [exchange(): lax.all_to_all(rows.reshape(each, CAP, LANES), AXES, split_axis=0, concat...]
  transfers between devices with their start and end apart: 14 -> 10, of which waited for: 8 -> 3; matrix products, arithmetic and copies ran while one was open for 4% -> 1% of each run, Pallas kernels for 0% -> 1%
where the time goes in v1:
time: 134 us; the launch traced here: 131 us
  Pallas kernels  70.1 us (52%)
  starting transfers between devices  45.3 us (34%)
  waiting for transfers between devices  8.02 us (6%)
  local copies, waits for them, and re-layouts  6.76 us (5%)
    pallas_call x1, Pallas kernels, run_steps(): kernel_call(steps_kernel, (shape(slots * BACK, LANES), shape(comps, colum...  64.1 us
    ppermute x8, starting transfers between devices, shift(): lax.ppermute(edge, axis, [(i, i + step) for i in range(n) if 0 <= i + ste...  27 us
    all_to_all x2, starting transfers between devices, exchange(): lax.all_to_all(rows.reshape(each, CAP, LANES), AXES, split_axis=0, concat...  18.3 us
    ppermute x8, waiting for transfers between devices, shift(): lax.ppermute(edge, axis, [(i, i + step) for i in range(n) if 0 <= i + ste...  8.01 us
    unnamed x19, local copies, waits for them, and re-layouts  5.23 us
    pallas_call x1, Pallas kernels, local(): kernel_call(pack_kernel, (shape(slots * SEND, LANES), jax.ShapeDtypeStruc...  3.36 us
  transfers between devices with their start and end apart: 10, of which 3 were waited for; matrix products, arithmetic and copies ran while one was open for 1% of the time, Pallas kernels for 1%

profile of v1, /device:TPU:14, one launch (start us, length us, event | category | flops | bytes accessed | tf_op | source)
XLA Modules:
  0.0 131.1 jit_solution(8650181404109238512)
XLA Ops:
  0.6 1.3 copy.38.velo
  1.9 0.9 copy-done
  2.8 0.9 copy-done.1
  3.7 0.7 copy-done.3
  4.4 0.7 copy-done.4
  5.1 3.4 %shard_map.112 = (f32[2560,128]{1,0:T(8,128)}, s32[256]{0:T(256)S(1)}) custom-call(s32[256]{0:T(256)S(1)} %copy-done.3, s32[256]{0:T(256)S(1)} %copy-done.4, f32[256,3,128]{2,1,0:T(4,128)S(1)} %copy.38.velo, f32[256,128]{1,0:T(8,128)S(1)} %copy-done, s32[256,128]{1,0:T(8,128)S(1)} %copy-done.1), custom_call_target="tpu_custom_call" | custom-call | tf_op jit(solution)/shard_map/pallas_call | solution.py:238
  8.4 0.0 copy-start.7
  8.5 0.0 copy-start.5
  8.5 10.4 %all-to-all-start = ((f32[640,4,128]{2,1,0:T(4,128)}), f32[640,4,128]{2,1,0:T(4,128)S(1)}, u32[]{:S(2)}, u32[]{:S(2)}) async-start(f32[640,4,128]{2,1,0:T(4,128)} %bitcast), calls=%async_computation | async-start | bytes 2621440 | tf_op jit(solution)/shard_map/all_to_all | solution.py:227
  18.9 2.1 %collective-permute-start = (f32[7,16,128]{2,1,0:T(8,128)S(1)}, f32[7,16,128]{2,1,0:T(8,128)S(1)}, u32[]{:S(2)}, u32[]{:S(2)}) collective-permute-start(f32[7,16,128]{2,1,0:T(8,128)S(1)} %get-tuple-element.36), channel_id=1, source_target_pairs={{0,1},{1,2},{2,3},{3,4},{4,5},{5,6},{6,7},{7,8},{8,9},{9,10},{10,1... | collective-permute-start | bytes 172040 | tf_op jit(solution)/shard_map/ppermute | solution.py:199
  21.0 5.6 %collective-permute-start.1 = (f32[7,16,128]{2,1,0:T(8,128)S(1)}, f32[7,16,128]{2,1,0:T(8,128)S(1)}, u32[]{:S(2)}, u32[]{:S(2)}) collective-permute-start(f32[7,16,128]{2,1,0:T(8,128)S(1)} %get-tuple-element.35), channel_id=1, source_target_pairs={{1,0},{2,1},{3,2},{4,3},{5,4},{6,5},{7,6},{8,7},{9,8},{10,9},{11,1... | collective-permute-start | bytes 172040 | tf_op jit(solution)/shard_map/ppermute | solution.py:199
  26.6 0.2 slice_reduce_fusion
  26.8 3.4 %collective-permute-start.2 = (f32[7,32]{1,0:T(8,128)S(1)}, f32[7,32]{1,0:T(8,128)S(1)}, u32[]{:S(2)}, u32[]{:S(2)}) collective-permute-start(f32[7,32]{1,0:T(8,128)S(1)} %get-tuple-element.32), channel_id=1, source_target_pairs={{0,32},{32,64},{64,96},{1,33},{33,65},{65,97},{2,34},{34,66},{66,9... | collective-permute-start | bytes 2696 | tf_op jit(solution)/shard_map/ppermute | solution.py:199
  30.2 2.4 %collective-permute-start.3 = (f32[7,32]{1,0:T(8,128)S(1)}, f32[7,32]{1,0:T(8,128)S(1)}, u32[]{:S(2)}, u32[]{:S(2)}) collective-permute-start(f32[7,32]{1,0:T(8,128)S(1)} %get-tuple-element.31), channel_id=1, source_target_pairs={{32,0},{64,32},{96,64},{33,1},{65,33},{97,65},{34,2},{66,34},{98,6... | collective-permute-start | bytes 2696 | tf_op jit(solution)/shard_map/ppermute | solution.py:199
  32.7 0.1 copy.40.low_z
  32.8 3.0 %collective-permute-done.3 = f32[7,32]{1,0:T(8,128)S(1)} collective-permute-done((f32[7,32]{1,0:T(8,128)S(1)}, f32[7,32]{1,0:T(8,128)S(1)}, u32[]{:S(2)}, u32[]{:S(2)}) %collective-permute-start.3) | collective-permute-done | bytes 928 | tf_op jit(solution)/shard_map/ppermute | solution.py:199
  35.7 0.1 copy.41.high_z
  35.9 2.1 %collective-permute-done.low_x = f32[7,16,128]{2,1,0:T(8,128)S(1)} collective-permute-done((f32[7,16,128]{2,1,0:T(8,128)S(1)}, f32[7,16,128]{2,1,0:T(8,128)S(1)}, u32[]{:S(2)}, u32[]{:S(2)}) %collective-permute-start) | collective-permute-done | bytes 57376 | tf_op jit(solution)/shard_map/ppermute | solution.py:199
  38.0 64.1 %shard_map.113 = (f32[2048,128]{1,0:T(8,128)}, f32[7,32,128]{2,1,0:T(8,128)S(1)}, f32[112,256]{1,0:T(8,128)S(1)}) custom-call(f32[3]{0:T(128)S(1)} %copy-done.5, f32[3]{0:T(128)S(1)} %copy-done.6, f32[7]{0:T(128)S(1)} %copy-done.2, f32[2560,128]{1,0:T(8,128)S(1)} %bitcast.15, f32[7,32,128]{2,1,0:T(8,128)S(1)} %bitcast.19, ...), custom_call_target="tpu_custom_call" | custom-call | tf_op jit(solution)/shard_map/pallas_call | solution.py:212
  102.1 7.9 %all-to-all-start.1 = ((f32[512,4,128]{2,1,0:T(4,128)}), f32[512,4,128]{2,1,0:T(4,128)S(1)}, u32[]{:S(2)}, u32[]{:S(2)}) async-start(f32[512,4,128]{2,1,0:T(4,128)} %bitcast.11), calls=%async_computation.1 | async-start | bytes 2097152 | tf_op jit(solution)/shard_map/all_to_all | solution.py:227
  110.0 2.1 %collective-permute-start.4 = (f32[7,16,128]{2,1,0:T(8,128)S(1)}, f32[7,16,128]{2,1,0:T(8,128)S(1)}, u32[]{:S(2)}, u32[]{:S(2)}) collective-permute-start(f32[7,16,128]{2,1,0:T(8,128)S(1)} %get-tuple-element.34), channel_id=1, source_target_pairs={{0,1},{1,2},{2,3},{3,4},{4,5},{5,6},{6,7},{7,8},{8,9},{9,10},{10,1... | collective-permute-start | bytes 172040 | tf_op jit(solution)/shard_map/ppermute | solution.py:199
  112.1 5.6 %collective-permute-start.5 = (f32[7,16,128]{2,1,0:T(8,128)S(1)}, f32[7,16,128]{2,1,0:T(8,128)S(1)}, u32[]{:S(2)}, u32[]{:S(2)}) collective-permute-start(f32[7,16,128]{2,1,0:T(8,128)S(1)} %get-tuple-element.33), channel_id=1, source_target_pairs={{1,0},{2,1},{3,2},{4,3},{5,4},{6,5},{7,6},{8,7},{9,8},{10,9},{11,1... | collective-permute-start | bytes 172040 | tf_op jit(solution)/shard_map/ppermute | solution.py:199
  117.7 0.2 slice_reduce_fusion.2
  117.9 3.4 %collective-permute-start.6 = (f32[7,32]{1,0:T(8,128)S(1)}, f32[7,32]{1,0:T(8,128)S(1)}, u32[]{:S(2)}, u32[]{:S(2)}) collective-permute-start(f32[7,32]{1,0:T(8,128)S(1)} %get-tuple-element.30), channel_id=1, source_target_pairs={{0,32},{32,64},{64,96},{1,33},{33,65},{65,97},{2,34},{34,66},{66,9... | collective-permute-start | bytes 2696 | tf_op jit(solution)/shard_map/ppermute | solution.py:199
  121.3 2.4 %collective-permute-start.7 = (f32[7,32]{1,0:T(8,128)S(1)}, f32[7,32]{1,0:T(8,128)S(1)}, u32[]{:S(2)}, u32[]{:S(2)}) collective-permute-start(f32[7,32]{1,0:T(8,128)S(1)} %get-tuple-element.29), channel_id=1, source_target_pairs={{32,0},{64,32},{96,64},{33,1},{65,33},{97,65},{34,2},{66,34},{98,6... | collective-permute-start | bytes 2696 | tf_op jit(solution)/shard_map/ppermute | solution.py:199
  123.8 0.1 copy.42.low_z
  123.9 3.0 %collective-permute-done.7 = f32[7,32]{1,0:T(8,128)S(1)} collective-permute-done((f32[7,32]{1,0:T(8,128)S(1)}, f32[7,32]{1,0:T(8,128)S(1)}, u32[]{:S(2)}, u32[]{:S(2)}) %collective-permute-start.7) | collective-permute-done | bytes 928 | tf_op jit(solution)/shard_map/ppermute | solution.py:199
  126.8 0.1 copy.43.high_z
  127.0 0.7 shard_map.114
  127.7 0.7 copy.47
  128.4 1.9 %shard_map.115 = (f32[256,3,128]{2,1,0:T(4,128)S(1)}, f32[256,128]{1,0:T(8,128)}) custom-call(s32[256]{0:T(256)S(1)} %get-tuple-element.13.slot_of, f32[2048,128]{1,0:T(8,128)S(1)} %bitcast.16), custom_call_target="tpu_custom_call" | custom-call | tf_op jit(solution)/shard_map/pallas_call | solution.py:258
  130.3 0.8 copy.45
  (20 shorter events, 0.1 us)
Async XLA Ops:
  1.9 0.9 copy-start
  2.8 0.9 copy-start.1
  3.7 0.7 copy-start.3
  4.4 0.7 copy-start.4
  8.4 10.4 %copy-start.7 = (f32[2,16,7,128]{3,1,2,0:T(8,128)S(1)}, f32[2,16,7,128]{3,1,2,0:T(8,128)}, u32[]{:S(2)}) copy-start(f32[2,16,7,128]{3,1,2,0:T(8,128)} %param.9) | copy-start | bytes 344068
  8.5 29.5 %copy-start.2 = (f32[7]{0:T(128)S(1)}, f32[7]{0:T(128)}, u32[]{:S(2)}) copy-start(f32[7]{0:T(128)} %rate.3) | copy-start | bytes 88
  8.5 29.5 %copy-start.5 = (f32[3]{0:T(128)S(1)}, f32[3]{0:T(128)}, u32[]{:S(2)}) copy-start(f32[3]{0:T(128)} %slope.1) | copy-start | bytes 40
  8.5 29.5 %copy-start.6 = (f32[3]{0:T(128)S(1)}, f32[3]{0:T(128)}, u32[]{:S(2)}) copy-start(f32[3]{0:T(128)} %partition.1) | copy-start | bytes 40
  8.5 29.5 %all-to-all-start = ((f32[640,4,128]{2,1,0:T(4,128)}), f32[640,4,128]{2,1,0:T(4,128)S(1)}, u32[]{:S(2)}, u32[]{:S(2)}) async-start(f32[640,4,128]{2,1,0:T(4,128)} %bitcast), calls=%async_computation | async-start | bytes 2621440 | tf_op jit(solution)/shard_map/all_to_all | solution.py:227
  18.9 19.0 %collective-permute-start = (f32[7,16,128]{2,1,0:T(8,128)S(1)}, f32[7,16,128]{2,1,0:T(8,128)S(1)}, u32[]{:S(2)}, u32[]{:S(2)}) collective-permute-start(f32[7,16,128]{2,1,0:T(8,128)S(1)} %get-tuple-element.36), channel_id=1, source_target_pairs={{0,1},{1,2},{2,3},{3,4},{4,5},{5,6},{6,7},{7,8},{8,9},{9,10},{10,1... | collective-permute-start | bytes 172040 | tf_op jit(solution)/shard_map/ppermute | solution.py:199
  21.0 17.0 %collective-permute-start.1 = (f32[7,16,128]{2,1,0:T(8,128)S(1)}, f32[7,16,128]{2,1,0:T(8,128)S(1)}, u32[]{:S(2)}, u32[]{:S(2)}) collective-permute-start(f32[7,16,128]{2,1,0:T(8,128)S(1)} %get-tuple-element.35), channel_id=1, source_target_pairs={{1,0},{2,1},{3,2},{4,3},{5,4},{6,5},{7,6},{8,7},{9,8},{10,9},{11,1... | collective-permute-start | bytes 172040 | tf_op jit(solution)/shard_map/ppermute | solution.py:199
  26.8 5.9 %collective-permute-start.2 = (f32[7,32]{1,0:T(8,128)S(1)}, f32[7,32]{1,0:T(8,128)S(1)}, u32[]{:S(2)}, u32[]{:S(2)}) collective-permute-start(f32[7,32]{1,0:T(8,128)S(1)} %get-tuple-element.32), channel_id=1, source_target_pairs={{0,32},{32,64},{64,96},{1,33},{33,65},{65,97},{2,34},{34,66},{66,9... | collective-permute-start | bytes 2696 | tf_op jit(solution)/shard_map/ppermute | solution.py:199
  30.2 5.5 %collective-permute-start.3 = (f32[7,32]{1,0:T(8,128)S(1)}, f32[7,32]{1,0:T(8,128)S(1)}, u32[]{:S(2)}, u32[]{:S(2)}) collective-permute-start(f32[7,32]{1,0:T(8,128)S(1)} %get-tuple-element.31), channel_id=1, source_target_pairs={{32,0},{64,32},{96,64},{33,1},{65,33},{97,65},{34,2},{66,34},{98,6... | collective-permute-start | bytes 2696 | tf_op jit(solution)/shard_map/ppermute | solution.py:199
  102.1 26.3 %all-to-all-start.1 = ((f32[512,4,128]{2,1,0:T(4,128)}), f32[512,4,128]{2,1,0:T(4,128)S(1)}, u32[]{:S(2)}, u32[]{:S(2)}) async-start(f32[512,4,128]{2,1,0:T(4,128)} %bitcast.11), calls=%async_computation.1 | async-start | bytes 2097152 | tf_op jit(solution)/shard_map/all_to_all | solution.py:227
  110.0 17.0 %collective-permute-start.4 = (f32[7,16,128]{2,1,0:T(8,128)S(1)}, f32[7,16,128]{2,1,0:T(8,128)S(1)}, u32[]{:S(2)}, u32[]{:S(2)}) collective-permute-start(f32[7,16,128]{2,1,0:T(8,128)S(1)} %get-tuple-element.34), channel_id=1, source_target_pairs={{0,1},{1,2},{2,3},{3,4},{4,5},{5,6},{6,7},{7,8},{8,9},{9,10},{10,1... | collective-permute-start | bytes 172040 | tf_op jit(solution)/shard_map/ppermute | solution.py:199
  112.1 14.9 %collective-permute-start.5 = (f32[7,16,128]{2,1,0:T(8,128)S(1)}, f32[7,16,128]{2,1,0:T(8,128)S(1)}, u32[]{:S(2)}, u32[]{:S(2)}) collective-permute-start(f32[7,16,128]{2,1,0:T(8,128)S(1)} %get-tuple-element.33), channel_id=1, source_target_pairs={{1,0},{2,1},{3,2},{4,3},{5,4},{6,5},{7,6},{8,7},{9,8},{10,9},{11,1... | collective-permute-start | bytes 172040 | tf_op jit(solution)/shard_map/ppermute | solution.py:199
  117.9 5.9 %collective-permute-start.6 = (f32[7,32]{1,0:T(8,128)S(1)}, f32[7,32]{1,0:T(8,128)S(1)}, u32[]{:S(2)}, u32[]{:S(2)}) collective-permute-start(f32[7,32]{1,0:T(8,128)S(1)} %get-tuple-element.30), channel_id=1, source_target_pairs={{0,32},{32,64},{64,96},{1,33},{33,65},{65,97},{2,34},{34,66},{66,9... | collective-permute-start | bytes 2696 | tf_op jit(solution)/shard_map/ppermute | solution.py:199
  121.3 5.5 %collective-permute-start.7 = (f32[7,32]{1,0:T(8,128)S(1)}, f32[7,32]{1,0:T(8,128)S(1)}, u32[]{:S(2)}, u32[]{:S(2)}) collective-permute-start(f32[7,32]{1,0:T(8,128)S(1)} %get-tuple-element.29), channel_id=1, source_target_pairs={{32,0},{64,32},{96,64},{33,1},{65,33},{97,65},{34,2},{66,34},{98,6... | collective-permute-start | bytes 2696 | tf_op jit(solution)/shard_map/ppermute | solution.py:199

commit v2 on v1

--- a/solution.py
+++ b/solution.py
@@ -12,6 +12,8 @@
 SEND = 5
 BACK = 4
 GROUP = 8
+PAIRS = 3
+TINY = 2.0**-126
 
 GROW = 0.4
 DRAG = 0.25
@@ -21,49 +23,85 @@
 
 VMEM = pl.BlockSpec(memory_space=pltpu.VMEM)
 SMEM = pl.BlockSpec(memory_space=pltpu.SMEM)
-LIMIT = 48 * 2**20
-
-
-def pack_kernel(target, count, velo, radi, cell, sent, slot_of, seen):
+HBM = pl.BlockSpec(memory_space=pltpu.HBM)
+LIMIT = 16 * 2**20
+WHOLE = 64 * 2**20
+
+
+def pack_kernel(
+    target_hbm, count_hbm, velo_hbm, radi_hbm, cell_hbm,
+    sent, slot_of, target, count, velo, radi, cell, seen, ready,
+):
     blocks = radi.shape[0]
     bricks = seen.shape[0]
-    sent[...] = jnp.full(sent.shape, -1.0, jnp.float32)
-    lane = lax.broadcasted_iota(jnp.int32, (1, LANES), 1)
+    pairs = [
+        (target_hbm, target),
+        (count_hbm, count),
+        (velo_hbm, velo),
+        (radi_hbm, radi),
+        (cell_hbm, cell),
+    ]
+    copies = [
+        pltpu.make_async_copy(source, into, ready.at[i]) for i, (source, into) in enumerate(pairs)
+    ]
+    for copy in copies:
+        copy.start()
 
     def clear(i, _):
         seen[i] = 0
         return 0
 
-    lax.fori_loop(0, bricks, clear, 0, unroll=8)
+    lax.fori_loop(0, bricks, clear, 0, unroll=16)
+    sent[...] = jnp.full(sent.shape, -1.0, jnp.float32)
+    lane = lax.broadcasted_iota(jnp.int32, (1, LANES), 1)
+    copies[0].wait()
+
+    def rank(k, _):
+        brick = target[k]
+        earlier = seen[brick]
+        seen[brick] = earlier + 1
+        slot_of[k] = brick * CAP + earlier
+        return 0
+
+    lax.fori_loop(0, blocks, rank, 0, unroll=16)
+    for copy in copies[1:]:
+        copy.wait()
 
     def place(k, _):
-        brick = target[k]
-        rank = seen[brick]
-        seen[brick] = rank + 1
-        slot = brick * CAP + rank
-        slot_of[k] = slot
-        row = slot * SEND
+        row = slot_of[k] * SEND
         for c in range(3):
-            sent[pl.ds(row + c, 1), :] = velo[k, pl.ds(c, 1), :]
+            sent[pl.ds(row + c, 1), :] = velo[c, pl.ds(k, 1), :]
         sent[pl.ds(row + 3, 1), :] = radi[pl.ds(k, 1), :]
         where = cell[pl.ds(k, 1), :].astype(jnp.float32)
         sent[pl.ds(row + 4, 1), :] = jnp.where(lane < count[k], where, -1.0)
         return 0
 
-    lax.fori_loop(0, blocks, place, 0, unroll=4)
-
-
-def unpack_kernel(slot_of, back, velo, radi):
+    lax.fori_loop(0, blocks, place, 0, unroll=8)
+
+
+def unpack_kernel(slot_of, back, velo_hbm, radi_hbm, velo, radi, done):
     blocks = radi.shape[0]
+    half = blocks // 2
 
     def place(k, _):
         row = slot_of[k] * BACK
         for c in range(3):
-            velo[k, pl.ds(c, 1), :] = back[pl.ds(row + c, 1), :]
+            velo[c, pl.ds(k, 1), :] = back[pl.ds(row + c, 1), :]
         radi[pl.ds(k, 1), :] = back[pl.ds(row + 3, 1), :]
         return 0
 
-    lax.fori_loop(0, blocks, place, 0, unroll=4)
+    copies = []
+    for part in range(2):
+        lax.fori_loop(part * half, (part + 1) * half, place, 0, unroll=8)
+        own = pl.ds(part * half, half)
+        copies += [
+            pltpu.make_async_copy(velo.at[:, own], velo_hbm.at[:, own], done.at[2 * part]),
+            pltpu.make_async_copy(radi.at[own], radi_hbm.at[own], done.at[2 * part + 1]),
+        ]
+        copies[-2].start()
+        copies[-1].start()
+    for copy in copies:
+        copy.wait()
 
 
 def diffused(melt, low_x, high_x, low_z, high_z, rate):
@@ -89,8 +127,43 @@
     )
 
 
+def code_of(value):
+    size = jnp.abs(value)
+    exponent = jnp.floor(jnp.log2(jnp.maximum(size, TINY)))
+    mantissa = size * power(-exponent)
+    high = mantissa >= 2.0
+    low = mantissa < 1.0
+    exponent = jnp.where(high, exponent + 1.0, jnp.where(low, exponent - 1.0, exponent))
+    mantissa = jnp.where(high, mantissa * 0.5, jnp.where(low, mantissa * 2.0, mantissa))
+    code = (exponent + 126.0) * 128.0 + mantissa * 128.0
+    code = jnp.where(size < TINY, 0.0, code)
+    return jnp.where(value < 0.0, -code, code).astype(jnp.int32)
+
+
+def value_of(code):
+    size = jnp.abs(code)
+    scale = power((size >> 7).astype(jnp.float32) - 127.0)
+    value = ((size & 127) + 128).astype(jnp.float32) * (1.0 / 128.0) * scale
+    value = jnp.where(size == 0, 0.0, value)
+    return jnp.where(code < 0, -value, value)
+
+
+def power(exponent):
+    return jnp.exp2(exponent).astype(jnp.bfloat16).astype(jnp.float32)
+
+
+def paired(high, low):
+    return code_of(high) * 65536 + (code_of(low) & 65535)
+
+
+def unpaired(found):
+    first = [value_of(word >> 16) for word in found[:PAIRS]]
+    second = [value_of((word << 16) >> 16) for word in found[:PAIRS]]
+    return [*first, found[PAIRS], *second]
+
+
 def steps_kernel(
-    slope, partition, rate, got, melt, low_x, high_x, low_z, high_z, back, melt_mid, acc, table
+    slope, partition, rate, got, melt, low_x, high_x, low_z, high_z, back, melt_mid, acc, table, plain, fed_rows
 ):
     size_y = low_x.shape[1]
     columns = melt.shape[1]
@@ -100,10 +173,26 @@
     row_iota = lax.broadcasted_iota(jnp.int32, (size_x * size_z, LANES), 0)
     y_iota = lax.broadcasted_iota(jnp.int32, (size_y, LANES), 0)
 
-    def one_step(first):
-        acc[...] = jnp.zeros_like(acc)
-
-        def group(g, _):
+    def one_step(first, *sums):
+
+        def look(g):
+            cell = got[pl.ds(g * (SEND * GROUP) + 4, GROUP, stride=SEND), :].astype(jnp.int32)
+            z = cell & (size_z - 1)
+            column = cell >> 7
+            words = [jnp.zeros((GROUP, LANES), jnp.int32)] * PAIRS
+            single = jnp.zeros((GROUP, LANES), jnp.float32)
+            for j in range(columns):
+                here = column == j
+                for c in range(PAIRS):
+                    row = jnp.broadcast_to(table[c, j : j + 1, :], (GROUP, LANES))
+                    words[c] = jnp.where(here, jnp.take_along_axis(row, z, axis=1), words[c])
+                row = jnp.broadcast_to(plain[j : j + 1, :], (GROUP, LANES))
+                single = jnp.where(here, jnp.take_along_axis(row, z, axis=1), single)
+            return (*words, single)
+
+        def work(g, found):
+            probe = unpaired(found)
+
             def rows(field):
                 if first:
                     return got[pl.ds(g * (SEND * GROUP) + field, GROUP, stride=SEND), :]
@@ -113,13 +202,6 @@
             live = cell >= 0
             z = cell & (size_z - 1)
             column = cell >> 7
-            probe = [jnp.zeros((GROUP, LANES), jnp.float32)] * COMPS
-            for j in range(columns):
-                here = column == j
-                for c in range(COMPS):
-                    line = jnp.broadcast_to(table[c, j : j + 1, :], (GROUP, LANES))
-                    picked = jnp.take_along_axis(line, z, axis=1)
-                    probe[c] = jnp.where(here, picked, probe[c])
             velo = [rows(0), rows(1), rows(2)]
             radi = rows(3)
             under = (
@@ -139,35 +221,80 @@
             for c in range(3):
                 back[pl.ds(base + c, GROUP, stride=BACK), :] = jnp.where(live, new_velo[c], velo[c])
             back[pl.ds(base + 3, GROUP, stride=BACK), :] = jnp.where(live, new_radi, radi)
+            for c in range(COMPS):
+                fed_rows[c] = sources[c]
+
+        def spend(g):
+            cell = got[pl.ds(g * (SEND * GROUP) + 4, GROUP, stride=SEND), :].astype(jnp.int32)
+            live = cell >= 0
+            z = cell & (size_z - 1)
+            column = cell >> 7
             y = jnp.where(live, column & (size_y - 1), size_y)
             line = ((column >> 4) * size_z) | z
-            lefts, rights = [], []
-            for b in range(GROUP):
-                mask = y_iota == y[b : b + 1, :]
-                lefts.append(
-                    jnp.concatenate(
-                        [jnp.where(mask, s[b : b + 1, :], 0.0).astype(jnp.bfloat16) for s in sources],
-                        axis=0,
+            for t in range(GROUP // 2):
+                lefts, rights = [], []
+                for b in (2 * t, 2 * t + 1):
+                    mask = y_iota == y[b : b + 1, :]
+                    lefts.append(
+                        jnp.concatenate(
+                            [
+                                jnp.where(mask, fed_rows[c, b : b + 1, :], 0.0).astype(jnp.bfloat16)
+                                for c in range(COMPS)
+                            ],
+                            axis=0,
+                        )
                     )
+                    rights.append(jnp.where(row_iota == line[b : b + 1, :], 1.0, 0.0).astype(jnp.bfloat16))
+                unit, stage = t % 2, t // 2
+                pltpu.matmul_push_rhs(
+                    jnp.concatenate(rights, axis=1),
+                    staging_register=stage,
+                    mxu_index=unit,
+                    transpose=True,
                 )
-                rights.append((row_iota == line[b : b + 1, :]).astype(jnp.bfloat16))
-            left = jnp.concatenate(lefts, axis=1)
-            right = jnp.concatenate(rights, axis=1)
-            acc[...] += lax.dot_general(
-                left, right, (((1,), (1,)), ((), ())), preferred_element_type=jnp.float32
-            )
-            return 0
-
-        lax.fori_loop(0, groups, group, 0)
-
-    table[...] = melt[...].astype(jnp.bfloat16).astype(jnp.float32)
-    one_step(True)
+                pltpu.matmul_acc_lhs(
+                    sums[unit], jnp.concatenate(lefts, axis=1), load_staged_rhs=stage
+                )
+
+        def group(g, probe):
+            spend(g - 1)
+            later = look(jnp.minimum(g + 1, groups - 1))
+            work(g, probe)
+            return later
+
+        work(0, look(0))
+        first_found = group(1, look(1))
+
+        def two(i, found):
+            return group(2 * i + 1, group(2 * i, found))
+
+        lax.fori_loop(1, groups // 2, two, first_found)
+        spend(groups - 1)
+        acc[...] = pltpu.matmul_pop(sums[0]) + pltpu.matmul_pop(sums[1])
+
+    def scoped(first):
+        rows = acc.shape[0]
+        width = acc.shape[1]
+        pl.run_scoped(
+            lambda *sums: one_step(first, *sums),
+            pltpu.ACC(mxu_id=0)((rows, width), jnp.float32),
+            pltpu.ACC(mxu_id=1)((rows, width), jnp.float32),
+        )
+
+    def fill(value):
+        rounded = [value(c).astype(jnp.bfloat16).astype(jnp.float32) for c in range(COMPS)]
+        for c in range(PAIRS):
+            table[c] = paired(rounded[c], rounded[PAIRS + 1 + c])
+        plain[...] = rounded[PAIRS]
+
+    fill(lambda c: melt[c])
+    scoped(True)
     for c in range(COMPS):
         fresh = diffused(melt[c], low_x[c], high_x[c], low_z[c], high_z[c], rate[c])
         fresh = fresh + deposit_of(acc, c, size_x, size_y)
         melt_mid[c] = fresh
-        table[c] = fresh.astype(jnp.bfloat16).astype(jnp.float32)
-    one_step(False)
+    fill(lambda c: melt_mid[c])
+    scoped(False)
 
 
 def finish_kernel(rate, melt, acc, low_x, high_x, low_z, high_z, out):
@@ -178,14 +305,14 @@
         out[c] = fresh + deposit_of(acc, c, size_x, size_y)
 
 
-def kernel_call(kernel, outs, in_specs, out_specs, scratch=()):
+def kernel_call(kernel, outs, in_specs, out_specs, scratch=(), limit=LIMIT):
     return pl.pallas_call(
         kernel,
         out_shape=outs,
         in_specs=in_specs,
         out_specs=out_specs,
         scratch_shapes=list(scratch),
-        compiler_params=pltpu.CompilerParams(vmem_limit_bytes=LIMIT),
+        compiler_params=pltpu.CompilerParams(vmem_limit_bytes=limit),
     )
 
 
@@ -218,7 +345,11 @@
         ),
         [SMEM, SMEM, SMEM] + [VMEM] * 6,
         (VMEM, VMEM, VMEM),
-        [pltpu.VMEM((comps, columns, size_z), jnp.float32)],
+        [
+            pltpu.VMEM((PAIRS, columns, size_z), jnp.int32),
+            pltpu.VMEM((columns, size_z), jnp.float32),
+            pltpu.VMEM((comps, GROUP, LANES), jnp.float32),
+        ],
     )(slope, partition, rate, got, melt, *halo)
 
 
@@ -238,10 +369,19 @@
     sent, slot_of = kernel_call(
         pack_kernel,
         (shape(slots * SEND, LANES), jax.ShapeDtypeStruct((blocks,), jnp.int32)),
-        [SMEM, SMEM, VMEM, VMEM, VMEM],
+        [HBM] * 5,
         (VMEM, SMEM),
-        [pltpu.SMEM((devices,), jnp.int32)],
-    )(target, count, velocity, radius, cell)
+        [
+            pltpu.SMEM((blocks,), jnp.int32),
+            pltpu.SMEM((blocks,), jnp.int32),
+            pltpu.VMEM((3, blocks, LANES), jnp.float32),
+            pltpu.VMEM((blocks, LANES), jnp.float32),
+            pltpu.VMEM((blocks, LANES), jnp.int32),
+            pltpu.SMEM((devices,), jnp.int32),
+            pltpu.SemaphoreType.DMA((5,)),
+        ],
+        limit=WHOLE,
+    )(target, count, jnp.transpose(velocity, (1, 0, 2)), radius, cell)
     got = exchange(sent, devices)
     start = jnp.transpose(melt, (2, 0, 1, 3)).reshape(comps, size_x * size_y, size_z)
     halo = neighbours(start, size_y)
@@ -257,11 +397,16 @@
     melt_out = jnp.transpose(final.reshape(comps, size_x, size_y, size_z), (1, 2, 0, 3))
     velocity_out, radius_out = kernel_call(
         unpack_kernel,
-        (shape(blocks, 3, LANES), shape(blocks, LANES)),
+        (shape(3, blocks, LANES), shape(blocks, LANES)),
         [SMEM, VMEM],
-        (VMEM, VMEM),
+        (HBM, HBM),
+        [
+            pltpu.VMEM((3, blocks, LANES), jnp.float32),
+            pltpu.VMEM((blocks, LANES), jnp.float32),
+            pltpu.SemaphoreType.DMA((4,)),
+        ],
     )(slot_of, returned)
-    return melt_out, velocity_out, radius_out
+    return melt_out, jnp.transpose(velocity_out, (1, 0, 2)), radius_out
 
 
 def solution(mesh):

time: 134 us -> 94.1 us (0.70)
  the two profiles are of different devices: /device:TPU:14 before, /device:TPU:0 now
where the time goes in v2:
time: 94.1 us; the launch traced here: 93.6 us
  Pallas kernels  35.8 us (38%)
  starting transfers between devices  30.7 us (33%)
  waiting for transfers between devices  24.8 us (26%)
  local copies, waits for them, and re-layouts  1.57 us (2%)
    pallas_call x1, Pallas kernels, run_steps(): kernel_call(steps_kernel, (shape(slots * BACK, LANES), shape(comps, colum...  29.3 us
    all_to_all x2, waiting for transfers between devices, exchange(): lax.all_to_all(rows.reshape(each, CAP, LANES), AXES, split_axis=0, concat...  16 us
    all_to_all x2, starting transfers between devices, exchange(): lax.all_to_all(rows.reshape(each, CAP, LANES), AXES, split_axis=0, concat...  15.8 us
    ppermute x8, starting transfers between devices, shift(): lax.ppermute(edge, axis, [(i, i + step) for i in range(n) if 0 <= i + ste...  14.9 us
    ppermute x8, waiting for transfers between devices, shift(): lax.ppermute(edge, axis, [(i, i + step) for i in range(n) if 0 <= i + ste...  8.8 us
    pallas_call x1, Pallas kernels, local(): kernel_call(pack_kernel, (shape(slots * SEND, LANES), jax.ShapeDtypeStruc...  3.84 us
    pallas_call x1, Pallas kernels, local(): kernel_call(unpack_kernel, (shape(3, blocks, LANES), shape(blocks, LANES)...  1.93 us
  transfers between devices with their start and end apart: 10, of which 4 were waited for; matrix products, arithmetic and copies ran while one was open for 2% of the time, Pallas kernels for 1%

profile of v2, /device:TPU:0, one launch (start us, length us, event | category | flops | bytes accessed | tf_op | source)
XLA Modules:
  0.0 93.6 jit_solution(4332391602175301416)
XLA Ops:
  0.6 3.8 %shard_map.112 = (f32[2560,128]{1,0:T(8,128)}, s32[256]{0:T(256)}) custom-call(s32[256]{0:T(256)} %target_hbm.1, s32[256]{0:T(256)} %count_hbm.1, f32[3,256,128]{2,1,0:T(8,128)} %bitcast.24, f32[256,128]{1,0:T(8,128)} %radi_hbm.1, s32[256,128]{1,0:T(8,128)} %cell_hbm.1), custom_call_target="tpu_custom_call" | custom-call | tf_op jit(solution)/shard_map/pallas_call | solution.py:369
  4.5 0.0 copy-start.4
  4.5 0.0 copy-start
  4.5 0.0 copy-start.2
  4.5 0.0 copy-start.3
  4.5 11.1 %all-to-all-start = ((f32[640,4,128]{2,1,0:T(4,128)}), f32[640,4,128]{2,1,0:T(4,128)S(1)}, u32[]{:S(2)}, u32[]{:S(2)}) async-start(f32[640,4,128]{2,1,0:T(4,128)} %bitcast.23), calls=%async_computation | async-start | bytes 2621440 | tf_op jit(solution)/shard_map/all_to_all | solution.py:358
  15.7 1.3 %collective-permute-start = (f32[7,16,128]{2,1,0:T(8,128)S(1)}, f32[7,16,128]{2,1,0:T(8,128)S(1)}, u32[]{:S(2)}, u32[]{:S(2)}) collective-permute-start(f32[7,16,128]{2,1,0:T(8,128)S(1)} %get-tuple-element.24), channel_id=1, source_target_pairs={{0,1},{1,2},{2,3},{3,4},{4,5},{5,6},{6,7},{7,8},{8,9},{9,10},{10,1... | collective-permute-start | bytes 172040 | tf_op jit(solution)/shard_map/ppermute | solution.py:326
  17.1 1.3 %collective-permute-start.1 = (f32[7,16,128]{2,1,0:T(8,128)S(1)}, f32[7,16,128]{2,1,0:T(8,128)S(1)}, u32[]{:S(2)}, u32[]{:S(2)}) collective-permute-start(f32[7,16,128]{2,1,0:T(8,128)S(1)} %get-tuple-element.23), channel_id=1, source_target_pairs={{1,0},{2,1},{3,2},{4,3},{5,4},{6,5},{7,6},{8,7},{9,8},{10,9},{11,1... | collective-permute-start | bytes 172040 | tf_op jit(solution)/shard_map/ppermute | solution.py:326
  18.4 0.2 slice_reduce_fusion
  18.6 3.6 %collective-permute-start.2 = (f32[7,32]{1,0:T(8,128)S(1)}, f32[7,32]{1,0:T(8,128)S(1)}, u32[]{:S(2)}, u32[]{:S(2)}) collective-permute-start(f32[7,32]{1,0:T(8,128)S(1)} %get-tuple-element.20), channel_id=1, source_target_pairs={{0,32},{32,64},{64,96},{1,33},{33,65},{65,97},{2,34},{34,66},{66,9... | collective-permute-start | bytes 2696 | tf_op jit(solution)/shard_map/ppermute | solution.py:326
  22.2 1.3 %collective-permute-start.3 = (f32[7,32]{1,0:T(8,128)S(1)}, f32[7,32]{1,0:T(8,128)S(1)}, u32[]{:S(2)}, u32[]{:S(2)}) collective-permute-start(f32[7,32]{1,0:T(8,128)S(1)} %get-tuple-element.19), channel_id=1, source_target_pairs={{32,0},{64,32},{96,64},{33,1},{65,33},{97,65},{34,2},{66,34},{98,6... | collective-permute-start | bytes 2696 | tf_op jit(solution)/shard_map/ppermute | solution.py:326
  23.5 0.0 collective-permute-done.2
  23.5 0.1 copy.33.low_z
  23.6 4.5 %collective-permute-done.3 = f32[7,32]{1,0:T(8,128)S(1)} collective-permute-done((f32[7,32]{1,0:T(8,128)S(1)}, f32[7,32]{1,0:T(8,128)S(1)}, u32[]{:S(2)}, u32[]{:S(2)}) %collective-permute-start.3) | collective-permute-done | bytes 928 | tf_op jit(solution)/shard_map/ppermute | solution.py:326
  28.1 0.1 copy.34.high_z
  28.3 9.9 %all-to-all-done = f32[640,4,128]{2,1,0:T(4,128)S(1)} async-done(((f32[640,4,128]{2,1,0:T(4,128)}), f32[640,4,128]{2,1,0:T(4,128)S(1)}, u32[]{:S(2)}, u32[]{:S(2)}) %all-to-all-start) | async-done | bytes 1310752 | tf_op jit(solution)/shard_map/all_to_all | solution.py:358
  38.1 29.3 %shard_map.113 = (f32[2048,128]{1,0:T(8,128)}, f32[7,32,128]{2,1,0:T(8,128)S(1)}, f32[112,256]{1,0:T(8,128)S(1)}) custom-call(f32[3]{0:T(128)S(1)} %copy-done.2, f32[3]{0:T(128)S(1)} %copy-done.3, f32[7]{0:T(128)S(1)} %copy-done, f32[2560,128]{1,0:T(8,128)S(1)} %bitcast.17, f32[7,32,128]{2,1,0:T(8,128)S(1)} %bitcast.21, ...), custom_call_target="tpu_custom_call" | custom-call | tf_op jit(solution)/shard_map/pallas_call | solution.py:339
  67.4 4.6 %all-to-all-start.1 = ((f32[512,4,128]{2,1,0:T(4,128)}), f32[512,4,128]{2,1,0:T(4,128)S(1)}, u32[]{:S(2)}, u32[]{:S(2)}) async-start(f32[512,4,128]{2,1,0:T(4,128)} %bitcast.12), calls=%async_computation.1 | async-start | bytes 2097152 | tf_op jit(solution)/shard_map/all_to_all | solution.py:358
  72.0 0.0 copy-start.1
  72.1 1.3 %collective-permute-start.4 = (f32[7,16,128]{2,1,0:T(8,128)S(1)}, f32[7,16,128]{2,1,0:T(8,128)S(1)}, u32[]{:S(2)}, u32[]{:S(2)}) collective-permute-start(f32[7,16,128]{2,1,0:T(8,128)S(1)} %get-tuple-element.22), channel_id=1, source_target_pairs={{0,1},{1,2},{2,3},{3,4},{4,5},{5,6},{6,7},{7,8},{8,9},{9,10},{10,1... | collective-permute-start | bytes 172040 | tf_op jit(solution)/shard_map/ppermute | solution.py:326
  73.4 1.3 %collective-permute-start.5 = (f32[7,16,128]{2,1,0:T(8,128)S(1)}, f32[7,16,128]{2,1,0:T(8,128)S(1)}, u32[]{:S(2)}, u32[]{:S(2)}) collective-permute-start(f32[7,16,128]{2,1,0:T(8,128)S(1)} %get-tuple-element.21), channel_id=1, source_target_pairs={{1,0},{2,1},{3,2},{4,3},{5,4},{6,5},{7,6},{8,7},{9,8},{10,9},{11,1... | collective-permute-start | bytes 172040 | tf_op jit(solution)/shard_map/ppermute | solution.py:326
  74.7 0.2 slice_reduce_fusion.2
  74.8 3.5 %collective-permute-start.6 = (f32[7,32]{1,0:T(8,128)S(1)}, f32[7,32]{1,0:T(8,128)S(1)}, u32[]{:S(2)}, u32[]{:S(2)}) collective-permute-start(f32[7,32]{1,0:T(8,128)S(1)} %get-tuple-element.18), channel_id=1, source_target_pairs={{0,32},{32,64},{64,96},{1,33},{33,65},{65,97},{2,34},{34,66},{66,9... | collective-permute-start | bytes 2696 | tf_op jit(solution)/shard_map/ppermute | solution.py:326
  78.4 1.3 %collective-permute-start.7 = (f32[7,32]{1,0:T(8,128)S(1)}, f32[7,32]{1,0:T(8,128)S(1)}, u32[]{:S(2)}, u32[]{:S(2)}) collective-permute-start(f32[7,32]{1,0:T(8,128)S(1)} %get-tuple-element.17), channel_id=1, source_target_pairs={{32,0},{64,32},{96,64},{33,1},{65,33},{97,65},{34,2},{66,34},{98,6... | collective-permute-start | bytes 2696 | tf_op jit(solution)/shard_map/ppermute | solution.py:326
  79.7 0.0 collective-permute-done.6
  79.7 0.1 copy.35.low_z
  79.8 4.2 %collective-permute-done.7 = f32[7,32]{1,0:T(8,128)S(1)} collective-permute-done((f32[7,32]{1,0:T(8,128)S(1)}, f32[7,32]{1,0:T(8,128)S(1)}, u32[]{:S(2)}, u32[]{:S(2)}) %collective-permute-start.7) | collective-permute-done | bytes 928 | tf_op jit(solution)/shard_map/ppermute | solution.py:326
  84.1 0.1 copy.36.high_z
  84.2 0.7 shard_map.114
  84.9 0.7 copy.39
  85.6 6.1 %all-to-all-done.1 = f32[512,4,128]{2,1,0:T(4,128)S(1)} async-done(((f32[512,4,128]{2,1,0:T(4,128)}), f32[512,4,128]{2,1,0:T(4,128)S(1)}, u32[]{:S(2)}, u32[]{:S(2)}) %all-to-all-start.1) | async-done | bytes 1048608 | tf_op jit(solution)/shard_map/all_to_all | solution.py:358
  91.7 1.9 %shard_map.115 = (f32[3,256,128]{2,1,0:T(8,128)}, f32[256,128]{1,0:T(8,128)}) custom-call(s32[256]{0:T(256)S(1)} %copy-done.1, f32[2048,128]{1,0:T(8,128)S(1)} %bitcast.18), custom_call_target="tpu_custom_call" | custom-call | tf_op jit(solution)/shard_map/pallas_call | solution.py:398
  (12 shorter events, 0.1 us)
Async XLA Ops:
  4.5 11.2 %copy-start.4 = (f32[2,16,7,128]{3,1,2,0:T(8,128)S(1)}, f32[2,16,7,128]{3,1,2,0:T(8,128)}, u32[]{:S(2)}) copy-start(f32[2,16,7,128]{3,1,2,0:T(8,128)} %param.9) | copy-start | bytes 344068
  4.5 33.6 %copy-start = (f32[7]{0:T(128)S(1)}, f32[7]{0:T(128)}, u32[]{:S(2)}) copy-start(f32[7]{0:T(128)} %rate.3) | copy-start | bytes 88
  4.5 33.6 %copy-start.2 = (f32[3]{0:T(128)S(1)}, f32[3]{0:T(128)}, u32[]{:S(2)}) copy-start(f32[3]{0:T(128)} %slope.1) | copy-start | bytes 40
  4.5 33.6 %copy-start.3 = (f32[3]{0:T(128)S(1)}, f32[3]{0:T(128)}, u32[]{:S(2)}) copy-start(f32[3]{0:T(128)} %partition.1) | copy-start | bytes 40
  4.5 33.6 %all-to-all-start = ((f32[640,4,128]{2,1,0:T(4,128)}), f32[640,4,128]{2,1,0:T(4,128)S(1)}, u32[]{:S(2)}, u32[]{:S(2)}) async-start(f32[640,4,128]{2,1,0:T(4,128)} %bitcast.23), calls=%async_computation | async-start | bytes 2621440 | tf_op jit(solution)/shard_map/all_to_all | solution.py:358
  15.7 12.5 %collective-permute-start = (f32[7,16,128]{2,1,0:T(8,128)S(1)}, f32[7,16,128]{2,1,0:T(8,128)S(1)}, u32[]{:S(2)}, u32[]{:S(2)}) collective-permute-start(f32[7,16,128]{2,1,0:T(8,128)S(1)} %get-tuple-element.24), channel_id=1, source_target_pairs={{0,1},{1,2},{2,3},{3,4},{4,5},{5,6},{6,7},{7,8},{8,9},{9,10},{10,1... | collective-permute-start | bytes 172040 | tf_op jit(solution)/shard_map/ppermute | solution.py:326
  17.1 11.2 %collective-permute-start.1 = (f32[7,16,128]{2,1,0:T(8,128)S(1)}, f32[7,16,128]{2,1,0:T(8,128)S(1)}, u32[]{:S(2)}, u32[]{:S(2)}) collective-permute-start(f32[7,16,128]{2,1,0:T(8,128)S(1)} %get-tuple-element.23), channel_id=1, source_target_pairs={{1,0},{2,1},{3,2},{4,3},{5,4},{6,5},{7,6},{8,7},{9,8},{10,9},{11,1... | collective-permute-start | bytes 172040 | tf_op jit(solution)/shard_map/ppermute | solution.py:326
  18.6 4.9 %collective-permute-start.2 = (f32[7,32]{1,0:T(8,128)S(1)}, f32[7,32]{1,0:T(8,128)S(1)}, u32[]{:S(2)}, u32[]{:S(2)}) collective-permute-start(f32[7,32]{1,0:T(8,128)S(1)} %get-tuple-element.20), channel_id=1, source_target_pairs={{0,32},{32,64},{64,96},{1,33},{33,65},{65,97},{2,34},{34,66},{66,9... | collective-permute-start | bytes 2696 | tf_op jit(solution)/shard_map/ppermute | solution.py:326
  22.2 6.0 %collective-permute-start.3 = (f32[7,32]{1,0:T(8,128)S(1)}, f32[7,32]{1,0:T(8,128)S(1)}, u32[]{:S(2)}, u32[]{:S(2)}) collective-permute-start(f32[7,32]{1,0:T(8,128)S(1)} %get-tuple-element.19), channel_id=1, source_target_pairs={{32,0},{64,32},{96,64},{33,1},{65,33},{97,65},{34,2},{66,34},{98,6... | collective-permute-start | bytes 2696 | tf_op jit(solution)/shard_map/ppermute | solution.py:326
  67.4 24.3 %all-to-all-start.1 = ((f32[512,4,128]{2,1,0:T(4,128)}), f32[512,4,128]{2,1,0:T(4,128)S(1)}, u32[]{:S(2)}, u32[]{:S(2)}) async-start(f32[512,4,128]{2,1,0:T(4,128)} %bitcast.12), calls=%async_computation.1 | async-start | bytes 2097152 | tf_op jit(solution)/shard_map/all_to_all | solution.py:358
  72.0 19.7 %copy-start.1 = (s32[256]{0:T(256)S(1)}, s32[256]{0:T(256)}, u32[]{:S(2)}) copy-start(s32[256]{0:T(256)} %get-tuple-element.13.slot_of) | copy-start | bytes 3076
  72.1 12.1 %collective-permute-start.4 = (f32[7,16,128]{2,1,0:T(8,128)S(1)}, f32[7,16,128]{2,1,0:T(8,128)S(1)}, u32[]{:S(2)}, u32[]{:S(2)}) collective-permute-start(f32[7,16,128]{2,1,0:T(8,128)S(1)} %get-tuple-element.22), channel_id=1, source_target_pairs={{0,1},{1,2},{2,3},{3,4},{4,5},{5,6},{6,7},{7,8},{8,9},{9,10},{10,1... | collective-permute-start | bytes 172040 | tf_op jit(solution)/shard_map/ppermute | solution.py:326
  73.4 10.8 %collective-permute-start.5 = (f32[7,16,128]{2,1,0:T(8,128)S(1)}, f32[7,16,128]{2,1,0:T(8,128)S(1)}, u32[]{:S(2)}, u32[]{:S(2)}) collective-permute-start(f32[7,16,128]{2,1,0:T(8,128)S(1)} %get-tuple-element.21), channel_id=1, source_target_pairs={{1,0},{2,1},{3,2},{4,3},{5,4},{6,5},{7,6},{8,7},{9,8},{10,9},{11,1... | collective-permute-start | bytes 172040 | tf_op jit(solution)/shard_map/ppermute | solution.py:326
  74.8 4.9 %collective-permute-start.6 = (f32[7,32]{1,0:T(8,128)S(1)}, f32[7,32]{1,0:T(8,128)S(1)}, u32[]{:S(2)}, u32[]{:S(2)}) collective-permute-start(f32[7,32]{1,0:T(8,128)S(1)} %get-tuple-element.18), channel_id=1, source_target_pairs={{0,32},{32,64},{64,96},{1,33},{33,65},{65,97},{2,34},{34,66},{66,9... | collective-permute-start | bytes 2696 | tf_op jit(solution)/shard_map/ppermute | solution.py:326
  78.4 5.7 %collective-permute-start.7 = (f32[7,32]{1,0:T(8,128)S(1)}, f32[7,32]{1,0:T(8,128)S(1)}, u32[]{:S(2)}, u32[]{:S(2)}) collective-permute-start(f32[7,32]{1,0:T(8,128)S(1)} %get-tuple-element.17), channel_id=1, source_target_pairs={{32,0},{64,32},{96,64},{33,1},{65,33},{97,65},{34,2},{66,34},{98,6... | collective-permute-start | bytes 2696 | tf_op jit(solution)/shard_map/ppermute | solution.py:326

commit v3 on v2

--- a/solution.py
+++ b/solution.py
@@ -1,3 +1,5 @@
+import functools
+
 import jax
 import jax.numpy as jnp
 from jax import lax
@@ -162,139 +164,240 @@
     return [*first, found[PAIRS], *second]
 
 
-def steps_kernel(
-    slope, partition, rate, got, melt, low_x, high_x, low_z, high_z, back, melt_mid, acc, table, plain, fed_rows
-):
-    size_y = low_x.shape[1]
-    columns = melt.shape[1]
-    size_z = melt.shape[2]
-    size_x = columns // size_y
-    groups = got.shape[0] // (SEND * GROUP)
+def spend_group(cell, fed_rows, dims, sums):
+    size_x, size_y, size_z = dims
     row_iota = lax.broadcasted_iota(jnp.int32, (size_x * size_z, LANES), 0)
     y_iota = lax.broadcasted_iota(jnp.int32, (size_y, LANES), 0)
-
-    def one_step(first, *sums):
-
-        def look(g):
-            cell = got[pl.ds(g * (SEND * GROUP) + 4, GROUP, stride=SEND), :].astype(jnp.int32)
-            z = cell & (size_z - 1)
-            column = cell >> 7
-            words = [jnp.zeros((GROUP, LANES), jnp.int32)] * PAIRS
-            single = jnp.zeros((GROUP, LANES), jnp.float32)
-            for j in range(columns):
-                here = column == j
-                for c in range(PAIRS):
-                    row = jnp.broadcast_to(table[c, j : j + 1, :], (GROUP, LANES))
-                    words[c] = jnp.where(here, jnp.take_along_axis(row, z, axis=1), words[c])
-                row = jnp.broadcast_to(plain[j : j + 1, :], (GROUP, LANES))
-                single = jnp.where(here, jnp.take_along_axis(row, z, axis=1), single)
-            return (*words, single)
-
-        def work(g, found):
-            probe = unpaired(found)
-
-            def rows(field):
-                if first:
-                    return got[pl.ds(g * (SEND * GROUP) + field, GROUP, stride=SEND), :]
-                return back[pl.ds(g * (BACK * GROUP) + field, GROUP, stride=BACK), :]
-
-            cell = got[pl.ds(g * (SEND * GROUP) + 4, GROUP, stride=SEND), :].astype(jnp.int32)
-            live = cell >= 0
-            z = cell & (size_z - 1)
-            column = cell >> 7
-            velo = [rows(0), rows(1), rows(2)]
-            radi = rows(3)
-            under = (
-                probe[4] * slope[0] + probe[5] * slope[1] + probe[6] * slope[2]
-            ) - probe[3]
-            growth = GROW * (jnp.maximum(under, 0.0) + jnp.log1p(jnp.exp(-jnp.abs(under))))
-            beta = DRAG / (radi * radi)
-            push = -(MOMENT * radi * radi * radi * beta)
-            slip = [probe[c] - velo[c] for c in range(3)]
-            fed = growth * radi
-            sources = [push * slip[c] for c in range(3)] + [LATENT * growth * radi]
-            sources += [(1.0 - partition[s]) * probe[4 + s] * fed for s in range(3)]
-            new_velo = [velo[c] + beta * slip[c] for c in range(3)]
-            new_velo[2] = new_velo[2] - SETTLE * radi
-            new_radi = radi + growth / radi
-            base = g * (BACK * GROUP)
-            for c in range(3):
-                back[pl.ds(base + c, GROUP, stride=BACK), :] = jnp.where(live, new_velo[c], velo[c])
-            back[pl.ds(base + 3, GROUP, stride=BACK), :] = jnp.where(live, new_radi, radi)
+    z = cell & (size_z - 1)
+    column = cell >> 7
+    y = jnp.where(cell >= 0, column & (size_y - 1), size_y)
+    line = ((column >> 4) * size_z) | z
+    for t in range(GROUP // 2):
+        lefts, rights = [], []
+        for b in (2 * t, 2 * t + 1):
+            mask = y_iota == y[b : b + 1, :]
+            lefts.append(
+                jnp.concatenate(
+                    [
+                        jnp.where(mask, fed_rows[c, b : b + 1, :], 0.0).astype(jnp.bfloat16)
+                        for c in range(COMPS)
+                    ],
+                    axis=0,
+                )
+            )
+            rights.append(
+                jnp.where(row_iota == line[b : b + 1, :], 1.0, 0.0).astype(jnp.bfloat16)
+            )
+        unit, stage = t % 2, t // 2
+        pltpu.matmul_push_rhs(
+            jnp.concatenate(rights, axis=1),
+            staging_register=stage,
+            mxu_index=unit,
+            transpose=True,
+        )
+        pltpu.matmul_acc_lhs(
+            sums[unit], jnp.concatenate(lefts, axis=1), load_staged_rhs=stage
+        )
+
+
+def matrix_probe(cell, lines, dims, sums):
+    size_x, size_y, size_z = dims
+    row_iota = lax.broadcasted_iota(jnp.int32, (size_x * size_z, LANES), 0)
+    y_iota = lax.broadcasted_iota(jnp.int32, (size_y, LANES), 0)
+    column = cell >> 7
+    y = jnp.where(cell >= 0, column & (size_y - 1), size_y)
+    line = ((column >> 4) * size_z) | (cell & (size_z - 1))
+    found = [[] for _ in range(COMPS)]
+    for t in range(GROUP // 2):
+        pair = (2 * t, 2 * t + 1)
+        unit, stage = t % 2, t // 2
+        pltpu.matmul_push_rhs(
+            jnp.concatenate(
+                [
+                    jnp.where(row_iota == line[b : b + 1, :], 1.0, 0.0).astype(jnp.bfloat16)
+                    for b in pair
+                ],
+                axis=1,
+            ),
+            staging_register=stage,
+            mxu_index=unit,
+        )
+        pltpu.matmul_acc_lhs(sums[2 * stage + unit], lines[...], load_staged_rhs=stage)
+        lifted = pltpu.matmul_pop(sums[2 * stage + unit])
+        for i, b in enumerate(pair):
+            mask = y_iota == y[b : b + 1, :]
             for c in range(COMPS):
-                fed_rows[c] = sources[c]
-
-        def spend(g):
-            cell = got[pl.ds(g * (SEND * GROUP) + 4, GROUP, stride=SEND), :].astype(jnp.int32)
-            live = cell >= 0
-            z = cell & (size_z - 1)
-            column = cell >> 7
-            y = jnp.where(live, column & (size_y - 1), size_y)
-            line = ((column >> 4) * size_z) | z
-            for t in range(GROUP // 2):
-                lefts, rights = [], []
-                for b in (2 * t, 2 * t + 1):
-                    mask = y_iota == y[b : b + 1, :]
-                    lefts.append(
-                        jnp.concatenate(
-                            [
-                                jnp.where(mask, fed_rows[c, b : b + 1, :], 0.0).astype(jnp.bfloat16)
-                                for c in range(COMPS)
-                            ],
-                            axis=0,
-                        )
-                    )
-                    rights.append(jnp.where(row_iota == line[b : b + 1, :], 1.0, 0.0).astype(jnp.bfloat16))
-                unit, stage = t % 2, t // 2
-                pltpu.matmul_push_rhs(
-                    jnp.concatenate(rights, axis=1),
-                    staging_register=stage,
-                    mxu_index=unit,
-                    transpose=True,
-                )
-                pltpu.matmul_acc_lhs(
-                    sums[unit], jnp.concatenate(lefts, axis=1), load_staged_rhs=stage
-                )
-
-        def group(g, probe):
+                part = lifted[c * size_y : (c + 1) * size_y, i * LANES : (i + 1) * LANES]
+                found[c].append(jnp.sum(jnp.where(mask, part, 0.0), axis=0, keepdims=True))
+    return [jnp.concatenate(rows, axis=0) for rows in found]
+
+
+def coupling_step(slope, partition, dims, refs, load_cell, load, store, span, sums, kept=None):
+    size_x, size_y, size_z = dims
+    table, plain, lines, fed_rows = refs
+    columns = size_x * size_y
+
+    def look(g):
+        cell = load_cell(g)
+        z = cell & (size_z - 1)
+        column = cell >> 7
+        words = [jnp.zeros((GROUP, LANES), jnp.int32)] * PAIRS
+        single = jnp.zeros((GROUP, LANES), jnp.float32)
+        for j in range(columns):
+            here = column == j
+            for c in range(PAIRS):
+                row = jnp.broadcast_to(table[c, j : j + 1, :], (GROUP, LANES))
+                words[c] = jnp.where(here, jnp.take_along_axis(row, z, axis=1), words[c])
+            row = jnp.broadcast_to(plain[j : j + 1, :], (GROUP, LANES))
+            single = jnp.where(here, jnp.take_along_axis(row, z, axis=1), single)
+        return (*words, single)
+
+    def work(g, probe, into):
+        live = load_cell(g) >= 0
+        velo = [load(g, 0), load(g, 1), load(g, 2)]
+        radi = load(g, 3)
+        under = (
+            probe[4] * slope[0] + probe[5] * slope[1] + probe[6] * slope[2]
+        ) - probe[3]
+        growth = GROW * (jnp.maximum(under, 0.0) + jnp.log1p(jnp.exp(-jnp.abs(under))))
+        beta = DRAG / (radi * radi)
+        push = -(MOMENT * radi * radi * radi * beta)
+        slip = [probe[c] - velo[c] for c in range(3)]
+        fed = growth * radi
+        sources = [push * slip[c] for c in range(3)] + [LATENT * growth * radi]
+        sources += [(1.0 - partition[s]) * probe[4 + s] * fed for s in range(3)]
+        new_velo = [velo[c] + beta * slip[c] for c in range(3)]
+        new_velo[2] = new_velo[2] - SETTLE * radi
+        new_radi = radi + growth / radi
+        for c in range(3):
+            store(g, c, jnp.where(live, new_velo[c], velo[c]))
+        store(g, 3, jnp.where(live, new_radi, radi))
+        for c in range(COMPS):
+            into[c] = sources[c]
+
+    def spend(g):
+        spend_group(load_cell(g), fed_rows, dims, sums)
+
+    first, stop = span
+    last = stop - 1
+
+    if kept is None:
+
+        def group(g, found):
             spend(g - 1)
-            later = look(jnp.minimum(g + 1, groups - 1))
-            work(g, probe)
+            later = look(jnp.minimum(g + 1, last))
+            work(g, unpaired(found), fed_rows)
             return later
-
-        work(0, look(0))
-        first_found = group(1, look(1))
 
         def two(i, found):
             return group(2 * i + 1, group(2 * i, found))
 
-        lax.fori_loop(1, groups // 2, two, first_found)
-        spend(groups - 1)
-        acc[...] = pltpu.matmul_pop(sums[0]) + pltpu.matmul_pop(sums[1])
-
-    def scoped(first):
-        rows = acc.shape[0]
-        width = acc.shape[1]
-        pl.run_scoped(
-            lambda *sums: one_step(first, *sums),
-            pltpu.ACC(mxu_id=0)((rows, width), jnp.float32),
-            pltpu.ACC(mxu_id=1)((rows, width), jnp.float32),
+        work(first, unpaired(look(first)), fed_rows)
+        lax.fori_loop(first // 2 + 1, stop // 2, two, group(first + 1, look(first + 1)))
+        spend(last)
+    else:
+
+        def pair(g):
+            return look(g), tuple(matrix_probe(load_cell(g + 1), lines, dims, sums))
+
+        def both(i, found):
+            g = 2 * i
+            later = pair(jnp.minimum(g + 2, last - 1))
+            work(g, unpaired(found[0]), kept.at[g - first])
+            work(g + 1, found[1], kept.at[g + 1 - first])
+            return later
+
+        def four(i, found):
+            return both(2 * i + 1, both(2 * i, found))
+
+        lax.fori_loop(first // 4, stop // 4, four, pair(first))
+
+
+def deposit_scope(rows, width, body):
+    pl.run_scoped(
+        lambda *sums: body(sums),
+        pltpu.ACC(mxu_id=0)((rows, width), jnp.float32),
+        pltpu.ACC(mxu_id=1)((rows, width), jnp.float32),
+    )
+
+
+def fill_lines(lines, value, size_y):
+    for c in range(COMPS):
+        part = value(c).astype(jnp.bfloat16)
+        lines[c * size_y : (c + 1) * size_y, :] = jnp.concatenate(
+            [part[x : x + size_y] for x in range(0, part.shape[0], size_y)], axis=1
         )
 
-    def fill(value):
-        rounded = [value(c).astype(jnp.bfloat16).astype(jnp.float32) for c in range(COMPS)]
-        for c in range(PAIRS):
-            table[c] = paired(rounded[c], rounded[PAIRS + 1 + c])
-        plain[...] = rounded[PAIRS]
-
-    fill(lambda c: melt[c])
-    scoped(True)
+
+def fill_table(table, plain, value):
+    rounded = [value(c).astype(jnp.bfloat16).astype(jnp.float32) for c in range(COMPS)]
+    for c in range(PAIRS):
+        table[c] = paired(rounded[c], rounded[PAIRS + 1 + c])
+    plain[...] = rounded[PAIRS]
+
+
+def got_cell(got, g):
+    return got[pl.ds(g * (SEND * GROUP) + 4, GROUP, stride=SEND), :].astype(jnp.int32)
+
+
+def steps_kernel(
+    slope, partition, rate, got, melt, low_x, high_x, low_z, high_z,
+    back, melt_mid, acc, kept, *refs,
+):
+    table, plain, lines, _ = refs
+    size_y = low_x.shape[1]
+    size_x = melt.shape[1] // size_y
+    dims = (size_x, size_y, melt.shape[2])
+    groups = got.shape[0] // (SEND * GROUP)
+
+    def stay(g, f):
+        return pl.ds(g * (BACK * GROUP) + f, GROUP, stride=BACK)
+
+    def store(g, f, value):
+        back[stay(g, f), :] = value
+
+    def step(load, share, kept):
+        def body(sums):
+            coupling_step(
+                slope, partition, dims, refs, lambda g: got_cell(got, g), load, store,
+                (share, groups), sums,
+            )
+            acc[...] = pltpu.matmul_pop(sums[0]) + pltpu.matmul_pop(sums[1])
+
+        def keep(*sums):
+            coupling_step(
+                slope, partition, dims, refs, lambda g: got_cell(got, g), load, store,
+                (0, share), sums, kept,
+            )
+
+        if share:
+            pl.run_scoped(
+                keep, *[pltpu.ACC(mxu_id=i % 2)(acc.shape, jnp.float32) for i in range(4)]
+            )
+        deposit_scope(*acc.shape, body)
+
+    fill_table(table, plain, lambda c: melt[c])
+    step(lambda g, f: got[pl.ds(g * (SEND * GROUP) + f, GROUP, stride=SEND), :], 0, None)
     for c in range(COMPS):
         fresh = diffused(melt[c], low_x[c], high_x[c], low_z[c], high_z[c], rate[c])
-        fresh = fresh + deposit_of(acc, c, size_x, size_y)
-        melt_mid[c] = fresh
-    fill(lambda c: melt_mid[c])
-    scoped(False)
+        melt_mid[c] = fresh + deposit_of(acc, c, size_x, size_y)
+    fill_table(table, plain, lambda c: melt_mid[c])
+    fill_lines(lines, lambda c: melt_mid[c], size_y)
+    step(lambda g, f: back[stay(g, f), :], kept.shape[0], kept)
+
+
+def kept_kernel(dims, got, kept, before, acc):
+
+    def body(sums):
+        def two(i, _):
+            for g in (2 * i, 2 * i + 1):
+                spend_group(got_cell(got, g), kept.at[g], dims, sums)
+            return 0
+
+        lax.fori_loop(0, kept.shape[0] // 2, two, 0)
+        acc[...] = before[...] + (pltpu.matmul_pop(sums[0]) + pltpu.matmul_pop(sums[1]))
+
+    deposit_scope(*acc.shape, body)
 
 
 def finish_kernel(rate, melt, acc, low_x, high_x, low_z, high_z, out):
@@ -305,7 +408,7 @@
         out[c] = fresh + deposit_of(acc, c, size_x, size_y)
 
 
-def kernel_call(kernel, outs, in_specs, out_specs, scratch=(), limit=LIMIT):
+def kernel_call(kernel, outs, in_specs, out_specs, scratch=(), limit=LIMIT, cost=None):
     return pl.pallas_call(
         kernel,
         out_shape=outs,
@@ -313,6 +416,9 @@
         out_specs=out_specs,
         scratch_shapes=list(scratch),
         compiler_params=pltpu.CompilerParams(vmem_limit_bytes=limit),
+        cost_estimate=None
+        if cost is None
+        else pl.CostEstimate(flops=cost, bytes_accessed=2**20, transcendentals=0),
     )
 
 
@@ -336,21 +442,34 @@
     comps, columns, size_z = melt.shape
     size_x = columns // size_y
     slots = got.shape[0] // SEND
+    sums = shape(comps * size_y, size_x * size_z)
     return kernel_call(
         steps_kernel,
         (
             shape(slots * BACK, LANES),
             shape(comps, columns, size_z),
-            shape(comps * size_y, size_x * size_z),
+            sums,
+            shape(slots // GROUP * 3 // 4, comps, GROUP, LANES),
         ),
         [SMEM, SMEM, SMEM] + [VMEM] * 6,
-        (VMEM, VMEM, VMEM),
+        (VMEM, VMEM, VMEM, VMEM),
         [
             pltpu.VMEM((PAIRS, columns, size_z), jnp.int32),
             pltpu.VMEM((columns, size_z), jnp.float32),
+            pltpu.VMEM((comps * size_y, size_x * size_z), jnp.bfloat16),
             pltpu.VMEM((comps, GROUP, LANES), jnp.float32),
         ],
     )(slope, partition, rate, got, melt, *halo)
+
+
+def run_kept(got, kept, before, dims):
+    return kernel_call(
+        functools.partial(kept_kernel, dims),
+        shape(*before.shape),
+        [VMEM] * 3,
+        VMEM,
+        cost=8_000_000_000,
+    )(got, kept, before)
 
 
 def exchange(rows, devices):
@@ -385,9 +504,10 @@
     got = exchange(sent, devices)
     start = jnp.transpose(melt, (2, 0, 1, 3)).reshape(comps, size_x * size_y, size_z)
     halo = neighbours(start, size_y)
-    back, middle, acc = run_steps(got, start, halo, slope, partition, rate, size_y)
+    back, middle, acc, kept = run_steps(got, start, halo, slope, partition, rate, size_y)
     returned = exchange(back, devices)
     halo = neighbours(middle, size_y)
+    acc = run_kept(got, kept, acc, (size_x, size_y, size_z))
     final = kernel_call(
         finish_kernel,
         shape(comps, size_x * size_y, size_z),

time: 94.1 us -> 95.5 us (1.015)
  the two profiles are of different devices: /device:TPU:0 before, /device:TPU:14 now
where the time goes in v3:
time: 95.5 us; the launch traced here: 94.8 us
  starting transfers between devices  44.1 us (46%)
  Pallas kernels  40.5 us (42%)
  waiting for transfers between devices  5.43 us (6%)
  local copies, waits for them, and re-layouts  4.01 us (4%)
    ppermute x8, starting transfers between devices, shift(): lax.ppermute(edge, axis, [(i, i + step) for i in range(n) if 0 <= i + ste...  25.8 us
    pallas_call x1, Pallas kernels, run_steps(): kernel_call(steps_kernel, (shape(slots * BACK, LANES), shape(comps, colum...  25.2 us
    all_to_all x2, starting transfers between devices, exchange(): lax.all_to_all(rows.reshape(each, CAP, LANES), AXES, split_axis=0, concat...  18.3 us
    pallas_call x1, Pallas kernels, run_kept(): kernel_call(functools.partial(kept_kernel, dims), shape(*before.shape), [...  8.8 us
    ppermute x8, waiting for transfers between devices, shift(): lax.ppermute(edge, axis, [(i, i + step) for i in range(n) if 0 <= i + ste...  5.43 us
    pallas_call x1, Pallas kernels, local(): kernel_call(pack_kernel, (shape(slots * SEND, LANES), jax.ShapeDtypeStruc...  3.83 us
    unnamed x15, local copies, waits for them, and re-layouts  2.48 us
    pallas_call x1, Pallas kernels, local(): kernel_call(unpack_kernel, (shape(3, blocks, LANES), shape(blocks, LANES)...  1.93 us
  transfers between devices with their start and end apart: 10, of which 3 were waited for; matrix products, arithmetic and copies ran while one was open for 2% of the time, Pallas kernels for 10%

profile of v3, /device:TPU:14, one launch (start us, length us, event | category | flops | bytes accessed | tf_op | source)
XLA Modules:
  0.0 94.8 jit_solution(6156804830571336408)
XLA Ops:
  0.6 3.8 %shard_map.112 = (f32[2560,128]{1,0:T(8,128)}, s32[256]{0:T(256)}) custom-call(s32[256]{0:T(256)} %target_hbm.1, s32[256]{0:T(256)} %count_hbm.1, f32[3,256,128]{2,1,0:T(8,128)} %bitcast.25, f32[256,128]{1,0:T(8,128)} %radi_hbm.1, s32[256,128]{1,0:T(8,128)} %cell_hbm.1), custom_call_target="tpu_custom_call" | custom-call | tf_op jit(solution)/shard_map/pallas_call | solution.py:488
  4.5 0.0 copy-start.6
  4.5 0.0 copy-start
  4.5 0.0 copy-start.2
  4.5 0.0 copy-start.3
  4.5 10.4 %all-to-all-start = ((f32[640,4,128]{2,1,0:T(4,128)}), f32[640,4,128]{2,1,0:T(4,128)S(1)}, u32[]{:S(2)}, u32[]{:S(2)}) async-start(f32[640,4,128]{2,1,0:T(4,128)} %bitcast.24), calls=%async_computation | async-start | bytes 2621440 | tf_op jit(solution)/shard_map/all_to_all | solution.py:477
  14.9 5.4 %collective-permute-start.1 = (f32[7,16,128]{2,1,0:T(8,128)S(1)}, f32[7,16,128]{2,1,0:T(8,128)S(1)}, u32[]{:S(2)}, u32[]{:S(2)}) collective-permute-start(f32[7,16,128]{2,1,0:T(8,128)S(1)} %get-tuple-element.25), channel_id=1, source_target_pairs={{1,0},{2,1},{3,2},{4,3},{5,4},{6,5},{7,6},{8,7},{9,8},{10,9},{11,1... | collective-permute-start | bytes 172040 | tf_op jit(solution)/shard_map/ppermute | solution.py:432
  20.3 1.9 %collective-permute-start = (f32[7,16,128]{2,1,0:T(8,128)S(1)}, f32[7,16,128]{2,1,0:T(8,128)S(1)}, u32[]{:S(2)}, u32[]{:S(2)}) collective-permute-start(f32[7,16,128]{2,1,0:T(8,128)S(1)} %get-tuple-element.26), channel_id=1, source_target_pairs={{0,1},{1,2},{2,3},{3,4},{4,5},{5,6},{6,7},{7,8},{8,9},{9,10},{10,1... | collective-permute-start | bytes 172040 | tf_op jit(solution)/shard_map/ppermute | solution.py:432
  22.3 0.2 slice_reduce_fusion
  22.5 3.4 %collective-permute-start.2 = (f32[7,32]{1,0:T(8,128)S(1)}, f32[7,32]{1,0:T(8,128)S(1)}, u32[]{:S(2)}, u32[]{:S(2)}) collective-permute-start(f32[7,32]{1,0:T(8,128)S(1)} %get-tuple-element.22), channel_id=1, source_target_pairs={{0,32},{32,64},{64,96},{1,33},{33,65},{65,97},{2,34},{34,66},{66,9... | collective-permute-start | bytes 2696 | tf_op jit(solution)/shard_map/ppermute | solution.py:432
  25.9 2.4 %collective-permute-start.3 = (f32[7,32]{1,0:T(8,128)S(1)}, f32[7,32]{1,0:T(8,128)S(1)}, u32[]{:S(2)}, u32[]{:S(2)}) collective-permute-start(f32[7,32]{1,0:T(8,128)S(1)} %get-tuple-element.21), channel_id=1, source_target_pairs={{32,0},{64,32},{96,64},{33,1},{65,33},{97,65},{34,2},{66,34},{98,6... | collective-permute-start | bytes 2696 | tf_op jit(solution)/shard_map/ppermute | solution.py:432
  28.3 0.3 collective-permute-done.2
  28.6 0.1 copy.33.low_z
  28.7 2.7 %collective-permute-done.3 = f32[7,32]{1,0:T(8,128)S(1)} collective-permute-done((f32[7,32]{1,0:T(8,128)S(1)}, f32[7,32]{1,0:T(8,128)S(1)}, u32[]{:S(2)}, u32[]{:S(2)}) %collective-permute-start.3) | collective-permute-done | bytes 928 | tf_op jit(solution)/shard_map/ppermute | solution.py:432
  31.4 0.1 copy.34.high_z
  31.5 0.0 collective-permute-done.1.high_x
  31.5 2.4 %collective-permute-done.low_x = f32[7,16,128]{2,1,0:T(8,128)S(1)} collective-permute-done((f32[7,16,128]{2,1,0:T(8,128)S(1)}, f32[7,16,128]{2,1,0:T(8,128)S(1)}, u32[]{:S(2)}, u32[]{:S(2)}) %collective-permute-start) | collective-permute-done | bytes 57376 | tf_op jit(solution)/shard_map/ppermute | solution.py:432
  34.0 25.2 %shard_map.113 = (f32[2048,128]{1,0:T(8,128)}, f32[7,32,128]{2,1,0:T(8,128)S(1)}, f32[112,256]{1,0:T(8,128)S(1)}, f32[48,7,8,128]{3,2,1,0:T(8,128)S(1)}) custom-call(f32[3]{0:T(128)S(1)} %copy-done.2, f32[3]{0:T(128)S(1)} %copy-done.3, f32[7]{0:T(128)S(1)} %copy-done, f32[2560,128]{1,0:T(8,128)S(1)} %bitcast.17, f32[7,32,128]{2,1,0:T(8,128)S(1)} %bitcast.22, ...), custom_call_target="tpu_custom_call" | custom-call | tf_op jit(solution)/shard_map/pallas_call | solution.py:446
  59.2 1.1 %copy-done.4 = f32[48,7,8,128]{3,2,1,0:T(8,128)} copy-done((f32[48,7,8,128]{3,2,1,0:T(8,128)}, f32[48,7,8,128]{3,2,1,0:T(8,128)S(1)}, u32[]{:S(2)}) %copy-start.4) | copy-done | bytes 1376280
  60.3 8.0 %all-to-all-start.1 = ((f32[512,4,128]{2,1,0:T(4,128)}), f32[512,4,128]{2,1,0:T(4,128)S(1)}, u32[]{:S(2)}, u32[]{:S(2)}) async-start(f32[512,4,128]{2,1,0:T(4,128)} %bitcast.12), calls=%async_computation.1 | async-start | bytes 2097152 | tf_op jit(solution)/shard_map/all_to_all | solution.py:477
  68.2 0.2 slice_reduce_fusion.2
  68.4 2.4 %collective-permute-start.7 = (f32[7,32]{1,0:T(8,128)S(1)}, f32[7,32]{1,0:T(8,128)S(1)}, u32[]{:S(2)}, u32[]{:S(2)}) collective-permute-start(f32[7,32]{1,0:T(8,128)S(1)} %get-tuple-element.19), channel_id=1, source_target_pairs={{32,0},{64,32},{96,64},{33,1},{65,33},{97,65},{34,2},{66,34},{98,6... | collective-permute-start | bytes 2696 | tf_op jit(solution)/shard_map/ppermute | solution.py:432
  70.8 3.4 %collective-permute-start.6 = (f32[7,32]{1,0:T(8,128)S(1)}, f32[7,32]{1,0:T(8,128)S(1)}, u32[]{:S(2)}, u32[]{:S(2)}) collective-permute-start(f32[7,32]{1,0:T(8,128)S(1)} %get-tuple-element.20), channel_id=1, source_target_pairs={{0,32},{32,64},{64,96},{1,33},{33,65},{65,97},{2,34},{34,66},{66,9... | collective-permute-start | bytes 2696 | tf_op jit(solution)/shard_map/ppermute | solution.py:432
  74.3 4.9 %collective-permute-start.5 = (f32[7,16,128]{2,1,0:T(8,128)S(1)}, f32[7,16,128]{2,1,0:T(8,128)S(1)}, u32[]{:S(2)}, u32[]{:S(2)}) collective-permute-start(f32[7,16,128]{2,1,0:T(8,128)S(1)} %get-tuple-element.23), channel_id=1, source_target_pairs={{1,0},{2,1},{3,2},{4,3},{5,4},{6,5},{7,6},{8,7},{9,8},{10,9},{11,1... | collective-permute-start | bytes 172040 | tf_op jit(solution)/shard_map/ppermute | solution.py:432
  79.2 1.9 %collective-permute-start.4 = (f32[7,16,128]{2,1,0:T(8,128)S(1)}, f32[7,16,128]{2,1,0:T(8,128)S(1)}, u32[]{:S(2)}, u32[]{:S(2)}) collective-permute-start(f32[7,16,128]{2,1,0:T(8,128)S(1)} %get-tuple-element.24), channel_id=1, source_target_pairs={{0,1},{1,2},{2,3},{3,4},{4,5},{5,6},{6,7},{7,8},{8,9},{9,10},{10,1... | collective-permute-start | bytes 172040 | tf_op jit(solution)/shard_map/ppermute | solution.py:432
  81.1 1.3 %copy-done.5 = f32[48,7,8,128]{3,2,1,0:T(8,128)S(1)} copy-done((f32[48,7,8,128]{3,2,1,0:T(8,128)S(1)}, f32[48,7,8,128]{3,2,1,0:T(8,128)}, u32[]{:S(2)}) %copy-start.5) | copy-done | bytes 1376280
  82.4 8.8 %shard_map.114.acc = f32[112,256]{1,0:T(8,128)S(1)} custom-call(f32[2560,128]{1,0:T(8,128)S(1)} %bitcast.18, f32[48,7,8,128]{3,2,1,0:T(8,128)S(1)} %copy-done.5, f32[112,256]{1,0:T(8,128)S(1)} %get-tuple-element.14.before), custom_call_target="tpu_custom_call" | custom-call | flops 8000000000 | bytes 1048576 | tf_op jit(solution)/shard_map/pallas_call | solution.py:466
  91.3 0.1 copy.35.low_z
  91.4 0.1 copy.36.high_z
  91.5 0.7 shard_map.115
  92.2 0.7 copy.39
  92.9 1.9 %shard_map.116 = (f32[3,256,128]{2,1,0:T(8,128)}, f32[256,128]{1,0:T(8,128)}) custom-call(s32[256]{0:T(256)S(1)} %copy-done.1, f32[2048,128]{1,0:T(8,128)S(1)} %bitcast.19), custom_call_target="tpu_custom_call" | custom-call | tf_op jit(solution)/shard_map/pallas_call | solution.py:518
  (17 shorter events, 0.1 us)
Async XLA Ops:
  4.5 10.4 %copy-start.6 = (f32[2,16,7,128]{3,1,2,0:T(8,128)S(1)}, f32[2,16,7,128]{3,1,2,0:T(8,128)}, u32[]{:S(2)}) copy-start(f32[2,16,7,128]{3,1,2,0:T(8,128)} %param.9) | copy-start | bytes 344068
  4.5 29.5 %copy-start = (f32[7]{0:T(128)S(1)}, f32[7]{0:T(128)}, u32[]{:S(2)}) copy-start(f32[7]{0:T(128)} %rate.3) | copy-start | bytes 88
  4.5 29.5 %copy-start.2 = (f32[3]{0:T(128)S(1)}, f32[3]{0:T(128)}, u32[]{:S(2)}) copy-start(f32[3]{0:T(128)} %slope.1) | copy-start | bytes 40
  4.5 29.5 %copy-start.3 = (f32[3]{0:T(128)S(1)}, f32[3]{0:T(128)}, u32[]{:S(2)}) copy-start(f32[3]{0:T(128)} %partition.1) | copy-start | bytes 40
  4.5 29.5 %all-to-all-start = ((f32[640,4,128]{2,1,0:T(4,128)}), f32[640,4,128]{2,1,0:T(4,128)S(1)}, u32[]{:S(2)}, u32[]{:S(2)}) async-start(f32[640,4,128]{2,1,0:T(4,128)} %bitcast.24), calls=%async_computation | async-start | bytes 2621440 | tf_op jit(solution)/shard_map/all_to_all | solution.py:477
  14.9 16.6 %collective-permute-start.1 = (f32[7,16,128]{2,1,0:T(8,128)S(1)}, f32[7,16,128]{2,1,0:T(8,128)S(1)}, u32[]{:S(2)}, u32[]{:S(2)}) collective-permute-start(f32[7,16,128]{2,1,0:T(8,128)S(1)} %get-tuple-element.25), channel_id=1, source_target_pairs={{1,0},{2,1},{3,2},{4,3},{5,4},{6,5},{7,6},{8,7},{9,8},{10,9},{11,1... | collective-permute-start | bytes 172040 | tf_op jit(solution)/shard_map/ppermute | solution.py:432
  20.3 13.6 %collective-permute-start = (f32[7,16,128]{2,1,0:T(8,128)S(1)}, f32[7,16,128]{2,1,0:T(8,128)S(1)}, u32[]{:S(2)}, u32[]{:S(2)}) collective-permute-start(f32[7,16,128]{2,1,0:T(8,128)S(1)} %get-tuple-element.26), channel_id=1, source_target_pairs={{0,1},{1,2},{2,3},{3,4},{4,5},{5,6},{6,7},{7,8},{8,9},{9,10},{10,1... | collective-permute-start | bytes 172040 | tf_op jit(solution)/shard_map/ppermute | solution.py:432
  22.5 6.2 %collective-permute-start.2 = (f32[7,32]{1,0:T(8,128)S(1)}, f32[7,32]{1,0:T(8,128)S(1)}, u32[]{:S(2)}, u32[]{:S(2)}) collective-permute-start(f32[7,32]{1,0:T(8,128)S(1)} %get-tuple-element.22), channel_id=1, source_target_pairs={{0,32},{32,64},{64,96},{1,33},{33,65},{65,97},{2,34},{34,66},{66,9... | collective-permute-start | bytes 2696 | tf_op jit(solution)/shard_map/ppermute | solution.py:432
  25.9 5.5 %collective-permute-start.3 = (f32[7,32]{1,0:T(8,128)S(1)}, f32[7,32]{1,0:T(8,128)S(1)}, u32[]{:S(2)}, u32[]{:S(2)}) collective-permute-start(f32[7,32]{1,0:T(8,128)S(1)} %get-tuple-element.21), channel_id=1, source_target_pairs={{32,0},{64,32},{96,64},{33,1},{65,33},{97,65},{34,2},{66,34},{98,6... | collective-permute-start | bytes 2696 | tf_op jit(solution)/shard_map/ppermute | solution.py:432
  59.2 1.1 %copy-start.4 = (f32[48,7,8,128]{3,2,1,0:T(8,128)}, f32[48,7,8,128]{3,2,1,0:T(8,128)S(1)}, u32[]{:S(2)}) copy-start(f32[48,7,8,128]{3,2,1,0:T(8,128)S(1)} %get-tuple-element.13.kept) | copy-start | bytes 4128772
  60.3 32.6 %all-to-all-start.1 = ((f32[512,4,128]{2,1,0:T(4,128)}), f32[512,4,128]{2,1,0:T(4,128)S(1)}, u32[]{:S(2)}, u32[]{:S(2)}) async-start(f32[512,4,128]{2,1,0:T(4,128)} %bitcast.12), calls=%async_computation.1 | async-start | bytes 2097152 | tf_op jit(solution)/shard_map/all_to_all | solution.py:477
  68.4 23.0 %collective-permute-start.7 = (f32[7,32]{1,0:T(8,128)S(1)}, f32[7,32]{1,0:T(8,128)S(1)}, u32[]{:S(2)}, u32[]{:S(2)}) collective-permute-start(f32[7,32]{1,0:T(8,128)S(1)} %get-tuple-element.19), channel_id=1, source_target_pairs={{32,0},{64,32},{96,64},{33,1},{65,33},{97,65},{34,2},{66,34},{98,6... | collective-permute-start | bytes 2696 | tf_op jit(solution)/shard_map/ppermute | solution.py:432
  70.8 20.4 %collective-permute-start.6 = (f32[7,32]{1,0:T(8,128)S(1)}, f32[7,32]{1,0:T(8,128)S(1)}, u32[]{:S(2)}, u32[]{:S(2)}) collective-permute-start(f32[7,32]{1,0:T(8,128)S(1)} %get-tuple-element.20), channel_id=1, source_target_pairs={{0,32},{32,64},{64,96},{1,33},{33,65},{65,97},{2,34},{34,66},{66,9... | collective-permute-start | bytes 2696 | tf_op jit(solution)/shard_map/ppermute | solution.py:432
  74.3 17.2 %collective-permute-start.5 = (f32[7,16,128]{2,1,0:T(8,128)S(1)}, f32[7,16,128]{2,1,0:T(8,128)S(1)}, u32[]{:S(2)}, u32[]{:S(2)}) collective-permute-start(f32[7,16,128]{2,1,0:T(8,128)S(1)} %get-tuple-element.23), channel_id=1, source_target_pairs={{1,0},{2,1},{3,2},{4,3},{5,4},{6,5},{7,6},{8,7},{9,8},{10,9},{11,1... | collective-permute-start | bytes 172040 | tf_op jit(solution)/shard_map/ppermute | solution.py:432
  79.2 12.3 %collective-permute-start.4 = (f32[7,16,128]{2,1,0:T(8,128)S(1)}, f32[7,16,128]{2,1,0:T(8,128)S(1)}, u32[]{:S(2)}, u32[]{:S(2)}) collective-permute-start(f32[7,16,128]{2,1,0:T(8,128)S(1)} %get-tuple-element.24), channel_id=1, source_target_pairs={{0,1},{1,2},{2,3},{3,4},{4,5},{5,6},{6,7},{7,8},{8,9},{9,10},{10,1... | collective-permute-start | bytes 172040 | tf_op jit(solution)/shard_map/ppermute | solution.py:432
  81.1 1.3 %copy-start.5 = (f32[48,7,8,128]{3,2,1,0:T(8,128)S(1)}, f32[48,7,8,128]{3,2,1,0:T(8,128)}, u32[]{:S(2)}) copy-start(f32[48,7,8,128]{3,2,1,0:T(8,128)} %copy-done.4) | copy-start | bytes 4128772
  82.4 10.5 %copy-start.1 = (s32[256]{0:T(256)S(1)}, s32[256]{0:T(256)}, u32[]{:S(2)}) copy-start(s32[256]{0:T(256)} %get-tuple-element.15.slot_of) | copy-start | bytes 3076

commit v4 on v3

--- a/solution.py
+++ b/solution.py
@@ -274,6 +274,8 @@
         store(g, 3, jnp.where(live, new_radi, radi))
         for c in range(COMPS):
             into[c] = sources[c]
+        if kept is not None:
+            into[COMPS] = load_cell(g).astype(jnp.float32)
 
     def spend(g):
         spend_group(load_cell(g), fed_rows, dims, sums)
@@ -386,12 +388,12 @@
     step(lambda g, f: back[stay(g, f), :], kept.shape[0], kept)
 
 
-def kept_kernel(dims, got, kept, before, acc):
+def kept_kernel(dims, kept, before, acc):
 
     def body(sums):
         def two(i, _):
             for g in (2 * i, 2 * i + 1):
-                spend_group(got_cell(got, g), kept.at[g], dims, sums)
+                spend_group(kept[g, COMPS].astype(jnp.int32), kept.at[g], dims, sums)
             return 0
 
         lax.fori_loop(0, kept.shape[0] // 2, two, 0)
@@ -449,7 +451,7 @@
             shape(slots * BACK, LANES),
             shape(comps, columns, size_z),
             sums,
-            shape(slots // GROUP * 3 // 4, comps, GROUP, LANES),
+            shape(slots // GROUP * 5 // 8, comps + 1, GROUP, LANES),
         ),
         [SMEM, SMEM, SMEM] + [VMEM] * 6,
         (VMEM, VMEM, VMEM, VMEM),
@@ -462,14 +464,14 @@
     )(slope, partition, rate, got, melt, *halo)
 
 
-def run_kept(got, kept, before, dims):
+def run_kept(kept, before, dims):
     return kernel_call(
         functools.partial(kept_kernel, dims),
         shape(*before.shape),
-        [VMEM] * 3,
+        [VMEM] * 2,
         VMEM,
         cost=8_000_000_000,
-    )(got, kept, before)
+    )(kept, before)
 
 
 def exchange(rows, devices):
@@ -507,7 +509,7 @@
     back, middle, acc, kept = run_steps(got, start, halo, slope, partition, rate, size_y)
     returned = exchange(back, devices)
     halo = neighbours(middle, size_y)
-    acc = run_kept(got, kept, acc, (size_x, size_y, size_z))
+    acc = run_kept(kept, acc, (size_x, size_y, size_z))
     final = kernel_call(
         finish_kernel,
         shape(comps, size_x * size_y, size_z),

time: 95.5 us -> 92.3 us (0.966)
  local copies, waits for them, and re-layouts: 4.01 us -> 1.57 us
    unnamed x15 -> x11, local copies, waits for them, and re-layouts: 2.48 us -> 0.04 us
    pallas_call x1, Pallas kernels: 8.8 us -> 7.36 us  [run_kept(): kernel_call(functools.partial(kept_kernel, dims), shape(*before.shape), [...]
  transfers between devices with their start and end apart: 10 -> 10, of which waited for: 3 -> 3; matrix products, arithmetic and copies ran while one was open for 2% -> 2% of each run, Pallas kernels for 10% -> 9%
where the time goes in v4:
time: 92.3 us; the launch traced here: 91.6 us
  starting transfers between devices  44.1 us (48%)
  Pallas kernels  39.7 us (43%)
  waiting for transfers between devices  5.43 us (6%)
  local copies, waits for them, and re-layouts  1.57 us (2%)
    pallas_call x1, Pallas kernels, run_steps(): kernel_call(steps_kernel, (shape(slots * BACK, LANES), shape(comps, colum...  25.8 us
    ppermute x8, starting transfers between devices, shift(): lax.ppermute(edge, axis, [(i, i + step) for i in range(n) if 0 <= i + ste...  25.8 us
    all_to_all x2, starting transfers between devices, exchange(): lax.all_to_all(rows.reshape(each, CAP, LANES), AXES, split_axis=0, concat...  18.3 us
    pallas_call x1, Pallas kernels, run_kept(): kernel_call(functools.partial(kept_kernel, dims), shape(*before.shape), [...  7.36 us
    ppermute x8, waiting for transfers between devices, shift(): lax.ppermute(edge, axis, [(i, i + step) for i in range(n) if 0 <= i + ste...  5.43 us
    pallas_call x1, Pallas kernels, local(): kernel_call(pack_kernel, (shape(slots * SEND, LANES), jax.ShapeDtypeStruc...  3.84 us
    pallas_call x1, Pallas kernels, local(): kernel_call(unpack_kernel, (shape(3, blocks, LANES), shape(blocks, LANES)...  1.93 us
  transfers between devices with their start and end apart: 10, of which 3 were waited for; matrix products, arithmetic and copies ran while one was open for 2% of the time, Pallas kernels for 9%

profile of v4, /device:TPU:14, one launch (start us, length us, event | category | flops | bytes accessed | tf_op | source)
XLA Modules:
  0.0 91.6 jit_solution(6860363587465822085)
XLA Ops:
  0.6 3.8 %shard_map.112 = (f32[2560,128]{1,0:T(8,128)}, s32[256]{0:T(256)}) custom-call(s32[256]{0:T(256)} %target_hbm.1, s32[256]{0:T(256)} %count_hbm.1, f32[3,256,128]{2,1,0:T(8,128)} %bitcast.24, f32[256,128]{1,0:T(8,128)} %radi_hbm.1, s32[256,128]{1,0:T(8,128)} %cell_hbm.1), custom_call_target="tpu_custom_call" | custom-call | tf_op jit(solution)/shard_map/pallas_call | solution.py:490
  4.5 0.0 copy-start.4
  4.5 0.0 copy-start
  4.5 0.0 copy-start.2
  4.5 0.0 copy-start.3
  4.5 10.4 %all-to-all-start = ((f32[640,4,128]{2,1,0:T(4,128)}), f32[640,4,128]{2,1,0:T(4,128)S(1)}, u32[]{:S(2)}, u32[]{:S(2)}) async-start(f32[640,4,128]{2,1,0:T(4,128)} %bitcast.23), calls=%async_computation | async-start | bytes 2621440 | tf_op jit(solution)/shard_map/all_to_all | solution.py:479
  15.0 5.4 %collective-permute-start.1 = (f32[7,16,128]{2,1,0:T(8,128)S(1)}, f32[7,16,128]{2,1,0:T(8,128)S(1)}, u32[]{:S(2)}, u32[]{:S(2)}) collective-permute-start(f32[7,16,128]{2,1,0:T(8,128)S(1)} %get-tuple-element.25), channel_id=1, source_target_pairs={{1,0},{2,1},{3,2},{4,3},{5,4},{6,5},{7,6},{8,7},{9,8},{10,9},{11,1... | collective-permute-start | bytes 172040 | tf_op jit(solution)/shard_map/ppermute | solution.py:434
  20.3 1.9 %collective-permute-start = (f32[7,16,128]{2,1,0:T(8,128)S(1)}, f32[7,16,128]{2,1,0:T(8,128)S(1)}, u32[]{:S(2)}, u32[]{:S(2)}) collective-permute-start(f32[7,16,128]{2,1,0:T(8,128)S(1)} %get-tuple-element.26), channel_id=1, source_target_pairs={{0,1},{1,2},{2,3},{3,4},{4,5},{5,6},{6,7},{7,8},{8,9},{9,10},{10,1... | collective-permute-start | bytes 172040 | tf_op jit(solution)/shard_map/ppermute | solution.py:434
  22.3 0.2 slice_reduce_fusion
  22.5 3.4 %collective-permute-start.2 = (f32[7,32]{1,0:T(8,128)S(1)}, f32[7,32]{1,0:T(8,128)S(1)}, u32[]{:S(2)}, u32[]{:S(2)}) collective-permute-start(f32[7,32]{1,0:T(8,128)S(1)} %get-tuple-element.22), channel_id=1, source_target_pairs={{0,32},{32,64},{64,96},{1,33},{33,65},{65,97},{2,34},{34,66},{66,9... | collective-permute-start | bytes 2696 | tf_op jit(solution)/shard_map/ppermute | solution.py:434
  25.9 2.4 %collective-permute-start.3 = (f32[7,32]{1,0:T(8,128)S(1)}, f32[7,32]{1,0:T(8,128)S(1)}, u32[]{:S(2)}, u32[]{:S(2)}) collective-permute-start(f32[7,32]{1,0:T(8,128)S(1)} %get-tuple-element.21), channel_id=1, source_target_pairs={{32,0},{64,32},{96,64},{33,1},{65,33},{97,65},{34,2},{66,34},{98,6... | collective-permute-start | bytes 2696 | tf_op jit(solution)/shard_map/ppermute | solution.py:434
  28.3 0.3 collective-permute-done.2
  28.6 0.1 copy.33.low_z
  28.8 2.7 %collective-permute-done.3 = f32[7,32]{1,0:T(8,128)S(1)} collective-permute-done((f32[7,32]{1,0:T(8,128)S(1)}, f32[7,32]{1,0:T(8,128)S(1)}, u32[]{:S(2)}, u32[]{:S(2)}) %collective-permute-start.3) | collective-permute-done | bytes 928 | tf_op jit(solution)/shard_map/ppermute | solution.py:434
  31.4 0.1 copy.34.high_z
  31.5 0.0 collective-permute-done.1.high_x
  31.5 2.4 %collective-permute-done.low_x = f32[7,16,128]{2,1,0:T(8,128)S(1)} collective-permute-done((f32[7,16,128]{2,1,0:T(8,128)S(1)}, f32[7,16,128]{2,1,0:T(8,128)S(1)}, u32[]{:S(2)}, u32[]{:S(2)}) %collective-permute-start) | collective-permute-done | bytes 57376 | tf_op jit(solution)/shard_map/ppermute | solution.py:434
  34.0 0.0 all-to-all-done
  34.0 25.8 %shard_map.113 = (f32[2048,128]{1,0:T(8,128)}, f32[7,32,128]{2,1,0:T(8,128)S(1)}, f32[112,256]{1,0:T(8,128)S(1)}, f32[40,8,8,128]{3,2,1,0:T(8,128)S(1)}) custom-call(f32[3]{0:T(128)S(1)} %copy-done.2, f32[3]{0:T(128)S(1)} %copy-done.3, f32[7]{0:T(128)S(1)} %copy-done, f32[2560,128]{1,0:T(8,128)S(1)} %bitcast.17, f32[7,32,128]{2,1,0:T(8,128)S(1)} %bitcast.21, ...), custom_call_target="tpu_custom_call" | custom-call | tf_op jit(solution)/shard_map/pallas_call | solution.py:448
  59.8 7.9 %all-to-all-start.1 = ((f32[512,4,128]{2,1,0:T(4,128)}), f32[512,4,128]{2,1,0:T(4,128)S(1)}, u32[]{:S(2)}, u32[]{:S(2)}) async-start(f32[512,4,128]{2,1,0:T(4,128)} %bitcast.12), calls=%async_computation.1 | async-start | bytes 2097152 | tf_op jit(solution)/shard_map/all_to_all | solution.py:479
  67.8 0.2 slice_reduce_fusion.2
  68.0 2.4 %collective-permute-start.7 = (f32[7,32]{1,0:T(8,128)S(1)}, f32[7,32]{1,0:T(8,128)S(1)}, u32[]{:S(2)}, u32[]{:S(2)}) collective-permute-start(f32[7,32]{1,0:T(8,128)S(1)} %get-tuple-element.19), channel_id=1, source_target_pairs={{32,0},{64,32},{96,64},{33,1},{65,33},{97,65},{34,2},{66,34},{98,6... | collective-permute-start | bytes 2696 | tf_op jit(solution)/shard_map/ppermute | solution.py:434
  70.4 3.4 %collective-permute-start.6 = (f32[7,32]{1,0:T(8,128)S(1)}, f32[7,32]{1,0:T(8,128)S(1)}, u32[]{:S(2)}, u32[]{:S(2)}) collective-permute-start(f32[7,32]{1,0:T(8,128)S(1)} %get-tuple-element.20), channel_id=1, source_target_pairs={{0,32},{32,64},{64,96},{1,33},{33,65},{65,97},{2,34},{34,66},{66,9... | collective-permute-start | bytes 2696 | tf_op jit(solution)/shard_map/ppermute | solution.py:434
  73.9 4.9 %collective-permute-start.5 = (f32[7,16,128]{2,1,0:T(8,128)S(1)}, f32[7,16,128]{2,1,0:T(8,128)S(1)}, u32[]{:S(2)}, u32[]{:S(2)}) collective-permute-start(f32[7,16,128]{2,1,0:T(8,128)S(1)} %get-tuple-element.23), channel_id=1, source_target_pairs={{1,0},{2,1},{3,2},{4,3},{5,4},{6,5},{7,6},{8,7},{9,8},{10,9},{11,1... | collective-permute-start | bytes 172040 | tf_op jit(solution)/shard_map/ppermute | solution.py:434
  78.7 1.9 %collective-permute-start.4 = (f32[7,16,128]{2,1,0:T(8,128)S(1)}, f32[7,16,128]{2,1,0:T(8,128)S(1)}, u32[]{:S(2)}, u32[]{:S(2)}) collective-permute-start(f32[7,16,128]{2,1,0:T(8,128)S(1)} %get-tuple-element.24), channel_id=1, source_target_pairs={{0,1},{1,2},{2,3},{3,4},{4,5},{5,6},{6,7},{7,8},{8,9},{9,10},{10,1... | collective-permute-start | bytes 172040 | tf_op jit(solution)/shard_map/ppermute | solution.py:434
  80.6 0.0 copy-start.1
  80.7 7.4 %shard_map.114.acc = f32[112,256]{1,0:T(8,128)S(1)} custom-call(f32[40,8,8,128]{3,2,1,0:T(8,128)S(1)} %get-tuple-element.13.kept, f32[112,256]{1,0:T(8,128)S(1)} %get-tuple-element.14.before), custom_call_target="tpu_custom_call" | custom-call | flops 8000000000 | bytes 1048576 | tf_op jit(solution)/shard_map/pallas_call | solution.py:468
  88.0 0.1 copy.35.low_z
  88.2 0.1 copy.36.high_z
  88.3 0.7 shard_map.115
  89.0 0.7 copy.39
  89.7 1.9 %shard_map.116 = (f32[3,256,128]{2,1,0:T(8,128)}, f32[256,128]{1,0:T(8,128)}) custom-call(s32[256]{0:T(256)S(1)} %copy-done.1, f32[2048,128]{1,0:T(8,128)S(1)} %bitcast.18), custom_call_target="tpu_custom_call" | custom-call | tf_op jit(solution)/shard_map/pallas_call | solution.py:520
  (13 shorter events, 0.1 us)
Async XLA Ops:
  4.5 10.4 %copy-start.4 = (f32[2,16,7,128]{3,1,2,0:T(8,128)S(1)}, f32[2,16,7,128]{3,1,2,0:T(8,128)}, u32[]{:S(2)}) copy-start(f32[2,16,7,128]{3,1,2,0:T(8,128)} %param.9) | copy-start | bytes 344068
  4.5 29.5 %copy-start = (f32[7]{0:T(128)S(1)}, f32[7]{0:T(128)}, u32[]{:S(2)}) copy-start(f32[7]{0:T(128)} %rate.3) | copy-start | bytes 88
  4.5 29.5 %copy-start.2 = (f32[3]{0:T(128)S(1)}, f32[3]{0:T(128)}, u32[]{:S(2)}) copy-start(f32[3]{0:T(128)} %slope.1) | copy-start | bytes 40
  4.5 29.5 %copy-start.3 = (f32[3]{0:T(128)S(1)}, f32[3]{0:T(128)}, u32[]{:S(2)}) copy-start(f32[3]{0:T(128)} %partition.1) | copy-start | bytes 40
  4.5 29.5 %all-to-all-start = ((f32[640,4,128]{2,1,0:T(4,128)}), f32[640,4,128]{2,1,0:T(4,128)S(1)}, u32[]{:S(2)}, u32[]{:S(2)}) async-start(f32[640,4,128]{2,1,0:T(4,128)} %bitcast.23), calls=%async_computation | async-start | bytes 2621440 | tf_op jit(solution)/shard_map/all_to_all | solution.py:479
  15.0 16.6 %collective-permute-start.1 = (f32[7,16,128]{2,1,0:T(8,128)S(1)}, f32[7,16,128]{2,1,0:T(8,128)S(1)}, u32[]{:S(2)}, u32[]{:S(2)}) collective-permute-start(f32[7,16,128]{2,1,0:T(8,128)S(1)} %get-tuple-element.25), channel_id=1, source_target_pairs={{1,0},{2,1},{3,2},{4,3},{5,4},{6,5},{7,6},{8,7},{9,8},{10,9},{11,1... | collective-permute-start | bytes 172040 | tf_op jit(solution)/shard_map/ppermute | solution.py:434
  20.3 13.6 %collective-permute-start = (f32[7,16,128]{2,1,0:T(8,128)S(1)}, f32[7,16,128]{2,1,0:T(8,128)S(1)}, u32[]{:S(2)}, u32[]{:S(2)}) collective-permute-start(f32[7,16,128]{2,1,0:T(8,128)S(1)} %get-tuple-element.26), channel_id=1, source_target_pairs={{0,1},{1,2},{2,3},{3,4},{4,5},{5,6},{6,7},{7,8},{8,9},{9,10},{10,1... | collective-permute-start | bytes 172040 | tf_op jit(solution)/shard_map/ppermute | solution.py:434
  22.5 6.2 %collective-permute-start.2 = (f32[7,32]{1,0:T(8,128)S(1)}, f32[7,32]{1,0:T(8,128)S(1)}, u32[]{:S(2)}, u32[]{:S(2)}) collective-permute-start(f32[7,32]{1,0:T(8,128)S(1)} %get-tuple-element.22), channel_id=1, source_target_pairs={{0,32},{32,64},{64,96},{1,33},{33,65},{65,97},{2,34},{34,66},{66,9... | collective-permute-start | bytes 2696 | tf_op jit(solution)/shard_map/ppermute | solution.py:434
  25.9 5.5 %collective-permute-start.3 = (f32[7,32]{1,0:T(8,128)S(1)}, f32[7,32]{1,0:T(8,128)S(1)}, u32[]{:S(2)}, u32[]{:S(2)}) collective-permute-start(f32[7,32]{1,0:T(8,128)S(1)} %get-tuple-element.21), channel_id=1, source_target_pairs={{32,0},{64,32},{96,64},{33,1},{65,33},{97,65},{34,2},{66,34},{98,6... | collective-permute-start | bytes 2696 | tf_op jit(solution)/shard_map/ppermute | solution.py:434
  59.8 29.9 %all-to-all-start.1 = ((f32[512,4,128]{2,1,0:T(4,128)}), f32[512,4,128]{2,1,0:T(4,128)S(1)}, u32[]{:S(2)}, u32[]{:S(2)}) async-start(f32[512,4,128]{2,1,0:T(4,128)} %bitcast.12), calls=%async_computation.1 | async-start | bytes 2097152 | tf_op jit(solution)/shard_map/all_to_all | solution.py:479
  68.0 20.2 %collective-permute-start.7 = (f32[7,32]{1,0:T(8,128)S(1)}, f32[7,32]{1,0:T(8,128)S(1)}, u32[]{:S(2)}, u32[]{:S(2)}) collective-permute-start(f32[7,32]{1,0:T(8,128)S(1)} %get-tuple-element.19), channel_id=1, source_target_pairs={{32,0},{64,32},{96,64},{33,1},{65,33},{97,65},{34,2},{66,34},{98,6... | collective-permute-start | bytes 2696 | tf_op jit(solution)/shard_map/ppermute | solution.py:434
  70.4 17.6 %collective-permute-start.6 = (f32[7,32]{1,0:T(8,128)S(1)}, f32[7,32]{1,0:T(8,128)S(1)}, u32[]{:S(2)}, u32[]{:S(2)}) collective-permute-start(f32[7,32]{1,0:T(8,128)S(1)} %get-tuple-element.20), channel_id=1, source_target_pairs={{0,32},{32,64},{64,96},{1,33},{33,65},{65,97},{2,34},{34,66},{66,9... | collective-permute-start | bytes 2696 | tf_op jit(solution)/shard_map/ppermute | solution.py:434
  73.9 14.4 %collective-permute-start.5 = (f32[7,16,128]{2,1,0:T(8,128)S(1)}, f32[7,16,128]{2,1,0:T(8,128)S(1)}, u32[]{:S(2)}, u32[]{:S(2)}) collective-permute-start(f32[7,16,128]{2,1,0:T(8,128)S(1)} %get-tuple-element.23), channel_id=1, source_target_pairs={{1,0},{2,1},{3,2},{4,3},{5,4},{6,5},{7,6},{8,7},{9,8},{10,9},{11,1... | collective-permute-start | bytes 172040 | tf_op jit(solution)/shard_map/ppermute | solution.py:434
  78.7 9.6 %collective-permute-start.4 = (f32[7,16,128]{2,1,0:T(8,128)S(1)}, f32[7,16,128]{2,1,0:T(8,128)S(1)}, u32[]{:S(2)}, u32[]{:S(2)}) collective-permute-start(f32[7,16,128]{2,1,0:T(8,128)S(1)} %get-tuple-element.24), channel_id=1, source_target_pairs={{0,1},{1,2},{2,3},{3,4},{4,5},{5,6},{6,7},{7,8},{8,9},{9,10},{10,1... | collective-permute-start | bytes 172040 | tf_op jit(solution)/shard_map/ppermute | solution.py:434
  80.6 9.0 %copy-start.1 = (s32[256]{0:T(256)S(1)}, s32[256]{0:T(256)}, u32[]{:S(2)}) copy-start(s32[256]{0:T(256)} %get-tuple-element.15.slot_of) | copy-start | bytes 3076

commit v5 on v4

--- a/solution.py
+++ b/solution.py
@@ -291,11 +291,16 @@
             work(g, unpaired(found), fed_rows)
             return later
 
-        def two(i, found):
-            return group(2 * i + 1, group(2 * i, found))
+        def four(i, found):
+            for r in range(4):
+                found = group(4 * i + r, found)
+            return found
 
         work(first, unpaired(look(first)), fed_rows)
-        lax.fori_loop(first // 2 + 1, stop // 2, two, group(first + 1, look(first + 1)))
+        found = look(first + 1)
+        for r in range(1, 4):
+            found = group(first + r, found)
+        lax.fori_loop(first // 4 + 1, stop // 4, four, found)
         spend(last)
     else:
 
@@ -407,7 +412,9 @@
     size_x = melt.shape[1] // size_y
     for c in range(COMPS):
         fresh = diffused(melt[c], low_x[c], high_x[c], low_z[c], high_z[c], rate[c])
-        out[c] = fresh + deposit_of(acc, c, size_x, size_y)
+        fresh = fresh + deposit_of(acc, c, size_x, size_y)
+        for x in range(size_x):
+            out[x, c] = fresh[x * size_y : (x + 1) * size_y]
 
 
 def kernel_call(kernel, outs, in_specs, out_specs, scratch=(), limit=LIMIT, cost=None):
@@ -451,7 +458,7 @@
             shape(slots * BACK, LANES),
             shape(comps, columns, size_z),
             sums,
-            shape(slots // GROUP * 5 // 8, comps + 1, GROUP, LANES),
+            shape(slots // GROUP // 2, comps + 1, GROUP, LANES),
         ),
         [SMEM, SMEM, SMEM] + [VMEM] * 6,
         (VMEM, VMEM, VMEM, VMEM),
@@ -512,11 +519,11 @@
     acc = run_kept(kept, acc, (size_x, size_y, size_z))
     final = kernel_call(
         finish_kernel,
-        shape(comps, size_x * size_y, size_z),
+        shape(size_x, comps, size_y, size_z),
         [SMEM] + [VMEM] * 6,
         VMEM,
     )(rate, middle, acc, *halo)
-    melt_out = jnp.transpose(final.reshape(comps, size_x, size_y, size_z), (1, 2, 0, 3))
+    melt_out = jnp.transpose(final, (0, 2, 1, 3))
     velocity_out, radius_out = kernel_call(
         unpack_kernel,
         (shape(3, blocks, LANES), shape(blocks, LANES)),

time: 92.3 us -> 91.2 us (0.988)
    pallas_call x1, Pallas kernels: 7.36 us -> 5.92 us  [run_kept(): kernel_call(functools.partial(kept_kernel, dims), shape(*before.shape), [...]
  transfers between devices with their start and end apart: 10 -> 10, of which waited for: 3 -> 3; matrix products, arithmetic and copies ran while one was open for 2% -> 1% of each run, Pallas kernels for 9% -> 8%
where the time goes in v5:
time: 91.2 us; the launch traced here: 90.6 us
  starting transfers between devices  44.1 us (48%)
  Pallas kernels  39.3 us (43%)
  waiting for transfers between devices  5.43 us (6%)
    pallas_call x1, Pallas kernels, run_steps(): kernel_call(steps_kernel, (shape(slots * BACK, LANES), shape(comps, colum...  26.2 us
    ppermute x8, starting transfers between devices, shift(): lax.ppermute(edge, axis, [(i, i + step) for i in range(n) if 0 <= i + ste...  25.8 us
    all_to_all x2, starting transfers between devices, exchange(): lax.all_to_all(rows.reshape(each, CAP, LANES), AXES, split_axis=0, concat...  18.3 us
    pallas_call x1, Pallas kernels, run_kept(): kernel_call(functools.partial(kept_kernel, dims), shape(*before.shape), [...  5.92 us
    ppermute x8, waiting for transfers between devices, shift(): lax.ppermute(edge, axis, [(i, i + step) for i in range(n) if 0 <= i + ste...  5.43 us
    pallas_call x1, Pallas kernels, local(): kernel_call(pack_kernel, (shape(slots * SEND, LANES), jax.ShapeDtypeStruc...  3.84 us
    pallas_call x1, Pallas kernels, local(): kernel_call(unpack_kernel, (shape(3, blocks, LANES), shape(blocks, LANES)...  1.93 us
  transfers between devices with their start and end apart: 10, of which 3 were waited for; matrix products, arithmetic and copies ran while one was open for 1% of the time, Pallas kernels for 8%

profile of v5, /device:TPU:14, one launch (start us, length us, event | category | flops | bytes accessed | tf_op | source)
XLA Modules:
  0.0 90.6 jit_solution(16236114735500222681)
XLA Ops:
  0.6 3.8 %shard_map.112 = (f32[2560,128]{1,0:T(8,128)}, s32[256]{0:T(256)}) custom-call(s32[256]{0:T(256)} %target_hbm.1, s32[256]{0:T(256)} %count_hbm.1, f32[3,256,128]{2,1,0:T(8,128)} %bitcast.20, f32[256,128]{1,0:T(8,128)} %radi_hbm.1, s32[256,128]{1,0:T(8,128)} %cell_hbm.1), custom_call_target="tpu_custom_call" | custom-call | tf_op jit(solution)/shard_map/pallas_call | solution.py:497
  4.5 0.0 copy-start.4
  4.5 0.0 copy-start
  4.5 0.0 copy-start.2
  4.5 0.0 copy-start.3
  4.5 10.4 %all-to-all-start = ((f32[640,4,128]{2,1,0:T(4,128)}), f32[640,4,128]{2,1,0:T(4,128)S(1)}, u32[]{:S(2)}, u32[]{:S(2)}) async-start(f32[640,4,128]{2,1,0:T(4,128)} %bitcast.19), calls=%async_computation | async-start | bytes 2621440 | tf_op jit(solution)/shard_map/all_to_all | solution.py:486
  15.0 5.4 %collective-permute-start.1 = (f32[7,16,128]{2,1,0:T(8,128)S(1)}, f32[7,16,128]{2,1,0:T(8,128)S(1)}, u32[]{:S(2)}, u32[]{:S(2)}) collective-permute-start(f32[7,16,128]{2,1,0:T(8,128)S(1)} %get-tuple-element.25), channel_id=1, source_target_pairs={{1,0},{2,1},{3,2},{4,3},{5,4},{6,5},{7,6},{8,7},{9,8},{10,9},{11,1... | collective-permute-start | bytes 172040 | tf_op jit(solution)/shard_map/ppermute | solution.py:441
  20.3 1.9 %collective-permute-start = (f32[7,16,128]{2,1,0:T(8,128)S(1)}, f32[7,16,128]{2,1,0:T(8,128)S(1)}, u32[]{:S(2)}, u32[]{:S(2)}) collective-permute-start(f32[7,16,128]{2,1,0:T(8,128)S(1)} %get-tuple-element.26), channel_id=1, source_target_pairs={{0,1},{1,2},{2,3},{3,4},{4,5},{5,6},{6,7},{7,8},{8,9},{9,10},{10,1... | collective-permute-start | bytes 172040 | tf_op jit(solution)/shard_map/ppermute | solution.py:441
  22.3 0.2 slice_reduce_fusion
  22.5 3.4 %collective-permute-start.2 = (f32[7,32]{1,0:T(8,128)S(1)}, f32[7,32]{1,0:T(8,128)S(1)}, u32[]{:S(2)}, u32[]{:S(2)}) collective-permute-start(f32[7,32]{1,0:T(8,128)S(1)} %get-tuple-element.22), channel_id=1, source_target_pairs={{0,32},{32,64},{64,96},{1,33},{33,65},{65,97},{2,34},{34,66},{66,9... | collective-permute-start | bytes 2696 | tf_op jit(solution)/shard_map/ppermute | solution.py:441
  25.9 2.4 %collective-permute-start.3 = (f32[7,32]{1,0:T(8,128)S(1)}, f32[7,32]{1,0:T(8,128)S(1)}, u32[]{:S(2)}, u32[]{:S(2)}) collective-permute-start(f32[7,32]{1,0:T(8,128)S(1)} %get-tuple-element.21), channel_id=1, source_target_pairs={{32,0},{64,32},{96,64},{33,1},{65,33},{97,65},{34,2},{66,34},{98,6... | collective-permute-start | bytes 2696 | tf_op jit(solution)/shard_map/ppermute | solution.py:441
  28.3 0.3 collective-permute-done.2
  28.6 0.1 copy.30.low_z
  28.8 2.7 %collective-permute-done.3 = f32[7,32]{1,0:T(8,128)S(1)} collective-permute-done((f32[7,32]{1,0:T(8,128)S(1)}, f32[7,32]{1,0:T(8,128)S(1)}, u32[]{:S(2)}, u32[]{:S(2)}) %collective-permute-start.3) | collective-permute-done | bytes 928 | tf_op jit(solution)/shard_map/ppermute | solution.py:441
  31.4 0.1 copy.31.high_z
  31.5 2.4 %collective-permute-done.low_x = f32[7,16,128]{2,1,0:T(8,128)S(1)} collective-permute-done((f32[7,16,128]{2,1,0:T(8,128)S(1)}, f32[7,16,128]{2,1,0:T(8,128)S(1)}, u32[]{:S(2)}, u32[]{:S(2)}) %collective-permute-start) | collective-permute-done | bytes 57376 | tf_op jit(solution)/shard_map/ppermute | solution.py:441
  34.0 0.0 all-to-all-done
  34.0 26.2 %shard_map.113 = (f32[2048,128]{1,0:T(8,128)}, f32[7,32,128]{2,1,0:T(8,128)S(1)}, f32[112,256]{1,0:T(8,128)S(1)}, f32[32,8,8,128]{3,2,1,0:T(8,128)S(1)}) custom-call(f32[3]{0:T(128)S(1)} %copy-done.2, f32[3]{0:T(128)S(1)} %copy-done.3, f32[7]{0:T(128)S(1)} %copy-done, f32[2560,128]{1,0:T(8,128)S(1)} %bitcast.14, f32[7,32,128]{2,1,0:T(8,128)S(1)} %bitcast.18, ...), custom_call_target="tpu_custom_call" | custom-call | tf_op jit(solution)/shard_map/pallas_call | solution.py:455
  60.2 7.9 %all-to-all-start.1 = ((f32[512,4,128]{2,1,0:T(4,128)}), f32[512,4,128]{2,1,0:T(4,128)S(1)}, u32[]{:S(2)}, u32[]{:S(2)}) async-start(f32[512,4,128]{2,1,0:T(4,128)} %bitcast.11), calls=%async_computation.1 | async-start | bytes 2097152 | tf_op jit(solution)/shard_map/all_to_all | solution.py:486
  68.2 0.2 slice_reduce_fusion.2
  68.4 2.4 %collective-permute-start.7 = (f32[7,32]{1,0:T(8,128)S(1)}, f32[7,32]{1,0:T(8,128)S(1)}, u32[]{:S(2)}, u32[]{:S(2)}) collective-permute-start(f32[7,32]{1,0:T(8,128)S(1)} %get-tuple-element.19), channel_id=1, source_target_pairs={{32,0},{64,32},{96,64},{33,1},{65,33},{97,65},{34,2},{66,34},{98,6... | collective-permute-start | bytes 2696 | tf_op jit(solution)/shard_map/ppermute | solution.py:441
  70.8 3.4 %collective-permute-start.6 = (f32[7,32]{1,0:T(8,128)S(1)}, f32[7,32]{1,0:T(8,128)S(1)}, u32[]{:S(2)}, u32[]{:S(2)}) collective-permute-start(f32[7,32]{1,0:T(8,128)S(1)} %get-tuple-element.20), channel_id=1, source_target_pairs={{0,32},{32,64},{64,96},{1,33},{33,65},{65,97},{2,34},{34,66},{66,9... | collective-permute-start | bytes 2696 | tf_op jit(solution)/shard_map/ppermute | solution.py:441
  74.3 4.9 %collective-permute-start.5 = (f32[7,16,128]{2,1,0:T(8,128)S(1)}, f32[7,16,128]{2,1,0:T(8,128)S(1)}, u32[]{:S(2)}, u32[]{:S(2)}) collective-permute-start(f32[7,16,128]{2,1,0:T(8,128)S(1)} %get-tuple-element.23), channel_id=1, source_target_pairs={{1,0},{2,1},{3,2},{4,3},{5,4},{6,5},{7,6},{8,7},{9,8},{10,9},{11,1... | collective-permute-start | bytes 172040 | tf_op jit(solution)/shard_map/ppermute | solution.py:441
  79.1 1.9 %collective-permute-start.4 = (f32[7,16,128]{2,1,0:T(8,128)S(1)}, f32[7,16,128]{2,1,0:T(8,128)S(1)}, u32[]{:S(2)}, u32[]{:S(2)}) collective-permute-start(f32[7,16,128]{2,1,0:T(8,128)S(1)} %get-tuple-element.24), channel_id=1, source_target_pairs={{0,1},{1,2},{2,3},{3,4},{4,5},{5,6},{6,7},{7,8},{8,9},{9,10},{10,1... | collective-permute-start | bytes 172040 | tf_op jit(solution)/shard_map/ppermute | solution.py:441
  81.1 0.0 copy-start.1
  81.1 5.9 %shard_map.114.acc = f32[112,256]{1,0:T(8,128)S(1)} custom-call(f32[32,8,8,128]{3,2,1,0:T(8,128)S(1)} %get-tuple-element.13.kept, f32[112,256]{1,0:T(8,128)S(1)} %get-tuple-element.14.before), custom_call_target="tpu_custom_call" | custom-call | flops 8000000000 | bytes 1048576 | tf_op jit(solution)/shard_map/pallas_call | solution.py:475
  87.0 0.1 copy.32.low_z
  87.1 0.1 copy.33.high_z
  87.3 0.0 collective-permute-done.5.high_x
  87.3 0.0 collective-permute-done.4.low_x
  87.3 1.4 %shard_map.115 = f32[2,7,16,128]{3,2,1,0:T(8,128)} custom-call(f32[7]{0:T(128)S(1)} %copy-done, f32[7,32,128]{2,1,0:T(8,128)S(1)} %get-tuple-element.12.melt, f32[112,256]{1,0:T(8,128)S(1)} %shard_map.114.acc, f32[7,16,128]{2,1,0:T(8,128)S(1)} %collective-permute-done.4.low_x, f32[7,16,128]{2,1,0:T(8,128)S(1)} %collective-permute-done.5.high_x, ...), custom_call_target="tpu_custom_call" | custom-call | tf_op jit(solution)/shard_map/pallas_call | solution.py:520
  88.6 1.9 %shard_map.116 = (f32[3,256,128]{2,1,0:T(8,128)}, f32[256,128]{1,0:T(8,128)}) custom-call(s32[256]{0:T(256)S(1)} %copy-done.1, f32[2048,128]{1,0:T(8,128)S(1)} %bitcast.15), custom_call_target="tpu_custom_call" | custom-call | tf_op jit(solution)/shard_map/pallas_call | solution.py:527
  (12 shorter events, 0.1 us)
Async XLA Ops:
  4.5 10.4 %copy-start.4 = (f32[2,16,7,128]{3,1,2,0:T(8,128)S(1)}, f32[2,16,7,128]{3,1,2,0:T(8,128)}, u32[]{:S(2)}) copy-start(f32[2,16,7,128]{3,1,2,0:T(8,128)} %param.9) | copy-start | bytes 344068
  4.5 29.5 %copy-start = (f32[7]{0:T(128)S(1)}, f32[7]{0:T(128)}, u32[]{:S(2)}) copy-start(f32[7]{0:T(128)} %rate.3) | copy-start | bytes 88
  4.5 29.5 %copy-start.2 = (f32[3]{0:T(128)S(1)}, f32[3]{0:T(128)}, u32[]{:S(2)}) copy-start(f32[3]{0:T(128)} %slope.1) | copy-start | bytes 40
  4.5 29.5 %copy-start.3 = (f32[3]{0:T(128)S(1)}, f32[3]{0:T(128)}, u32[]{:S(2)}) copy-start(f32[3]{0:T(128)} %partition.1) | copy-start | bytes 40
  4.5 29.5 %all-to-all-start = ((f32[640,4,128]{2,1,0:T(4,128)}), f32[640,4,128]{2,1,0:T(4,128)S(1)}, u32[]{:S(2)}, u32[]{:S(2)}) async-start(f32[640,4,128]{2,1,0:T(4,128)} %bitcast.19), calls=%async_computation | async-start | bytes 2621440 | tf_op jit(solution)/shard_map/all_to_all | solution.py:486
  15.0 16.6 %collective-permute-start.1 = (f32[7,16,128]{2,1,0:T(8,128)S(1)}, f32[7,16,128]{2,1,0:T(8,128)S(1)}, u32[]{:S(2)}, u32[]{:S(2)}) collective-permute-start(f32[7,16,128]{2,1,0:T(8,128)S(1)} %get-tuple-element.25), channel_id=1, source_target_pairs={{1,0},{2,1},{3,2},{4,3},{5,4},{6,5},{7,6},{8,7},{9,8},{10,9},{11,1... | collective-permute-start | bytes 172040 | tf_op jit(solution)/shard_map/ppermute | solution.py:441
  20.3 13.6 %collective-permute-start = (f32[7,16,128]{2,1,0:T(8,128)S(1)}, f32[7,16,128]{2,1,0:T(8,128)S(1)}, u32[]{:S(2)}, u32[]{:S(2)}) collective-permute-start(f32[7,16,128]{2,1,0:T(8,128)S(1)} %get-tuple-element.26), channel_id=1, source_target_pairs={{0,1},{1,2},{2,3},{3,4},{4,5},{5,6},{6,7},{7,8},{8,9},{9,10},{10,1... | collective-permute-start | bytes 172040 | tf_op jit(solution)/shard_map/ppermute | solution.py:441
  22.5 6.2 %collective-permute-start.2 = (f32[7,32]{1,0:T(8,128)S(1)}, f32[7,32]{1,0:T(8,128)S(1)}, u32[]{:S(2)}, u32[]{:S(2)}) collective-permute-start(f32[7,32]{1,0:T(8,128)S(1)} %get-tuple-element.22), channel_id=1, source_target_pairs={{0,32},{32,64},{64,96},{1,33},{33,65},{65,97},{2,34},{34,66},{66,9... | collective-permute-start | bytes 2696 | tf_op jit(solution)/shard_map/ppermute | solution.py:441
  25.9 5.5 %collective-permute-start.3 = (f32[7,32]{1,0:T(8,128)S(1)}, f32[7,32]{1,0:T(8,128)S(1)}, u32[]{:S(2)}, u32[]{:S(2)}) collective-permute-start(f32[7,32]{1,0:T(8,128)S(1)} %get-tuple-element.21), channel_id=1, source_target_pairs={{32,0},{64,32},{96,64},{33,1},{65,33},{97,65},{34,2},{66,34},{98,6... | collective-permute-start | bytes 2696 | tf_op jit(solution)/shard_map/ppermute | solution.py:441
  60.2 28.4 %all-to-all-start.1 = ((f32[512,4,128]{2,1,0:T(4,128)}), f32[512,4,128]{2,1,0:T(4,128)S(1)}, u32[]{:S(2)}, u32[]{:S(2)}) async-start(f32[512,4,128]{2,1,0:T(4,128)} %bitcast.11), calls=%async_computation.1 | async-start | bytes 2097152 | tf_op jit(solution)/shard_map/all_to_all | solution.py:486
  68.4 18.7 %collective-permute-start.7 = (f32[7,32]{1,0:T(8,128)S(1)}, f32[7,32]{1,0:T(8,128)S(1)}, u32[]{:S(2)}, u32[]{:S(2)}) collective-permute-start(f32[7,32]{1,0:T(8,128)S(1)} %get-tuple-element.19), channel_id=1, source_target_pairs={{32,0},{64,32},{96,64},{33,1},{65,33},{97,65},{34,2},{66,34},{98,6... | collective-permute-start | bytes 2696 | tf_op jit(solution)/shard_map/ppermute | solution.py:441
  70.8 16.2 %collective-permute-start.6 = (f32[7,32]{1,0:T(8,128)S(1)}, f32[7,32]{1,0:T(8,128)S(1)}, u32[]{:S(2)}, u32[]{:S(2)}) collective-permute-start(f32[7,32]{1,0:T(8,128)S(1)} %get-tuple-element.20), channel_id=1, source_target_pairs={{0,32},{32,64},{64,96},{1,33},{33,65},{65,97},{2,34},{34,66},{66,9... | collective-permute-start | bytes 2696 | tf_op jit(solution)/shard_map/ppermute | solution.py:441
  74.3 13.0 %collective-permute-start.5 = (f32[7,16,128]{2,1,0:T(8,128)S(1)}, f32[7,16,128]{2,1,0:T(8,128)S(1)}, u32[]{:S(2)}, u32[]{:S(2)}) collective-permute-start(f32[7,16,128]{2,1,0:T(8,128)S(1)} %get-tuple-element.23), channel_id=1, source_target_pairs={{1,0},{2,1},{3,2},{4,3},{5,4},{6,5},{7,6},{8,7},{9,8},{10,9},{11,1... | collective-permute-start | bytes 172040 | tf_op jit(solution)/shard_map/ppermute | solution.py:441
  79.1 8.1 %collective-permute-start.4 = (f32[7,16,128]{2,1,0:T(8,128)S(1)}, f32[7,16,128]{2,1,0:T(8,128)S(1)}, u32[]{:S(2)}, u32[]{:S(2)}) collective-permute-start(f32[7,16,128]{2,1,0:T(8,128)S(1)} %get-tuple-element.24), channel_id=1, source_target_pairs={{0,1},{1,2},{2,3},{3,4},{4,5},{5,6},{6,7},{7,8},{8,9},{9,10},{10,1... | collective-permute-start | bytes 172040 | tf_op jit(solution)/shard_map/ppermute | solution.py:441
  81.1 7.6 %copy-start.1 = (s32[256]{0:T(256)S(1)}, s32[256]{0:T(256)}, u32[]{:S(2)}) copy-start(s32[256]{0:T(256)} %get-tuple-element.15.slot_of) | copy-start | bytes 3076

commit v6 on v5

--- a/solution.py
+++ b/solution.py
@@ -436,15 +436,21 @@
 
 
 def neighbours(melt, size_y):
-    def shift(edge, axis, step):
+    def swap(low_face, high_face, axis):
         n = lax.axis_size(axis)
-        return lax.ppermute(edge, axis, [(i, i + step) for i in range(n) if 0 <= i + step < n])
-
-    low_x = shift(melt[:, -size_y:, :], "brick", 1)
-    high_x = shift(melt[:, :size_y, :], "brick", -1)
-    low_z = shift(melt[:, :, -1], "sec", 1)[:, :, None]
-    high_z = shift(melt[:, :, 0], "sec", -1)[:, :, None]
-    return low_x, high_x, low_z, high_z
+        even = lax.axis_index(axis) % 2 == 0
+
+        def meet(face, start):
+            pairs = [(i, i + 1) for i in range(start, n - 1, 2)]
+            return lax.ppermute(face, axis, pairs + [(j, i) for i, j in pairs])
+
+        first = meet(jnp.where(even, high_face, low_face), 0)
+        second = meet(jnp.where(even, low_face, high_face), 1)
+        return jnp.where(even, second, first), jnp.where(even, first, second)
+
+    low_x, high_x = swap(melt[:, :size_y, :], melt[:, -size_y:, :], "brick")
+    low_z, high_z = swap(melt[:, :, 0], melt[:, :, -1], "sec")
+    return low_x, high_x, low_z[:, :, None], high_z[:, :, None]
 
 
 def run_steps(got, melt, halo, slope, partition, rate, size_y):
@@ -458,7 +464,7 @@
             shape(slots * BACK, LANES),
             shape(comps, columns, size_z),
             sums,
-            shape(slots // GROUP // 2, comps + 1, GROUP, LANES),
+            shape(slots // GROUP * 3 // 4, comps + 1, GROUP, LANES),
         ),
         [SMEM, SMEM, SMEM] + [VMEM] * 6,
         (VMEM, VMEM, VMEM, VMEM),

time: 91.2 us -> 91.1 us (level)
  starting transfers between devices: 44.1 us -> 39.4 us
  waiting for transfers between devices: 5.43 us -> 7.96 us
  Pallas kernels: 39.3 us -> 40.8 us
    ppermute x8, starting transfers between devices: 25.8 us -> 21.1 us  [meet(): return lax.ppermute(face, axis, pairs + [(j, i) for i, j in pairs])]
    pallas_call x1, Pallas kernels: 5.92 us -> 8.81 us  [run_kept(): kernel_call(functools.partial(kept_kernel, dims), shape(*before.shape), [...]
    ppermute x8, waiting for transfers between devices: 5.43 us -> 7.96 us  [meet(): return lax.ppermute(face, axis, pairs + [(j, i) for i, j in pairs])]
    pallas_call x1, Pallas kernels: 26.2 us -> 24.8 us  [run_steps(): kernel_call(steps_kernel, (shape(slots * BACK, LANES), shape(comps, colum...]
  transfers between devices with their start and end apart: 10 -> 10, of which waited for: 3 -> 2; matrix products, arithmetic and copies ran while one was open for 1% -> 1% of each run, Pallas kernels for 8% -> 11%
where the time goes in v6:
time: 91.1 us; the launch traced here: 90.7 us
  Pallas kernels  40.8 us (45%)
  starting transfers between devices  39.4 us (43%)
  waiting for transfers between devices  7.96 us (9%)
  local copies, waits for them, and re-layouts  1.18 us (1%)
    pallas_call x1, Pallas kernels, run_steps(): kernel_call(steps_kernel, (shape(slots * BACK, LANES), shape(comps, colum...  24.8 us
    ppermute x8, starting transfers between devices, meet(): return lax.ppermute(face, axis, pairs + [(j, i) for i, j in pairs])  21.1 us
    all_to_all x2, starting transfers between devices, exchange(): lax.all_to_all(rows.reshape(each, CAP, LANES), AXES, split_axis=0, concat...  18.3 us
    pallas_call x1, Pallas kernels, run_kept(): kernel_call(functools.partial(kept_kernel, dims), shape(*before.shape), [...  8.81 us
    ppermute x8, waiting for transfers between devices, meet(): return lax.ppermute(face, axis, pairs + [(j, i) for i, j in pairs])  7.96 us
    pallas_call x1, Pallas kernels, local(): kernel_call(pack_kernel, (shape(slots * SEND, LANES), jax.ShapeDtypeStruc...  3.85 us
    pallas_call x1, Pallas kernels, local(): kernel_call(unpack_kernel, (shape(3, blocks, LANES), shape(blocks, LANES)...  1.93 us
  transfers between devices with their start and end apart: 10, of which 2 were waited for; matrix products, arithmetic and copies ran while one was open for 1% of the time, Pallas kernels for 11%

profile of v6, /device:TPU:14, one launch (start us, length us, event | category | flops | bytes accessed | tf_op | source)
XLA Modules:
  0.0 90.7 jit_solution(5287293276752408556)
XLA Ops:
  0.6 3.8 %shard_map.112 = (f32[2560,128]{1,0:T(8,128)}, s32[256]{0:T(256)}) custom-call(s32[256]{0:T(256)} %target_hbm.1, s32[256]{0:T(256)} %count_hbm.1, f32[3,256,128]{2,1,0:T(8,128)} %bitcast.24, f32[256,128]{1,0:T(8,128)} %radi_hbm.1, s32[256,128]{1,0:T(8,128)} %cell_hbm.1), custom_call_target="tpu_custom_call" | custom-call | tf_op jit(solution)/shard_map/pallas_call | solution.py:503
  4.5 0.0 copy-start.6
  4.5 0.0 copy-start
  4.5 0.0 copy-start.2
  4.5 0.0 copy-start.3
  4.5 10.4 %all-to-all-start = ((f32[640,4,128]{2,1,0:T(4,128)}), f32[640,4,128]{2,1,0:T(4,128)S(1)}, u32[]{:S(2)}, u32[]{:S(2)}) async-start(f32[640,4,128]{2,1,0:T(4,128)} %bitcast.23), calls=%async_computation | async-start | bytes 2621440 | tf_op jit(solution)/shard_map/all_to_all | solution.py:492
  15.0 0.2 select_reduce_fusion.2
  15.2 0.6 collective-permute-start.3
  15.8 4.1 %collective-permute-start.2 = (f32[7,32]{1,0:T(8,128)S(1)}, f32[7,32]{1,0:T(8,128)S(1)}, u32[]{:S(2)}, u32[]{:S(2)}) collective-permute-start(f32[7,32]{1,0:T(8,128)S(1)} %get-tuple-element.22), channel_id=1, source_target_pairs={{32,64},{64,32},{33,65},{65,33},{34,66},{66,34},{35,67},{67,35},{3... | collective-permute-start | bytes 2696 | tf_op jit(solution)/shard_map/ppermute | solution.py:445
  19.9 0.1 collective-permute-start.1
  20.0 5.8 %collective-permute-start = (f32[7,16,128]{2,1,0:T(8,128)S(1)}, f32[7,16,128]{2,1,0:T(8,128)S(1)}, u32[]{:S(2)}, u32[]{:S(2)}) collective-permute-start(f32[7,16,128]{2,1,0:T(8,128)S(1)} %get-tuple-element.30), channel_id=1, source_target_pairs={{1,2},{3,4},{5,6},{7,8},{9,10},{11,12},{13,14},{15,16},{17,18},{19... | collective-permute-start | bytes 172040 | tf_op jit(solution)/shard_map/ppermute | solution.py:445
  25.8 2.9 %collective-permute-done.3 = f32[7,32]{1,0:T(8,128)S(1)} collective-permute-done((f32[7,32]{1,0:T(8,128)S(1)}, f32[7,32]{1,0:T(8,128)S(1)}, u32[]{:S(2)}, u32[]{:S(2)}) %collective-permute-start.3) | collective-permute-done | bytes 928 | tf_op jit(solution)/shard_map/ppermute | solution.py:445
  28.6 0.0 collective-permute-done.2
  28.6 0.1 copy.86.high_z
  28.8 0.1 copy.85.low_z
  28.9 0.0 collective-permute-done.1
  28.9 5.1 %collective-permute-done = f32[7,16,128]{2,1,0:T(8,128)S(1)} collective-permute-done((f32[7,16,128]{2,1,0:T(8,128)S(1)}, f32[7,16,128]{2,1,0:T(8,128)S(1)}, u32[]{:S(2)}, u32[]{:S(2)}) %collective-permute-start) | collective-permute-done | bytes 57376 | tf_op jit(solution)/shard_map/ppermute | solution.py:445
  34.0 24.8 %shard_map.113 = (f32[2048,128]{1,0:T(8,128)}, f32[7,32,128]{2,1,0:T(8,128)S(1)}, f32[112,256]{1,0:T(8,128)S(1)}, f32[48,8,8,128]{3,2,1,0:T(8,128)S(1)}) custom-call(f32[3]{0:T(128)S(1)} %copy-done.2, f32[3]{0:T(128)S(1)} %copy-done.3, f32[7]{0:T(128)S(1)} %copy-done, f32[2560,128]{1,0:T(8,128)S(1)} %bitcast.18, f32[7,32,128]{2,1,0:T(8,128)S(1)} %bitcast.22, ...), custom_call_target="tpu_custom_call" | custom-call | tf_op jit(solution)/shard_map/pallas_call | solution.py:461
  58.8 0.6 copy-done.4
  59.5 0.2 select_reduce_fusion
  59.7 7.9 %all-to-all-start.1 = ((f32[512,4,128]{2,1,0:T(4,128)}), f32[512,4,128]{2,1,0:T(4,128)S(1)}, u32[]{:S(2)}, u32[]{:S(2)}) async-start(f32[512,4,128]{2,1,0:T(4,128)} %bitcast.11), calls=%async_computation.1 | async-start | bytes 2097152 | tf_op jit(solution)/shard_map/all_to_all | solution.py:492
  67.7 0.6 collective-permute-start.7
  68.2 4.2 %collective-permute-start.6 = (f32[7,32]{1,0:T(8,128)S(1)}, f32[7,32]{1,0:T(8,128)S(1)}, u32[]{:S(2)}, u32[]{:S(2)}) collective-permute-start(f32[7,32]{1,0:T(8,128)S(1)} %get-tuple-element.20), channel_id=1, source_target_pairs={{32,64},{64,32},{33,65},{65,33},{34,66},{66,34},{35,67},{67,35},{3... | collective-permute-start | bytes 2696 | tf_op jit(solution)/shard_map/ppermute | solution.py:445
  72.4 0.1 collective-permute-start.5
  72.5 5.8 %collective-permute-start.4 = (f32[7,16,128]{2,1,0:T(8,128)S(1)}, f32[7,16,128]{2,1,0:T(8,128)S(1)}, u32[]{:S(2)}, u32[]{:S(2)}) collective-permute-start(f32[7,16,128]{2,1,0:T(8,128)S(1)} %get-tuple-element.26), channel_id=1, source_target_pairs={{1,2},{3,4},{5,6},{7,8},{9,10},{11,12},{13,14},{15,16},{17,18},{19... | collective-permute-start | bytes 172040 | tf_op jit(solution)/shard_map/ppermute | solution.py:445
  78.3 0.0 copy-start.1
  78.3 8.8 %shard_map.114.acc = f32[112,256]{1,0:T(8,128)S(1)} custom-call(f32[48,8,8,128]{3,2,1,0:T(8,128)S(1)} %get-tuple-element.13.kept, f32[112,256]{1,0:T(8,128)S(1)} %copy-done.5), custom_call_target="tpu_custom_call" | custom-call | flops 8000000000 | bytes 1048576 | tf_op jit(solution)/shard_map/pallas_call | solution.py:481
  87.1 0.1 copy.88.high_z
  87.3 0.1 copy.87.low_z
  87.4 0.0 collective-permute-done.5
  87.4 1.4 %shard_map.115 = f32[2,7,16,128]{3,2,1,0:T(8,128)} custom-call(f32[7]{0:T(128)S(1)} %copy-done, f32[7,32,128]{2,1,0:T(8,128)S(1)} %get-tuple-element.12.melt, f32[112,256]{1,0:T(8,128)S(1)} %shard_map.114.acc, f32[7,16,128]{2,1,0:T(8,128)S(1)} %get-tuple-element.24.low_x, f32[7,16,128]{2,1,0:T(8,128)S(1)} %get-tuple-element.23.high_x, ...), custom_call_target="tpu_custom_call" | custom-call | tf_op jit(solution)/shard_map/pallas_call | solution.py:526
  88.8 1.9 %shard_map.116 = (f32[3,256,128]{2,1,0:T(8,128)}, f32[256,128]{1,0:T(8,128)}) custom-call(s32[256]{0:T(256)S(1)} %copy-done.1, f32[2048,128]{1,0:T(8,128)S(1)} %bitcast.19), custom_call_target="tpu_custom_call" | custom-call | tf_op jit(solution)/shard_map/pallas_call | solution.py:533
  (20 shorter events, 0.1 us)
Async XLA Ops:
  4.5 10.4 %copy-start.6 = (f32[2,16,7,128]{3,1,2,0:T(8,128)S(1)}, f32[2,16,7,128]{3,1,2,0:T(8,128)}, u32[]{:S(2)}) copy-start(f32[2,16,7,128]{3,1,2,0:T(8,128)} %param.9) | copy-start | bytes 344068
  4.5 29.5 %copy-start = (f32[7]{0:T(128)S(1)}, f32[7]{0:T(128)}, u32[]{:S(2)}) copy-start(f32[7]{0:T(128)} %rate.3) | copy-start | bytes 88
  4.5 29.5 %copy-start.2 = (f32[3]{0:T(128)S(1)}, f32[3]{0:T(128)}, u32[]{:S(2)}) copy-start(f32[3]{0:T(128)} %slope.1) | copy-start | bytes 40
  4.5 29.5 %copy-start.3 = (f32[3]{0:T(128)S(1)}, f32[3]{0:T(128)}, u32[]{:S(2)}) copy-start(f32[3]{0:T(128)} %partition.1) | copy-start | bytes 40
  4.5 29.5 %all-to-all-start = ((f32[640,4,128]{2,1,0:T(4,128)}), f32[640,4,128]{2,1,0:T(4,128)S(1)}, u32[]{:S(2)}, u32[]{:S(2)}) async-start(f32[640,4,128]{2,1,0:T(4,128)} %bitcast.23), calls=%async_computation | async-start | bytes 2621440 | tf_op jit(solution)/shard_map/all_to_all | solution.py:492
  15.2 13.5 %collective-permute-start.3 = (f32[7,32]{1,0:T(8,128)S(1)}, f32[7,32]{1,0:T(8,128)S(1)}, u32[]{:S(2)}, u32[]{:S(2)}) collective-permute-start(f32[7,32]{1,0:T(8,128)S(1)} %get-tuple-element.21), channel_id=1, source_target_pairs={{0,32},{64,96},{32,0},{96,64},{1,33},{65,97},{33,1},{97,65},{2,34}... | collective-permute-start | bytes 2696 | tf_op jit(solution)/shard_map/ppermute | solution.py:445
  15.8 12.8 %collective-permute-start.2 = (f32[7,32]{1,0:T(8,128)S(1)}, f32[7,32]{1,0:T(8,128)S(1)}, u32[]{:S(2)}, u32[]{:S(2)}) collective-permute-start(f32[7,32]{1,0:T(8,128)S(1)} %get-tuple-element.22), channel_id=1, source_target_pairs={{32,64},{64,32},{33,65},{65,33},{34,66},{66,34},{35,67},{67,35},{3... | collective-permute-start | bytes 2696 | tf_op jit(solution)/shard_map/ppermute | solution.py:445
  19.9 9.0 %collective-permute-start.1 = (f32[7,16,128]{2,1,0:T(8,128)S(1)}, f32[7,16,128]{2,1,0:T(8,128)S(1)}, u32[]{:S(2)}, u32[]{:S(2)}) collective-permute-start(f32[7,16,128]{2,1,0:T(8,128)S(1)} %get-tuple-element.29), channel_id=1, source_target_pairs={{0,1},{2,3},{4,5},{6,7},{8,9},{10,11},{12,13},{14,15},{16,17},{18,... | collective-permute-start | bytes 172040 | tf_op jit(solution)/shard_map/ppermute | solution.py:445
  20.0 14.0 %collective-permute-start = (f32[7,16,128]{2,1,0:T(8,128)S(1)}, f32[7,16,128]{2,1,0:T(8,128)S(1)}, u32[]{:S(2)}, u32[]{:S(2)}) collective-permute-start(f32[7,16,128]{2,1,0:T(8,128)S(1)} %get-tuple-element.30), channel_id=1, source_target_pairs={{1,2},{3,4},{5,6},{7,8},{9,10},{11,12},{13,14},{15,16},{17,18},{19... | collective-permute-start | bytes 172040 | tf_op jit(solution)/shard_map/ppermute | solution.py:445
  58.8 0.6 copy-start.4
  59.5 18.8 %copy-start.5 = (f32[112,256]{1,0:T(8,128)S(1)}, f32[112,256]{1,0:T(8,128)}, u32[]{:S(2)}) copy-start(f32[112,256]{1,0:T(8,128)} %copy-done.4) | copy-start | bytes 344068
  59.7 29.1 %all-to-all-start.1 = ((f32[512,4,128]{2,1,0:T(4,128)}), f32[512,4,128]{2,1,0:T(4,128)S(1)}, u32[]{:S(2)}, u32[]{:S(2)}) async-start(f32[512,4,128]{2,1,0:T(4,128)} %bitcast.11), calls=%async_computation.1 | async-start | bytes 2097152 | tf_op jit(solution)/shard_map/all_to_all | solution.py:492
  67.7 19.5 %collective-permute-start.7 = (f32[7,32]{1,0:T(8,128)S(1)}, f32[7,32]{1,0:T(8,128)S(1)}, u32[]{:S(2)}, u32[]{:S(2)}) collective-permute-start(f32[7,32]{1,0:T(8,128)S(1)} %get-tuple-element.19), channel_id=1, source_target_pairs={{0,32},{64,96},{32,0},{96,64},{1,33},{65,97},{33,1},{97,65},{2,34}... | collective-permute-start | bytes 2696 | tf_op jit(solution)/shard_map/ppermute | solution.py:445
  68.2 18.9 %collective-permute-start.6 = (f32[7,32]{1,0:T(8,128)S(1)}, f32[7,32]{1,0:T(8,128)S(1)}, u32[]{:S(2)}, u32[]{:S(2)}) collective-permute-start(f32[7,32]{1,0:T(8,128)S(1)} %get-tuple-element.20), channel_id=1, source_target_pairs={{32,64},{64,32},{33,65},{65,33},{34,66},{66,34},{35,67},{67,35},{3... | collective-permute-start | bytes 2696 | tf_op jit(solution)/shard_map/ppermute | solution.py:445
  72.4 15.0 %collective-permute-start.5 = (f32[7,16,128]{2,1,0:T(8,128)S(1)}, f32[7,16,128]{2,1,0:T(8,128)S(1)}, u32[]{:S(2)}, u32[]{:S(2)}) collective-permute-start(f32[7,16,128]{2,1,0:T(8,128)S(1)} %get-tuple-element.25), channel_id=1, source_target_pairs={{0,1},{2,3},{4,5},{6,7},{8,9},{10,11},{12,13},{14,15},{16,17},{18,... | collective-permute-start | bytes 172040 | tf_op jit(solution)/shard_map/ppermute | solution.py:445
  72.5 14.9 %collective-permute-start.4 = (f32[7,16,128]{2,1,0:T(8,128)S(1)}, f32[7,16,128]{2,1,0:T(8,128)S(1)}, u32[]{:S(2)}, u32[]{:S(2)}) collective-permute-start(f32[7,16,128]{2,1,0:T(8,128)S(1)} %get-tuple-element.26), channel_id=1, source_target_pairs={{1,2},{3,4},{5,6},{7,8},{9,10},{11,12},{13,14},{15,16},{17,18},{19... | collective-permute-start | bytes 172040 | tf_op jit(solution)/shard_map/ppermute | solution.py:445
  78.3 10.5 %copy-start.1 = (s32[256]{0:T(256)S(1)}, s32[256]{0:T(256)}, u32[]{:S(2)}) copy-start(s32[256]{0:T(256)} %get-tuple-element.15.slot_of) | copy-start | bytes 3076

commit v7 on v6

--- a/solution.py
+++ b/solution.py
@@ -464,7 +464,7 @@
             shape(slots * BACK, LANES),
             shape(comps, columns, size_z),
             sums,
-            shape(slots // GROUP * 3 // 4, comps + 1, GROUP, LANES),
+            shape(slots // GROUP * 5 // 8, comps + 1, GROUP, LANES),
         ),
         [SMEM, SMEM, SMEM] + [VMEM] * 6,
         (VMEM, VMEM, VMEM, VMEM),

time: 91.1 us -> 90.5 us (level)
    pallas_call x1, Pallas kernels: 8.81 us -> 7.36 us  [run_kept(): kernel_call(functools.partial(kept_kernel, dims), shape(*before.shape), [...]
  transfers between devices with their start and end apart: 10 -> 10, of which waited for: 2 -> 2; matrix products, arithmetic and copies ran while one was open for 1% -> 1% of each run, Pallas kernels for 11% -> 10%
where the time goes in v7:
time: 90.5 us; the launch traced here: 89.3 us
  Pallas kernels  40 us (44%)
  starting transfers between devices  39.4 us (44%)
  waiting for transfers between devices  7.96 us (9%)
    pallas_call x1, Pallas kernels, run_steps(): kernel_call(steps_kernel, (shape(slots * BACK, LANES), shape(comps, colum...  25.5 us
    ppermute x8, starting transfers between devices, meet(): return lax.ppermute(face, axis, pairs + [(j, i) for i, j in pairs])  21.1 us
    all_to_all x2, starting transfers between devices, exchange(): lax.all_to_all(rows.reshape(each, CAP, LANES), AXES, split_axis=0, concat...  18.3 us
    ppermute x8, waiting for transfers between devices, meet(): return lax.ppermute(face, axis, pairs + [(j, i) for i, j in pairs])  7.96 us
    pallas_call x1, Pallas kernels, run_kept(): kernel_call(functools.partial(kept_kernel, dims), shape(*before.shape), [...  7.36 us
    pallas_call x1, Pallas kernels, local(): kernel_call(pack_kernel, (shape(slots * SEND, LANES), jax.ShapeDtypeStruc...  3.82 us
    pallas_call x1, Pallas kernels, local(): kernel_call(unpack_kernel, (shape(3, blocks, LANES), shape(blocks, LANES)...  1.93 us
  transfers between devices with their start and end apart: 10, of which 2 were waited for; matrix products, arithmetic and copies ran while one was open for 1% of the time, Pallas kernels for 10%

profile of v7, /device:TPU:14, one launch (start us, length us, event | category | flops | bytes accessed | tf_op | source)
XLA Modules:
  0.0 89.3 jit_solution(13130727541427466133)
XLA Ops:
  0.6 3.8 %shard_map.112 = (f32[2560,128]{1,0:T(8,128)}, s32[256]{0:T(256)}) custom-call(s32[256]{0:T(256)} %target_hbm.1, s32[256]{0:T(256)} %count_hbm.1, f32[3,256,128]{2,1,0:T(8,128)} %bitcast.24, f32[256,128]{1,0:T(8,128)} %radi_hbm.1, s32[256,128]{1,0:T(8,128)} %cell_hbm.1), custom_call_target="tpu_custom_call" | custom-call | tf_op jit(solution)/shard_map/pallas_call | solution.py:503
  4.5 0.0 copy-start.4
  4.5 0.0 copy-start
  4.5 0.0 copy-start.2
  4.5 0.0 copy-start.3
  4.5 10.4 %all-to-all-start = ((f32[640,4,128]{2,1,0:T(4,128)}), f32[640,4,128]{2,1,0:T(4,128)S(1)}, u32[]{:S(2)}, u32[]{:S(2)}) async-start(f32[640,4,128]{2,1,0:T(4,128)} %bitcast.23), calls=%async_computation | async-start | bytes 2621440 | tf_op jit(solution)/shard_map/all_to_all | solution.py:492
  14.9 0.2 select_reduce_fusion.2
  15.2 0.6 collective-permute-start.3
  15.8 4.1 %collective-permute-start.2 = (f32[7,32]{1,0:T(8,128)S(1)}, f32[7,32]{1,0:T(8,128)S(1)}, u32[]{:S(2)}, u32[]{:S(2)}) collective-permute-start(f32[7,32]{1,0:T(8,128)S(1)} %get-tuple-element.22), channel_id=1, source_target_pairs={{32,64},{64,32},{33,65},{65,33},{34,66},{66,34},{35,67},{67,35},{3... | collective-permute-start | bytes 2696 | tf_op jit(solution)/shard_map/ppermute | solution.py:445
  19.9 0.1 collective-permute-start.1
  20.0 5.8 %collective-permute-start = (f32[7,16,128]{2,1,0:T(8,128)S(1)}, f32[7,16,128]{2,1,0:T(8,128)S(1)}, u32[]{:S(2)}, u32[]{:S(2)}) collective-permute-start(f32[7,16,128]{2,1,0:T(8,128)S(1)} %get-tuple-element.30), channel_id=1, source_target_pairs={{1,2},{3,4},{5,6},{7,8},{9,10},{11,12},{13,14},{15,16},{17,18},{19... | collective-permute-start | bytes 172040 | tf_op jit(solution)/shard_map/ppermute | solution.py:445
  25.8 2.9 %collective-permute-done.3 = f32[7,32]{1,0:T(8,128)S(1)} collective-permute-done((f32[7,32]{1,0:T(8,128)S(1)}, f32[7,32]{1,0:T(8,128)S(1)}, u32[]{:S(2)}, u32[]{:S(2)}) %collective-permute-start.3) | collective-permute-done | bytes 928 | tf_op jit(solution)/shard_map/ppermute | solution.py:445
  28.6 0.0 collective-permute-done.2
  28.6 0.1 copy.86.high_z
  28.7 0.1 copy.85.low_z
  28.9 0.0 collective-permute-done.1
  28.9 5.1 %collective-permute-done = f32[7,16,128]{2,1,0:T(8,128)S(1)} collective-permute-done((f32[7,16,128]{2,1,0:T(8,128)S(1)}, f32[7,16,128]{2,1,0:T(8,128)S(1)}, u32[]{:S(2)}, u32[]{:S(2)}) %collective-permute-start) | collective-permute-done | bytes 57376 | tf_op jit(solution)/shard_map/ppermute | solution.py:445
  34.0 25.5 %shard_map.113 = (f32[2048,128]{1,0:T(8,128)}, f32[7,32,128]{2,1,0:T(8,128)S(1)}, f32[112,256]{1,0:T(8,128)S(1)}, f32[40,8,8,128]{3,2,1,0:T(8,128)S(1)}) custom-call(f32[3]{0:T(128)S(1)} %copy-done.2, f32[3]{0:T(128)S(1)} %copy-done.3, f32[7]{0:T(128)S(1)} %copy-done, f32[2560,128]{1,0:T(8,128)S(1)} %bitcast.18, f32[7,32,128]{2,1,0:T(8,128)S(1)} %bitcast.22, ...), custom_call_target="tpu_custom_call" | custom-call | tf_op jit(solution)/shard_map/pallas_call | solution.py:461
  59.5 0.2 select_reduce_fusion
  59.8 7.9 %all-to-all-start.1 = ((f32[512,4,128]{2,1,0:T(4,128)}), f32[512,4,128]{2,1,0:T(4,128)S(1)}, u32[]{:S(2)}, u32[]{:S(2)}) async-start(f32[512,4,128]{2,1,0:T(4,128)} %bitcast.11), calls=%async_computation.1 | async-start | bytes 2097152 | tf_op jit(solution)/shard_map/all_to_all | solution.py:492
  67.7 0.6 collective-permute-start.7
  68.3 4.2 %collective-permute-start.6 = (f32[7,32]{1,0:T(8,128)S(1)}, f32[7,32]{1,0:T(8,128)S(1)}, u32[]{:S(2)}, u32[]{:S(2)}) collective-permute-start(f32[7,32]{1,0:T(8,128)S(1)} %get-tuple-element.20), channel_id=1, source_target_pairs={{32,64},{64,32},{33,65},{65,33},{34,66},{66,34},{35,67},{67,35},{3... | collective-permute-start | bytes 2696 | tf_op jit(solution)/shard_map/ppermute | solution.py:445
  72.5 0.1 collective-permute-start.5
  72.6 5.8 %collective-permute-start.4 = (f32[7,16,128]{2,1,0:T(8,128)S(1)}, f32[7,16,128]{2,1,0:T(8,128)S(1)}, u32[]{:S(2)}, u32[]{:S(2)}) collective-permute-start(f32[7,16,128]{2,1,0:T(8,128)S(1)} %get-tuple-element.26), channel_id=1, source_target_pairs={{1,2},{3,4},{5,6},{7,8},{9,10},{11,12},{13,14},{15,16},{17,18},{19... | collective-permute-start | bytes 172040 | tf_op jit(solution)/shard_map/ppermute | solution.py:445
  78.3 0.0 copy-start.1
  78.3 7.4 %shard_map.114.acc = f32[112,256]{1,0:T(8,128)S(1)} custom-call(f32[40,8,8,128]{3,2,1,0:T(8,128)S(1)} %get-tuple-element.13.kept, f32[112,256]{1,0:T(8,128)S(1)} %get-tuple-element.14.before), custom_call_target="tpu_custom_call" | custom-call | flops 8000000000 | bytes 1048576 | tf_op jit(solution)/shard_map/pallas_call | solution.py:481
  85.7 0.0 collective-permute-done.6
  85.7 0.1 copy.88.high_z
  85.9 0.1 copy.87.low_z
  86.0 0.0 collective-permute-done.5
  86.0 1.4 %shard_map.115 = f32[2,7,16,128]{3,2,1,0:T(8,128)} custom-call(f32[7]{0:T(128)S(1)} %copy-done, f32[7,32,128]{2,1,0:T(8,128)S(1)} %get-tuple-element.12.melt, f32[112,256]{1,0:T(8,128)S(1)} %shard_map.114.acc, f32[7,16,128]{2,1,0:T(8,128)S(1)} %get-tuple-element.24.low_x, f32[7,16,128]{2,1,0:T(8,128)S(1)} %get-tuple-element.23.high_x, ...), custom_call_target="tpu_custom_call" | custom-call | tf_op jit(solution)/shard_map/pallas_call | solution.py:526
  87.4 1.9 %shard_map.116 = (f32[3,256,128]{2,1,0:T(8,128)}, f32[256,128]{1,0:T(8,128)}) custom-call(s32[256]{0:T(256)S(1)} %copy-done.1, f32[2048,128]{1,0:T(8,128)S(1)} %bitcast.19), custom_call_target="tpu_custom_call" | custom-call | tf_op jit(solution)/shard_map/pallas_call | solution.py:533
  (16 shorter events, 0.1 us)
Async XLA Ops:
  4.5 10.4 %copy-start.4 = (f32[2,16,7,128]{3,1,2,0:T(8,128)S(1)}, f32[2,16,7,128]{3,1,2,0:T(8,128)}, u32[]{:S(2)}) copy-start(f32[2,16,7,128]{3,1,2,0:T(8,128)} %param.9) | copy-start | bytes 344068
  4.5 29.5 %copy-start = (f32[7]{0:T(128)S(1)}, f32[7]{0:T(128)}, u32[]{:S(2)}) copy-start(f32[7]{0:T(128)} %rate.3) | copy-start | bytes 88
  4.5 29.5 %copy-start.2 = (f32[3]{0:T(128)S(1)}, f32[3]{0:T(128)}, u32[]{:S(2)}) copy-start(f32[3]{0:T(128)} %slope.1) | copy-start | bytes 40
  4.5 29.5 %copy-start.3 = (f32[3]{0:T(128)S(1)}, f32[3]{0:T(128)}, u32[]{:S(2)}) copy-start(f32[3]{0:T(128)} %partition.1) | copy-start | bytes 40
  4.5 29.5 %all-to-all-start = ((f32[640,4,128]{2,1,0:T(4,128)}), f32[640,4,128]{2,1,0:T(4,128)S(1)}, u32[]{:S(2)}, u32[]{:S(2)}) async-start(f32[640,4,128]{2,1,0:T(4,128)} %bitcast.23), calls=%async_computation | async-start | bytes 2621440 | tf_op jit(solution)/shard_map/all_to_all | solution.py:492
  15.2 13.5 %collective-permute-start.3 = (f32[7,32]{1,0:T(8,128)S(1)}, f32[7,32]{1,0:T(8,128)S(1)}, u32[]{:S(2)}, u32[]{:S(2)}) collective-permute-start(f32[7,32]{1,0:T(8,128)S(1)} %get-tuple-element.21), channel_id=1, source_target_pairs={{0,32},{64,96},{32,0},{96,64},{1,33},{65,97},{33,1},{97,65},{2,34}... | collective-permute-start | bytes 2696 | tf_op jit(solution)/shard_map/ppermute | solution.py:445
  15.8 12.8 %collective-permute-start.2 = (f32[7,32]{1,0:T(8,128)S(1)}, f32[7,32]{1,0:T(8,128)S(1)}, u32[]{:S(2)}, u32[]{:S(2)}) collective-permute-start(f32[7,32]{1,0:T(8,128)S(1)} %get-tuple-element.22), channel_id=1, source_target_pairs={{32,64},{64,32},{33,65},{65,33},{34,66},{66,34},{35,67},{67,35},{3... | collective-permute-start | bytes 2696 | tf_op jit(solution)/shard_map/ppermute | solution.py:445
  19.9 9.0 %collective-permute-start.1 = (f32[7,16,128]{2,1,0:T(8,128)S(1)}, f32[7,16,128]{2,1,0:T(8,128)S(1)}, u32[]{:S(2)}, u32[]{:S(2)}) collective-permute-start(f32[7,16,128]{2,1,0:T(8,128)S(1)} %get-tuple-element.29), channel_id=1, source_target_pairs={{0,1},{2,3},{4,5},{6,7},{8,9},{10,11},{12,13},{14,15},{16,17},{18,... | collective-permute-start | bytes 172040 | tf_op jit(solution)/shard_map/ppermute | solution.py:445
  20.0 14.0 %collective-permute-start = (f32[7,16,128]{2,1,0:T(8,128)S(1)}, f32[7,16,128]{2,1,0:T(8,128)S(1)}, u32[]{:S(2)}, u32[]{:S(2)}) collective-permute-start(f32[7,16,128]{2,1,0:T(8,128)S(1)} %get-tuple-element.30), channel_id=1, source_target_pairs={{1,2},{3,4},{5,6},{7,8},{9,10},{11,12},{13,14},{15,16},{17,18},{19... | collective-permute-start | bytes 172040 | tf_op jit(solution)/shard_map/ppermute | solution.py:445
  59.8 27.6 %all-to-all-start.1 = ((f32[512,4,128]{2,1,0:T(4,128)}), f32[512,4,128]{2,1,0:T(4,128)S(1)}, u32[]{:S(2)}, u32[]{:S(2)}) async-start(f32[512,4,128]{2,1,0:T(4,128)} %bitcast.11), calls=%async_computation.1 | async-start | bytes 2097152 | tf_op jit(solution)/shard_map/all_to_all | solution.py:492
  67.7 18.0 %collective-permute-start.7 = (f32[7,32]{1,0:T(8,128)S(1)}, f32[7,32]{1,0:T(8,128)S(1)}, u32[]{:S(2)}, u32[]{:S(2)}) collective-permute-start(f32[7,32]{1,0:T(8,128)S(1)} %get-tuple-element.19), channel_id=1, source_target_pairs={{0,32},{64,96},{32,0},{96,64},{1,33},{65,97},{33,1},{97,65},{2,34}... | collective-permute-start | bytes 2696 | tf_op jit(solution)/shard_map/ppermute | solution.py:445
  68.3 17.4 %collective-permute-start.6 = (f32[7,32]{1,0:T(8,128)S(1)}, f32[7,32]{1,0:T(8,128)S(1)}, u32[]{:S(2)}, u32[]{:S(2)}) collective-permute-start(f32[7,32]{1,0:T(8,128)S(1)} %get-tuple-element.20), channel_id=1, source_target_pairs={{32,64},{64,32},{33,65},{65,33},{34,66},{66,34},{35,67},{67,35},{3... | collective-permute-start | bytes 2696 | tf_op jit(solution)/shard_map/ppermute | solution.py:445
  72.5 13.5 %collective-permute-start.5 = (f32[7,16,128]{2,1,0:T(8,128)S(1)}, f32[7,16,128]{2,1,0:T(8,128)S(1)}, u32[]{:S(2)}, u32[]{:S(2)}) collective-permute-start(f32[7,16,128]{2,1,0:T(8,128)S(1)} %get-tuple-element.25), channel_id=1, source_target_pairs={{0,1},{2,3},{4,5},{6,7},{8,9},{10,11},{12,13},{14,15},{16,17},{18,... | collective-permute-start | bytes 172040 | tf_op jit(solution)/shard_map/ppermute | solution.py:445
  72.6 13.4 %collective-permute-start.4 = (f32[7,16,128]{2,1,0:T(8,128)S(1)}, f32[7,16,128]{2,1,0:T(8,128)S(1)}, u32[]{:S(2)}, u32[]{:S(2)}) collective-permute-start(f32[7,16,128]{2,1,0:T(8,128)S(1)} %get-tuple-element.26), channel_id=1, source_target_pairs={{1,2},{3,4},{5,6},{7,8},{9,10},{11,12},{13,14},{15,16},{17,18},{19... | collective-permute-start | bytes 172040 | tf_op jit(solution)/shard_map/ppermute | solution.py:445
  78.3 9.1 %copy-start.1 = (s32[256]{0:T(256)S(1)}, s32[256]{0:T(256)}, u32[]{:S(2)}) copy-start(s32[256]{0:T(256)} %get-tuple-element.15.slot_of) | copy-start | bytes 3076

commit v8 on v7

--- a/solution.py
+++ b/solution.py
@@ -83,7 +83,7 @@
 
 def unpack_kernel(slot_of, back, velo_hbm, radi_hbm, velo, radi, done):
     blocks = radi.shape[0]
-    half = blocks // 2
+    share = blocks // 4
 
     def place(k, _):
         row = slot_of[k] * BACK
@@ -93,9 +93,9 @@
         return 0
 
     copies = []
-    for part in range(2):
-        lax.fori_loop(part * half, (part + 1) * half, place, 0, unroll=8)
-        own = pl.ds(part * half, half)
+    for part in range(4):
+        lax.fori_loop(part * share, (part + 1) * share, place, 0, unroll=8)
+        own = pl.ds(part * share, share)
         copies += [
             pltpu.make_async_copy(velo.at[:, own], velo_hbm.at[:, own], done.at[2 * part]),
             pltpu.make_async_copy(radi.at[own], radi_hbm.at[own], done.at[2 * part + 1]),
@@ -200,6 +200,24 @@
         )
 
 
+def row_sums(parts):
+    row = lax.broadcasted_iota(jnp.int32, parts[0].shape, 0)
+    width = len(parts) // 2
+    while width:
+        lower = row % (2 * width) < width
+        parts = [
+            jnp.where(lower, first, second)
+            + jnp.where(
+                lower,
+                pltpu.roll(first, GROUP - width, 0),
+                pltpu.roll(second, width, 0),
+            )
+            for first, second in zip(parts[:width], parts[width:])
+        ]
+        width //= 2
+    return parts[0]
+
+
 def matrix_probe(cell, lines, dims, sums):
     size_x, size_y, size_z = dims
     row_iota = lax.broadcasted_iota(jnp.int32, (size_x * size_z, LANES), 0)
@@ -228,8 +246,9 @@
             mask = y_iota == y[b : b + 1, :]
             for c in range(COMPS):
                 part = lifted[c * size_y : (c + 1) * size_y, i * LANES : (i + 1) * LANES]
-                found[c].append(jnp.sum(jnp.where(mask, part, 0.0), axis=0, keepdims=True))
-    return [jnp.concatenate(rows, axis=0) for rows in found]
+                part = jnp.where(mask, part, 0.0)
+                found[c].append(sum(part[r : r + GROUP] for r in range(0, size_y, GROUP)))
+    return [row_sums(parts) for parts in found]
 
 
 def coupling_step(slope, partition, dims, refs, load_cell, load, store, span, sums, kept=None):
@@ -538,7 +557,7 @@
         [
             pltpu.VMEM((3, blocks, LANES), jnp.float32),
             pltpu.VMEM((blocks, LANES), jnp.float32),
-            pltpu.SemaphoreType.DMA((4,)),
+            pltpu.SemaphoreType.DMA((8,)),
         ],
     )(slot_of, returned)
     return melt_out, jnp.transpose(velocity_out, (1, 0, 2)), radius_out

time: 90.5 us -> 90.2 us (level)
  no operation moved by 1% of the time
where the time goes in v8:
time: 90.2 us; the launch traced here: 89 us
  Pallas kernels  39.7 us (44%)
  starting transfers between devices  39.4 us (44%)
  waiting for transfers between devices  7.96 us (9%)
    pallas_call x1, Pallas kernels, run_steps(): kernel_call(steps_kernel, (shape(slots * BACK, LANES), shape(comps, colum...  25.2 us
    ppermute x8, starting transfers between devices, meet(): return lax.ppermute(face, axis, pairs + [(j, i) for i, j in pairs])  21.1 us
    all_to_all x2, starting transfers between devices, exchange(): lax.all_to_all(rows.reshape(each, CAP, LANES), AXES, split_axis=0, concat...  18.3 us
    ppermute x8, waiting for transfers between devices, meet(): return lax.ppermute(face, axis, pairs + [(j, i) for i, j in pairs])  7.96 us
    pallas_call x1, Pallas kernels, run_kept(): kernel_call(functools.partial(kept_kernel, dims), shape(*before.shape), [...  7.36 us
    pallas_call x1, Pallas kernels, local(): kernel_call(pack_kernel, (shape(slots * SEND, LANES), jax.ShapeDtypeStruc...  3.82 us
    pallas_call x1, Pallas kernels, local(): kernel_call(unpack_kernel, (shape(3, blocks, LANES), shape(blocks, LANES)...  1.92 us
  transfers between devices with their start and end apart: 10, of which 2 were waited for; matrix products, arithmetic and copies ran while one was open for 1% of the time, Pallas kernels for 10%

profile of v8, /device:TPU:14, one launch (start us, length us, event | category | flops | bytes accessed | tf_op | source)
XLA Modules:
  0.0 89.0 jit_solution(10361085147843502122)
XLA Ops:
  0.6 3.8 %shard_map.112 = (f32[2560,128]{1,0:T(8,128)}, s32[256]{0:T(256)}) custom-call(s32[256]{0:T(256)} %target_hbm.1, s32[256]{0:T(256)} %count_hbm.1, f32[3,256,128]{2,1,0:T(8,128)} %bitcast.24, f32[256,128]{1,0:T(8,128)} %radi_hbm.1, s32[256,128]{1,0:T(8,128)} %cell_hbm.1), custom_call_target="tpu_custom_call" | custom-call | tf_op jit(solution)/shard_map/pallas_call | solution.py:522
  4.5 0.0 copy-start.4
  4.5 0.0 copy-start
  4.5 0.0 copy-start.2
  4.5 0.0 copy-start.3
  4.5 10.4 %all-to-all-start = ((f32[640,4,128]{2,1,0:T(4,128)}), f32[640,4,128]{2,1,0:T(4,128)S(1)}, u32[]{:S(2)}, u32[]{:S(2)}) async-start(f32[640,4,128]{2,1,0:T(4,128)} %bitcast.23), calls=%async_computation | async-start | bytes 2621440 | tf_op jit(solution)/shard_map/all_to_all | solution.py:511
  14.9 0.2 select_reduce_fusion.2
  15.2 0.6 collective-permute-start.3
  15.8 4.1 %collective-permute-start.2 = (f32[7,32]{1,0:T(8,128)S(1)}, f32[7,32]{1,0:T(8,128)S(1)}, u32[]{:S(2)}, u32[]{:S(2)}) collective-permute-start(f32[7,32]{1,0:T(8,128)S(1)} %get-tuple-element.22), channel_id=1, source_target_pairs={{32,64},{64,32},{33,65},{65,33},{34,66},{66,34},{35,67},{67,35},{3... | collective-permute-start | bytes 2696 | tf_op jit(solution)/shard_map/ppermute | solution.py:464
  19.9 0.1 collective-permute-start.1
  20.0 5.8 %collective-permute-start = (f32[7,16,128]{2,1,0:T(8,128)S(1)}, f32[7,16,128]{2,1,0:T(8,128)S(1)}, u32[]{:S(2)}, u32[]{:S(2)}) collective-permute-start(f32[7,16,128]{2,1,0:T(8,128)S(1)} %get-tuple-element.30), channel_id=1, source_target_pairs={{1,2},{3,4},{5,6},{7,8},{9,10},{11,12},{13,14},{15,16},{17,18},{19... | collective-permute-start | bytes 172040 | tf_op jit(solution)/shard_map/ppermute | solution.py:464
  25.8 2.9 %collective-permute-done.3 = f32[7,32]{1,0:T(8,128)S(1)} collective-permute-done((f32[7,32]{1,0:T(8,128)S(1)}, f32[7,32]{1,0:T(8,128)S(1)}, u32[]{:S(2)}, u32[]{:S(2)}) %collective-permute-start.3) | collective-permute-done | bytes 928 | tf_op jit(solution)/shard_map/ppermute | solution.py:464
  28.6 0.0 collective-permute-done.2
  28.6 0.1 copy.86.high_z
  28.7 0.1 copy.85.low_z
  28.9 0.0 collective-permute-done.1
  28.9 5.1 %collective-permute-done = f32[7,16,128]{2,1,0:T(8,128)S(1)} collective-permute-done((f32[7,16,128]{2,1,0:T(8,128)S(1)}, f32[7,16,128]{2,1,0:T(8,128)S(1)}, u32[]{:S(2)}, u32[]{:S(2)}) %collective-permute-start) | collective-permute-done | bytes 57376 | tf_op jit(solution)/shard_map/ppermute | solution.py:464
  34.0 25.2 %shard_map.113 = (f32[2048,128]{1,0:T(8,128)}, f32[7,32,128]{2,1,0:T(8,128)S(1)}, f32[112,256]{1,0:T(8,128)S(1)}, f32[40,8,8,128]{3,2,1,0:T(8,128)S(1)}) custom-call(f32[3]{0:T(128)S(1)} %copy-done.2, f32[3]{0:T(128)S(1)} %copy-done.3, f32[7]{0:T(128)S(1)} %copy-done, f32[2560,128]{1,0:T(8,128)S(1)} %bitcast.18, f32[7,32,128]{2,1,0:T(8,128)S(1)} %bitcast.22, ...), custom_call_target="tpu_custom_call" | custom-call | tf_op jit(solution)/shard_map/pallas_call | solution.py:480
  59.2 0.2 select_reduce_fusion
  59.5 7.9 %all-to-all-start.1 = ((f32[512,4,128]{2,1,0:T(4,128)}), f32[512,4,128]{2,1,0:T(4,128)S(1)}, u32[]{:S(2)}, u32[]{:S(2)}) async-start(f32[512,4,128]{2,1,0:T(4,128)} %bitcast.11), calls=%async_computation.1 | async-start | bytes 2097152 | tf_op jit(solution)/shard_map/all_to_all | solution.py:511
  67.4 0.6 collective-permute-start.7
  68.0 4.2 %collective-permute-start.6 = (f32[7,32]{1,0:T(8,128)S(1)}, f32[7,32]{1,0:T(8,128)S(1)}, u32[]{:S(2)}, u32[]{:S(2)}) collective-permute-start(f32[7,32]{1,0:T(8,128)S(1)} %get-tuple-element.20), channel_id=1, source_target_pairs={{32,64},{64,32},{33,65},{65,33},{34,66},{66,34},{35,67},{67,35},{3... | collective-permute-start | bytes 2696 | tf_op jit(solution)/shard_map/ppermute | solution.py:464
  72.2 0.1 collective-permute-start.5
  72.3 5.8 %collective-permute-start.4 = (f32[7,16,128]{2,1,0:T(8,128)S(1)}, f32[7,16,128]{2,1,0:T(8,128)S(1)}, u32[]{:S(2)}, u32[]{:S(2)}) collective-permute-start(f32[7,16,128]{2,1,0:T(8,128)S(1)} %get-tuple-element.26), channel_id=1, source_target_pairs={{1,2},{3,4},{5,6},{7,8},{9,10},{11,12},{13,14},{15,16},{17,18},{19... | collective-permute-start | bytes 172040 | tf_op jit(solution)/shard_map/ppermute | solution.py:464
  78.0 0.0 copy-start.1
  78.0 7.4 %shard_map.114.acc = f32[112,256]{1,0:T(8,128)S(1)} custom-call(f32[40,8,8,128]{3,2,1,0:T(8,128)S(1)} %get-tuple-element.13.kept, f32[112,256]{1,0:T(8,128)S(1)} %get-tuple-element.14.before), custom_call_target="tpu_custom_call" | custom-call | flops 8000000000 | bytes 1048576 | tf_op jit(solution)/shard_map/pallas_call | solution.py:500
  85.4 0.0 collective-permute-done.6
  85.4 0.1 copy.88.high_z
  85.6 0.1 copy.87.low_z
  85.7 0.0 collective-permute-done.4
  85.7 1.4 %shard_map.115 = f32[2,7,16,128]{3,2,1,0:T(8,128)} custom-call(f32[7]{0:T(128)S(1)} %copy-done, f32[7,32,128]{2,1,0:T(8,128)S(1)} %get-tuple-element.12.melt, f32[112,256]{1,0:T(8,128)S(1)} %shard_map.114.acc, f32[7,16,128]{2,1,0:T(8,128)S(1)} %get-tuple-element.24.low_x, f32[7,16,128]{2,1,0:T(8,128)S(1)} %get-tuple-element.23.high_x, ...), custom_call_target="tpu_custom_call" | custom-call | tf_op jit(solution)/shard_map/pallas_call | solution.py:545
  87.1 1.9 %shard_map.116 = (f32[3,256,128]{2,1,0:T(8,128)}, f32[256,128]{1,0:T(8,128)}) custom-call(s32[256]{0:T(256)S(1)} %copy-done.1, f32[2048,128]{1,0:T(8,128)S(1)} %bitcast.19), custom_call_target="tpu_custom_call" | custom-call | tf_op jit(solution)/shard_map/pallas_call | solution.py:552
  (16 shorter events, 0.1 us)
Async XLA Ops:
  4.5 10.4 %copy-start.4 = (f32[2,16,7,128]{3,1,2,0:T(8,128)S(1)}, f32[2,16,7,128]{3,1,2,0:T(8,128)}, u32[]{:S(2)}) copy-start(f32[2,16,7,128]{3,1,2,0:T(8,128)} %param.9) | copy-start | bytes 344068
  4.5 29.5 %copy-start = (f32[7]{0:T(128)S(1)}, f32[7]{0:T(128)}, u32[]{:S(2)}) copy-start(f32[7]{0:T(128)} %rate.3) | copy-start | bytes 88
  4.5 29.5 %copy-start.2 = (f32[3]{0:T(128)S(1)}, f32[3]{0:T(128)}, u32[]{:S(2)}) copy-start(f32[3]{0:T(128)} %slope.1) | copy-start | bytes 40
  4.5 29.5 %copy-start.3 = (f32[3]{0:T(128)S(1)}, f32[3]{0:T(128)}, u32[]{:S(2)}) copy-start(f32[3]{0:T(128)} %partition.1) | copy-start | bytes 40
  4.5 29.5 %all-to-all-start = ((f32[640,4,128]{2,1,0:T(4,128)}), f32[640,4,128]{2,1,0:T(4,128)S(1)}, u32[]{:S(2)}, u32[]{:S(2)}) async-start(f32[640,4,128]{2,1,0:T(4,128)} %bitcast.23), calls=%async_computation | async-start | bytes 2621440 | tf_op jit(solution)/shard_map/all_to_all | solution.py:511
  15.2 13.5 %collective-permute-start.3 = (f32[7,32]{1,0:T(8,128)S(1)}, f32[7,32]{1,0:T(8,128)S(1)}, u32[]{:S(2)}, u32[]{:S(2)}) collective-permute-start(f32[7,32]{1,0:T(8,128)S(1)} %get-tuple-element.21), channel_id=1, source_target_pairs={{0,32},{64,96},{32,0},{96,64},{1,33},{65,97},{33,1},{97,65},{2,34}... | collective-permute-start | bytes 2696 | tf_op jit(solution)/shard_map/ppermute | solution.py:464
  15.8 12.8 %collective-permute-start.2 = (f32[7,32]{1,0:T(8,128)S(1)}, f32[7,32]{1,0:T(8,128)S(1)}, u32[]{:S(2)}, u32[]{:S(2)}) collective-permute-start(f32[7,32]{1,0:T(8,128)S(1)} %get-tuple-element.22), channel_id=1, source_target_pairs={{32,64},{64,32},{33,65},{65,33},{34,66},{66,34},{35,67},{67,35},{3... | collective-permute-start | bytes 2696 | tf_op jit(solution)/shard_map/ppermute | solution.py:464
  19.9 9.0 %collective-permute-start.1 = (f32[7,16,128]{2,1,0:T(8,128)S(1)}, f32[7,16,128]{2,1,0:T(8,128)S(1)}, u32[]{:S(2)}, u32[]{:S(2)}) collective-permute-start(f32[7,16,128]{2,1,0:T(8,128)S(1)} %get-tuple-element.29), channel_id=1, source_target_pairs={{0,1},{2,3},{4,5},{6,7},{8,9},{10,11},{12,13},{14,15},{16,17},{18,... | collective-permute-start | bytes 172040 | tf_op jit(solution)/shard_map/ppermute | solution.py:464
  20.0 14.0 %collective-permute-start = (f32[7,16,128]{2,1,0:T(8,128)S(1)}, f32[7,16,128]{2,1,0:T(8,128)S(1)}, u32[]{:S(2)}, u32[]{:S(2)}) collective-permute-start(f32[7,16,128]{2,1,0:T(8,128)S(1)} %get-tuple-element.30), channel_id=1, source_target_pairs={{1,2},{3,4},{5,6},{7,8},{9,10},{11,12},{13,14},{15,16},{17,18},{19... | collective-permute-start | bytes 172040 | tf_op jit(solution)/shard_map/ppermute | solution.py:464
  59.5 27.6 %all-to-all-start.1 = ((f32[512,4,128]{2,1,0:T(4,128)}), f32[512,4,128]{2,1,0:T(4,128)S(1)}, u32[]{:S(2)}, u32[]{:S(2)}) async-start(f32[512,4,128]{2,1,0:T(4,128)} %bitcast.11), calls=%async_computation.1 | async-start | bytes 2097152 | tf_op jit(solution)/shard_map/all_to_all | solution.py:511
  67.4 18.0 %collective-permute-start.7 = (f32[7,32]{1,0:T(8,128)S(1)}, f32[7,32]{1,0:T(8,128)S(1)}, u32[]{:S(2)}, u32[]{:S(2)}) collective-permute-start(f32[7,32]{1,0:T(8,128)S(1)} %get-tuple-element.19), channel_id=1, source_target_pairs={{0,32},{64,96},{32,0},{96,64},{1,33},{65,97},{33,1},{97,65},{2,34}... | collective-permute-start | bytes 2696 | tf_op jit(solution)/shard_map/ppermute | solution.py:464
  68.0 17.4 %collective-permute-start.6 = (f32[7,32]{1,0:T(8,128)S(1)}, f32[7,32]{1,0:T(8,128)S(1)}, u32[]{:S(2)}, u32[]{:S(2)}) collective-permute-start(f32[7,32]{1,0:T(8,128)S(1)} %get-tuple-element.20), channel_id=1, source_target_pairs={{32,64},{64,32},{33,65},{65,33},{34,66},{66,34},{35,67},{67,35},{3... | collective-permute-start | bytes 2696 | tf_op jit(solution)/shard_map/ppermute | solution.py:464
  72.2 13.5 %collective-permute-start.5 = (f32[7,16,128]{2,1,0:T(8,128)S(1)}, f32[7,16,128]{2,1,0:T(8,128)S(1)}, u32[]{:S(2)}, u32[]{:S(2)}) collective-permute-start(f32[7,16,128]{2,1,0:T(8,128)S(1)} %get-tuple-element.25), channel_id=1, source_target_pairs={{0,1},{2,3},{4,5},{6,7},{8,9},{10,11},{12,13},{14,15},{16,17},{18,... | collective-permute-start | bytes 172040 | tf_op jit(solution)/shard_map/ppermute | solution.py:464
  72.3 13.4 %collective-permute-start.4 = (f32[7,16,128]{2,1,0:T(8,128)S(1)}, f32[7,16,128]{2,1,0:T(8,128)S(1)}, u32[]{:S(2)}, u32[]{:S(2)}) collective-permute-start(f32[7,16,128]{2,1,0:T(8,128)S(1)} %get-tuple-element.26), channel_id=1, source_target_pairs={{1,2},{3,4},{5,6},{7,8},{9,10},{11,12},{13,14},{15,16},{17,18},{19... | collective-permute-start | bytes 172040 | tf_op jit(solution)/shard_map/ppermute | solution.py:464
  78.0 9.1 %copy-start.1 = (s32[256]{0:T(256)S(1)}, s32[256]{0:T(256)}, u32[]{:S(2)}) copy-start(s32[256]{0:T(256)} %get-tuple-element.15.slot_of) | copy-start | bytes 3076
